TPU v7x, 256 devices: a whole 4x4x8 slice. The times are simulated.
256 devices in a mesh: rows: 32 (over x, z_lo, y), vocab: 8 (over z_hi, core).
Axes of the slice: x: 4, y: 4, z: 8 (z_hi: 4, z_lo: 2; z = z_hi * 2 + z_lo), core: 2. Of those that a mesh axis runs over, the one named last changes fastest.
Arguments:
- teacher_hidden: bfloat16 [512, 4096], P(('rows', 'vocab')), may hold values from -48 to 48
- student_hidden: bfloat16 [512, 2048], P(('rows', 'vocab')), may hold values from -48 to 48
- teacher_head: bfloat16 [151552, 4096], P(('rows', 'vocab')), may hold values from -1 to 1
- student_head: bfloat16 [151552, 2048], P(('rows', 'vocab')), may hold values from -1 to 1
- loss_weight: float32 [512], P(('rows', 'vocab')), may hold values from 0.5 to 4
Outputs:
- student_hidden_grad: float32 [512, 2048], P(('rows', 'vocab'))
- student_head_grad: bfloat16 [151552, 2048], P(('rows', 'vocab'))
All inputs are finite; a program needn't handle non-finite values.
Results may differ from a plain program's by a relative error of at most 0.022.
Values may be sent and summed in bfloat16 or wider, within the bound.
No kernel may reach another device: no remote copies, remote signals or barrier semaphores. Data moves between devices by JAX's collectives and lax.ppermute only.
A program may use at most 64 MiB of HBM per device.

v0:
```python
import jax
import jax.numpy as jnp
from jax import lax
from jax.sharding import PartitionSpec as P


def row_logits(hidden, head):
    return lax.dot_general(
        hidden, head, (((1,), (1,)), ((), ())), preferred_element_type=jnp.float32
    )


def on_device(teacher_hidden, student_hidden, teacher_head, student_head, loss_weight):
    teach_all, stud_all, weight_all = (
        lax.all_gather(teacher_hidden, ("rows", "vocab"), axis=0, tiled=True),
        lax.all_gather(student_hidden, ("rows", "vocab"), axis=0, tiled=True),
        lax.all_gather(
            loss_weight.astype(jnp.bfloat16), ("rows", "vocab"), axis=0, tiled=True
        ).astype(loss_weight.dtype),
    )
    logit_teach = row_logits(teach_all, teacher_head)
    logit_stud = row_logits(stud_all, student_head)
    local_teach = jnp.max(logit_teach, axis=1)
    local_stud = jnp.max(logit_stud, axis=1)
    peak_teach, peak_stud = lax.pmax((local_teach, local_stud), ("rows", "vocab"))
    shifted_teach = jnp.sum(jnp.exp(logit_teach - peak_teach[:, None]), axis=1)
    shifted_stud = jnp.sum(jnp.exp(logit_stud - peak_stud[:, None]), axis=1)
    total_teach, total_stud = lax.psum((shifted_teach, shifted_stud), ("rows", "vocab"))
    lse_teach = peak_teach + jnp.log(total_teach)
    lse_stud = peak_stud + jnp.log(total_stud)
    logit_grad = (
        weight_all[:, None]
        * (jnp.exp(logit_stud - lse_stud[:, None]) - jnp.exp(logit_teach - lse_teach[:, None]))
    ).astype(jnp.bfloat16)
    head_grad = lax.dot_general(
        logit_grad, stud_all, (((0,), (0,)), ((), ())), preferred_element_type=jnp.float32
    ).astype(jnp.bfloat16)
    hidden_grad = lax.psum_scatter(
        jnp.dot(logit_grad, student_head, preferred_element_type=jnp.float32),
        ("rows", "vocab"),
        scatter_dimension=0,
        tiled=True,
    )
    return (hidden_grad, head_grad)


def solution(mesh):
    in_specs = (
        P(("rows", "vocab"), None),
        P(("rows", "vocab"), None),
        P(("rows", "vocab"), None),
        P(("rows", "vocab"), None),
        P(("rows", "vocab")),
    )
    out_specs = (P(("rows", "vocab"), None), P(("rows", "vocab"), None))
    return jax.shard_map(
        on_device, mesh=mesh, in_specs=in_specs, out_specs=out_specs, check_vma=False
    )
```

profile of v0, /device:TPU:32, one launch (start us, length us, event | category | flops | bytes accessed | tf_op | source)
XLA Modules:
  0.0 1274.3 jit_solution(4879867141908697381)
XLA Ops:
  7.2 0.0 copy-start
  7.2 0.0 all-gather.5.cloned.1.call-start
  7.2 0.7 all-gather.5.cloned.1.call-update
  7.9 0.0 all-gather.7.cloned.1.call-start
  8.0 0.7 all-gather.7.cloned.1.call-update
  8.7 0.0 all-reduce.6.cloned.1.call-start
  8.7 0.7 convert_element_type.12
  9.4 0.2 dynamic-update-slice
  9.6 79.9 %all-reduce = bf16[512]{0:T(512)(128)(2,1)S(1)} all-reduce(bf16[512]{0:T(512)(128)(2,1)S(1)} %dynamic-update-slice), channel_id=1, replica_groups=mesh['rows'=32,'vocab'=8] {'rows','vocab'}, use_global_device_ids=true, to_apply=%add | all-reduce | flops 512 | bytes 2048
  89.4 331.3 %all-gather.5.cloned.1.call-done = bf16[256,2,2048]{2,1,0:T(2,128)(2,1)} async-done(((bf16[1,2,2048]{2,1,0:T(2,128)(2,1)}), bf16[256,2,2048]{2,1,0:T(2,128)(2,1)}) %all-gather.5.cloned.1.call-update) | async-done | bytes 2097168 | tf_op jit(solution)/shard_map/all_gather | solution.py:16
  420.8 4.1 reshape.12
  424.9 4.1 fusion.1
  429.0 405.2 %all-gather.7.cloned.1.call-done = bf16[256,2,4096]{2,1,0:T(2,128)(2,1)} async-done(((bf16[1,2,4096]{2,1,0:T(2,128)(2,1)}), bf16[256,2,4096]{2,1,0:T(2,128)(2,1)}) %all-gather.7.cloned.1.call-update) | async-done | bytes 4194320 | tf_op jit(solution)/shard_map/all_gather | solution.py:15
  834.2 7.2 reshape.14
  841.4 7.4 fusion
  848.8 72.5 %all-reduce.3 = (f32[512]{0:T(512)S(1)}, f32[512]{0:T(512)S(1)}) all-reduce(f32[512]{0:T(512)S(1)} %get-tuple-element.6, f32[512]{0:T(512)S(1)} %get-tuple-element.8), channel_id=1, replica_groups=mesh['rows'=32,'vocab'=8] {'rows','vocab'}, use_global_device_ids=true, to_apply=%region_5.0 | all-reduce | flops 1024 | bytes 8192 | tf_op jit(solution)/shard_map/pmax | solution.py:25
  921.4 2.0 exponential_reduce_fusion
  923.4 74.8 %all-reduce.2 = (f32[512]{0:T(512)S(1)}, f32[512]{0:T(512)S(1)}) all-reduce(f32[512]{0:T(512)S(1)} %get-tuple-element.10, f32[512]{0:T(512)S(1)} %get-tuple-element.11), channel_id=1, replica_groups=mesh['rows'=32,'vocab'=8] {'rows','vocab'}, use_global_device_ids=true, to_apply=%region_7.0 | all-reduce | flops 1024 | bytes 8192 | tf_op jit(solution)/shard_map/psum | solution.py:28
  998.2 2.0 multiply_convert_fusion
  1000.2 3.8 fusion.2
  1004.0 0.0 all-reduce.6.cloned.1.call-update
  1004.0 4.4 convolution_convert_fusion
  1008.4 257.9 %all-reduce.6.cloned.1.call-done = f32[512,2048]{1,0:T(8,128)} async-done(((f32[512,2048]{1,0:T(8,128)}), f32[512,2048]{1,0:T(8,128)}) %all-reduce.6.cloned.1.call-update) | async-done | bytes 4194320
  1266.3 1.5 constant_dynamic-slice_fusion
  (5 shorter events, 0.0 us)
Async XLA Ops:
  7.2 417.8 %copy-start = (bf16[592,2048]{1,0:T(8,128)(2,1)S(1)}, bf16[592,2048]{1,0:T(8,128)(2,1)}, u32[]{:S(2)}) copy-start(bf16[592,2048]{1,0:T(8,128)(2,1)} %param.8) | copy-start | bytes 7274500
  7.2 413.6 %all-gather.5.cloned.1.call-start = ((), (), s32[]{:S(2)}) async-start(), calls=%async_computation | async-start | bytes 2105344 | tf_op jit(solution)/shard_map/all_gather | solution.py:16
  7.9 826.3 %all-gather.7.cloned.1.call-start = ((), (), s32[]{:S(2)}) async-start(), calls=%async_computation.1 | async-start | bytes 4210688 | tf_op jit(solution)/shard_map/all_gather | solution.py:15
  8.7 1257.7 %all-reduce.6.cloned.1.call-start = ((), (), s32[]{:S(2)}) async-start(), calls=%async_computation.2 | async-start | bytes 8388608
Sparse Core Ops, SparseCore 0:
  9.9 410.8 all-gather.4
  422.7 411.5 all-gather.6
  1004.1 262.1 all-reduce.5
where the time goes:
time: 1280 us; the launch traced here: 1270 us
  waiting for transfers between devices  996 us (78%)
  blocking collectives  227 us (18%)
  matrix products  19.7 us (2%)
  between operations  13.8 us (1%)
  local copies, waits for them, and re-layouts  13 us (1%)
    all_gather x1, waiting for transfers between devices, on_device(): lax.all_gather(teacher_hidden, ('rows', 'vocab'), axis=0, tiled=True)  405 us
    all_gather x1, waiting for transfers between devices, on_device(): lax.all_gather(student_hidden, ('rows', 'vocab'), axis=0, tiled=True)  331 us
    unnamed x4, waiting for transfers between devices  259 us
    unnamed x1, blocking collectives  79.9 us
    psum x1, blocking collectives, on_device(): lax.psum((shifted_teach, shifted_stud), ('rows', 'vocab'))  74.8 us
    pmax x1, blocking collectives, on_device(): lax.pmax((local_teach, local_stud), ('rows', 'vocab'))  72.5 us
  transfers between devices with their start and end apart: 3, of which 3 were waited for; matrix products, arithmetic and copies ran while one was open for 1% of the time, Pallas kernels for 0%

commit v1 on v0

v1 whole, which is shorter than its diff:
```python
import jax
import jax.numpy as jnp
from jax import lax
from jax.sharding import Mesh, PartitionSpec as P

AXES = ("x", "zl", "y", "zh", "c")
SIZES = (4, 2, 4, 4, 2)
PLANE, LINE, PAIR = ("x", "y"), ("zl", "zh"), ("c",)
NP, NL = 16, 8


def share(block, axes, n):
    return lax.all_to_all(
        jnp.broadcast_to(block[None], (n,) + block.shape), axes, 0, 0, tiled=True
    )


def swap(block):
    return lax.ppermute(block, PAIR, [(0, 1), (1, 0)])


def logits_of(head, hidden):
    return lax.dot_general(
        head, hidden, (((1,), (1,)), ((), ())), preferred_element_type=jnp.float32
    )


def join(stats):
    peak_t, total_t, peak_s, total_s, weight = (stats[:, i] for i in range(5))
    top_t, top_s = jnp.max(peak_t, 0), jnp.max(peak_s, 0)
    return jnp.stack(
        [
            top_t,
            jnp.sum(total_t * jnp.exp(peak_t - top_t), 0),
            top_s,
            jnp.sum(total_s * jnp.exp(peak_s - top_s), 0),
            jnp.sum(weight, 0),
        ]
    )


def on_device(teacher_hidden, student_hidden, teacher_head, student_head, loss_weight):
    tok, dt = teacher_hidden.shape
    ds = student_hidden.shape[1]
    nt = tok * NP * NL
    th = (teacher_head, swap(teacher_head))
    sh = (student_head, swap(student_head))

    mine = jnp.concatenate([teacher_hidden, student_hidden], 1)
    line = share(mine, LINE, NL).reshape(NL * tok, dt + ds)
    hidden = share(line, PLANE, NP).reshape(nt, dt + ds)
    teach, stud = hidden[:, :dt], hidden[:, dt:]

    lt = [logits_of(h, teach) for h in th]
    ls = [logits_of(h, stud) for h in sh]
    peak_t = jnp.maximum(jnp.max(lt[0], 0), jnp.max(lt[1], 0))
    peak_s = jnp.maximum(jnp.max(ls[0], 0), jnp.max(ls[1], 0))
    et = [jnp.exp(v - peak_t) for v in lt]
    es = [jnp.exp(v - peak_s) for v in ls]
    sum_t = jnp.sum(et[0], 0) + jnp.sum(et[1], 0)
    sum_s = jnp.sum(es[0], 0) + jnp.sum(es[1], 0)

    spot = (
        lax.axis_index("x") * 4 + lax.axis_index("y")
    ) * NL + lax.axis_index("zl") * 4 + lax.axis_index("zh")
    weight = lax.dynamic_update_slice(
        jnp.zeros((nt,), jnp.float32), loss_weight, (spot * tok,)
    )
    stats = jnp.stack([peak_t, sum_t, peak_s, sum_s, weight])
    stats = join(share(stats, PLANE, NP))
    stats = join(share(stats, LINE, NL))
    lse_t = stats[0] + jnp.log(stats[1])
    lse_s = stats[2] + jnp.log(stats[3])
    scale_t = stats[4] * jnp.exp(peak_t - lse_t)
    scale_s = stats[4] * jnp.exp(peak_s - lse_s)
    grad = [(s * scale_s - t * scale_t).astype(jnp.bfloat16) for s, t in zip(es, et)]

    theirs = swap(jnp.dot(grad[1], stud, preferred_element_type=jnp.float32))
    part = sum(
        lax.dot_general(
            g, h, (((0,), (0,)), ((), ())), preferred_element_type=jnp.float32
        )
        for g, h in zip(grad, sh)
    )
    part = lax.all_to_all(part.reshape(NP, NL * tok, ds), PLANE, 0, 0, tiled=True)
    part = jnp.sum(part, 0).reshape(NL, tok, ds)
    part = lax.all_to_all(part, LINE, 0, 0, tiled=True)
    hidden_grad = jnp.sum(part, 0)
    head_grad = (
        jnp.dot(grad[0], stud, preferred_element_type=jnp.float32) + theirs
    ).astype(jnp.bfloat16)
    return hidden_grad, head_grad


def solution(mesh):
    fine = Mesh(mesh.devices.reshape(SIZES), AXES)
    split = P(AXES, None)
    return jax.shard_map(
        on_device,
        mesh=fine,
        in_specs=(split, split, split, split, P(AXES)),
        out_specs=(split, split),
        check_vma=False,
    )
```

time: 1280 us -> 174 us (0.14)
  waiting for transfers between devices: 996 us -> 41.6 us
  blocking collectives: 227 us -> 86.6 us
  between operations: 13.8 us -> 0.85 us
    all_gather x2 -> x0, waiting for transfers between devices: 737 us -> none  [the longest x1 405 us: on_device(): lax.all_gather(teacher_hidden, ('rows', 'vocab'), axis=0, tiled=True)]
    unnamed x4 -> x0, waiting for transfers between devices: 259 us -> none
    all_to_all x0 -> x5, blocking collectives: none -> 86.6 us  [the longest x3 41.6 us: share(): lax.all_to_all(jnp.broadcast_to(block[None], (n,) + block.shape), axes, 0...]
    unnamed x1 -> x0, blocking collectives: 79.9 us -> none
    psum x1 -> x0, blocking collectives: 74.8 us -> none  [on_device(): lax.psum((shifted_teach, shifted_stud), ('rows', 'vocab'))]
    pmax x1 -> x0, blocking collectives: 72.5 us -> none  [on_device(): lax.pmax((local_teach, local_stud), ('rows', 'vocab'))]
    all_to_all x0 -> x1, waiting for transfers between devices: none -> 41.5 us  [share(): lax.all_to_all(jnp.broadcast_to(block[None], (n,) + block.shape), axes, 0...]
  transfers between devices with their start and end apart: 3 -> 4, of which waited for: 3 -> 1; matrix products, arithmetic and copies ran while one was open for 1% -> 13% of each run, Pallas kernels for 0% -> 0%
where the time goes in v1:
time: 174 us
  blocking collectives  86.6 us (50%)
  waiting for transfers between devices  41.6 us (24%)
  matrix products  24.5 us (14%)
  starting transfers between devices  7.36 us (4%)
  other arithmetic  7.29 us (4%)
  local copies, waits for them, and re-layouts  5.39 us (3%)
    all_to_all x3, blocking collectives, share(): lax.all_to_all(jnp.broadcast_to(block[None], (n,) + block.shape), axes, 0...  41.6 us
    all_to_all x1, waiting for transfers between devices, share(): lax.all_to_all(jnp.broadcast_to(block[None], (n,) + block.shape), axes, 0...  41.5 us
    all_to_all x1, blocking collectives, on_device(): lax.all_to_all(part.reshape(NP, NL * tok, ds), PLANE, 0, 0, tiled=True)  32.6 us
    dot_general x4, matrix products, logits_of(): lax.dot_general(head, hidden, (((1,), (1,)), ((), ())), preferred_element...  13.2 us
    all_to_all x1, blocking collectives, on_device(): part = lax.all_to_all(part, LINE, 0, 0, tiled=True)  12.4 us
    all_to_all x1, starting transfers between devices, share(): lax.all_to_all(jnp.broadcast_to(block[None], (n,) + block.shape), axes, 0...  7.17 us
    dot_general x1, matrix products, on_device(): jnp.dot(grad[0], stud, preferred_element_type=jnp.float32) + theirs  4.6 us
    dot_general x2, matrix products, on_device(): lax.dot_general(g, h, (((0,), (0,)), ((), ())), preferred_element_type=jn...  3.69 us
  transfers between devices with their start and end apart: 4, of which 1 were waited for; matrix products, arithmetic and copies ran while one was open for 13% of the time, Pallas kernels for 0%

profile of v1, /device:TPU:32, one launch (start us, length us, event | category | flops | bytes accessed | tf_op | source)
XLA Modules:
  0.0 173.5 jit_solution(13929910600973852920)
XLA Ops:
  0.7 0.8 pad_maximum_fusion
  1.6 18.0 %all_to_all.30 = bf16[8,2,6144]{2,1,0:T(2,128)(2,1)S(1)} all-to-all(bf16[8,2,6144]{2,1,0:T(2,128)(2,1)S(1)} %broadcast_in_dim.12), channel_id=1, replica_groups=mesh['x'=4,'zl'=2,'y'=4,'zh'=4,'c'=2] {'zl','zh'}, dimensions={0} | all-to-all | bytes 393216 | tf_op jit(solution)/shard_map/all_to_all | solution.py:13
  19.7 2.0 %broadcast_in_dim.14 = bf16[16,16,6144]{2,1,0:T(8,128)(2,1)} broadcast(bf16[16,6144]{1,0:T(8,128)(2,1)S(1)} %broadcast_in_dim.13), dimensions={1,2} | broadcast | bytes 3342336 | tf_op jit(solution)/shard_map/broadcast_in_dim | solution.py:14
  21.7 7.2 %all-to-all-start.1 = ((bf16[16,16,6144]{2,1,0:T(8,128)(2,1)}), bf16[16,16,6144]{2,1,0:T(8,128)(2,1)S(1)}, u32[]{:S(2)}, u32[]{:S(2)}) async-start(bf16[16,16,6144]{2,1,0:T(8,128)(2,1)} %broadcast_in_dim.14), calls=%async_computation.1 | async-start | bytes 6291456 | tf_op jit(solution)/shard_map/all_to_all | solution.py:13
  29.0 0.3 dynamic_update_slice.4
  29.3 41.5 %all-to-all-done.1 = bf16[16,16,6144]{2,1,0:T(8,128)(2,1)S(1)} async-done(((bf16[16,16,6144]{2,1,0:T(8,128)(2,1)}), bf16[16,16,6144]{2,1,0:T(8,128)(2,1)S(1)}, u32[]{:S(2)}, u32[]{:S(2)}) %all-to-all-start.1) | async-done | bytes 3145760 | tf_op jit(solution)/shard_map/all_to_all | solution.py:13
  70.8 2.5 %fusion.35 = (f32[256]{0:T(256)S(1)}, f32[256,592]{0,1:T(8,128)S(1)}) fusion(bf16[592,2048]{1,0:T(8,128)(2,1)} %param.8, bf16[256,6144]{1,0:T(8,128)(2,1)S(1)} %bitcast.70), kind=kOutput, calls=%fused_computation.56 | convolution fusion | flops 620908288 | bytes 4080640 | tf_op jit(solution)/shard_map/dot_general | solution.py:23
  73.4 2.8 %fusion.36 = (f32[256]{0:T(256)S(1)}, f32[256,592]{0,1:T(8,128)S(1)}) fusion(bf16[592,2048]{1,0:T(8,128)(2,1)} %collective-permute-done, bf16[256,6144]{1,0:T(8,128)(2,1)S(1)} %bitcast.71), kind=kOutput, calls=%fused_computation.57 | convolution fusion | flops 620908288 | bytes 4080640 | tf_op jit(solution)/shard_map/dot_general | solution.py:23
  76.4 0.6 copy-done.2
  77.0 3.8 %fusion.33 = (f32[256]{0:T(256)S(1)}, f32[256,592]{0,1:T(8,128)S(1)}) fusion(bf16[592,4096]{1,0:T(8,128)(2,1)} %param.7, bf16[256,6144]{1,0:T(8,128)(2,1)S(1)} %bitcast.72), kind=kOutput, calls=%fused_computation.54 | convolution fusion | flops 1241665280 | bytes 7554048 | tf_op jit(solution)/shard_map/dot_general | solution.py:23
  80.9 4.1 %fusion.34 = (f32[256]{0:T(256)S(1)}, f32[256,592]{0,1:T(8,128)S(1)}) fusion(bf16[592,4096]{1,0:T(8,128)(2,1)} %collective-permute-done.1, bf16[256,6144]{1,0:T(8,128)(2,1)S(1)} %bitcast.73), kind=kOutput, calls=%fused_computation.55 | convolution fusion | flops 1241665280 | bytes 7554048 | tf_op jit(solution)/shard_map/dot_general | solution.py:23
  85.2 0.6 copy-done.4
  85.8 11.4 %all_to_all.31 = f32[16,5,256]{2,1,0:T(8,128)S(1)} all-to-all(f32[16,5,256]{2,1,0:T(8,128)S(1)} %broadcast_in_dim.16), channel_id=1, replica_groups=mesh['x'=4,'zl'=2,'y'=4,'zh'=4,'c'=2] {'x','y'}, dimensions={0} | all-to-all | bytes 163840 | tf_op jit(solution)/shard_map/all_to_all | solution.py:13
  97.4 12.1 %all_to_all.32 = f32[8,5,256]{2,1,0:T(8,128)S(1)} all-to-all(f32[8,5,256]{2,1,0:T(8,128)S(1)} %broadcast_in_dim.17), channel_id=1, replica_groups=mesh['x'=4,'zl'=2,'y'=4,'zh'=4,'c'=2] {'zl','zh'}, dimensions={0} | all-to-all | bytes 81920 | tf_op jit(solution)/shard_map/all_to_all | solution.py:13
  109.6 2.0 %subtract_convert_fusion = (bf16[256,592]{0,1:T(8,128)(2,1)S(1)}, bf16[256,592]{0,1:T(8,128)(2,1)S(1)}) fusion(f32[256,592]{0,1:T(8,128)} %copy-done.4, f32[256,592]{0,1:T(8,128)} %copy-done.2, f32[256]{0:T(256)S(1)} %get-tuple-element.29, f32[256]{0:T(256)S(1)} %get-tuple-element.28, f32[256]{0:T(256)S(1)} %max.35, f32[256]{0:T(256)S(1)} %max.34, ...), kind=kLoop, calls=%fused_computation.13 | loop fusion | flops 1818624 | bytes 3035136 | tf_op jit(solution)/shard_map/convert
  111.6 3.0 %fusion.4 = f32[592,2048]{1,0:T(8,128)} fusion(bf16[256,592]{0,1:T(8,128)(2,1)S(1)} %get-tuple-element.26, bf16[256,6144]{1,0:T(8,128)(2,1)S(1)} %bitcast.74), kind=kOutput, calls=%fused_computation.6 | convolution fusion | flops 620756992 | bytes 6201344 | tf_op jit(solution)/shard_map/dot_general | solution.py:78
  114.6 1.0 fusion.37
  115.6 2.7 %convolution_add_fusion = f32[256,2048]{1,0:T(8,128)S(1)} fusion(f32[256,2048]{1,0:T(8,128)S(1)} %fusion.37, bf16[256,592]{0,1:T(8,128)(2,1)S(1)} %get-tuple-element.26, bf16[592,2048]{1,0:T(8,128)(2,1)} %collective-permute-done), kind=kOutput, calls=%fused_computation.1 | convolution fusion | flops 621281280 | bytes 6922240 | tf_op jit(solution)/shard_map/dot_general | solution.py:80
  118.3 32.6 %all_to_all.33 = f32[16,16,2048]{2,1,0:T(8,128)} all-to-all(f32[16,16,2048]{2,1,0:T(8,128)S(1)} %bitcast.76), channel_id=1, replica_groups=mesh['x'=4,'zl'=2,'y'=4,'zh'=4,'c'=2] {'x','y'}, dimensions={0} | all-to-all | bytes 4194304 | tf_op jit(solution)/shard_map/all_to_all | solution.py:85
  150.9 2.4 %reduce_sum.118 = f32[16,2048]{1,0:T(8,128)} reduce(f32[16,16,2048]{2,1,0:T(8,128)} %all_to_all.33, f32[]{:T(128)} %constant.12.clone.1), dimensions={0}, to_apply=%region_18.0 | reduce | flops 491520 | bytes 2228228 | tf_op jit(solution)/shard_map/reduce_sum | solution.py:86
  153.3 1.6 reshape.103
  154.9 12.4 %all_to_all.34 = f32[8,2,2048]{2,1,0:T(2,128)} all-to-all(f32[8,2,2048]{2,1,0:T(2,128)} %reshape.103), channel_id=1, replica_groups=mesh['x'=4,'zl'=2,'y'=4,'zh'=4,'c'=2] {'zl','zh'}, dimensions={0} | all-to-all | bytes 262144 | tf_op jit(solution)/shard_map/all_to_all | solution.py:87
  167.4 1.6 reduce_sum.119
  168.9 4.6 %add_convert_fusion = bf16[592,2048]{1,0:T(8,128)(2,1)} fusion(f32[592,2048]{1,0:T(8,128)} %collective-permute-done.2, bf16[256,592]{0,1:T(8,128)(2,1)S(1)} %get-tuple-element.27, bf16[256,6144]{1,0:T(8,128)(2,1)S(1)} %bitcast.75), kind=kOutput, calls=%fused_computation | convolution fusion | flops 623181824 | bytes 8626176 | tf_op jit(solution)/shard_map/dot_general | solution.py:90
  (35 shorter events, 1.1 us)
Async XLA Ops:
  0.6 80.2 %collective-permute-start.1 = (bf16[592,4096]{1,0:T(8,128)(2,1)}, bf16[592,4096]{1,0:T(8,128)(2,1)}, u32[]{:S(2)}, u32[]{:S(2)}) collective-permute-start(bf16[592,4096]{1,0:T(8,128)(2,1)} %param.7), channel_id=1, source_target_pairs={{0,1},{1,0},{2,3},{3,2},{4,5},{5,4},{6,7},{7,6},{8,9},{9,8},{10,11... | collective-permute-start | bytes 14549000 | tf_op jit(solution)/shard_map/ppermute | solution.py:19
  21.7 7.3 %copy-start.5 = (f32[2]{0:T(128)S(1)}, f32[2]{0:T(128)}, u32[]{:S(2)}) copy-start(f32[2]{0:T(128)} %param.9) | copy-start | bytes 28
  21.7 49.1 %all-to-all-start.1 = ((bf16[16,16,6144]{2,1,0:T(8,128)(2,1)}), bf16[16,16,6144]{2,1,0:T(8,128)(2,1)S(1)}, u32[]{:S(2)}, u32[]{:S(2)}) async-start(bf16[16,16,6144]{2,1,0:T(8,128)(2,1)} %broadcast_in_dim.14), calls=%async_computation.1 | async-start | bytes 6291456 | tf_op jit(solution)/shard_map/all_to_all | solution.py:13
  28.9 44.5 %collective-permute-start = (bf16[592,2048]{1,0:T(8,128)(2,1)}, bf16[592,2048]{1,0:T(8,128)(2,1)}, u32[]{:S(2)}, u32[]{:S(2)}) collective-permute-start(bf16[592,2048]{1,0:T(8,128)(2,1)} %param.8), channel_id=1, source_target_pairs={{0,1},{1,0},{2,3},{3,2},{4,5},{5,4},{6,7},{7,6},{8,9},{9,8},{10,11... | collective-permute-start | bytes 7274504 | tf_op jit(solution)/shard_map/ppermute | solution.py:19
  73.4 2.8 %copy-start.1 = (f32[256,592]{0,1:T(8,128)}, f32[256,592]{0,1:T(8,128)S(1)}, u32[]{:S(2)}) copy-start(f32[256,592]{0,1:T(8,128)S(1)} %get-tuple-element.35) | copy-start | bytes 1818628
  76.2 0.8 copy-start.2
  80.8 4.1 %copy-start.3 = (f32[256,592]{0,1:T(8,128)}, f32[256,592]{0,1:T(8,128)S(1)}, u32[]{:S(2)}) copy-start(f32[256,592]{0,1:T(8,128)S(1)} %get-tuple-element.31) | copy-start | bytes 1818628
  84.9 0.8 copy-start.4
  111.6 3.0 %copy-start = (bf16[592,2048]{1,0:T(8,128)(2,1)S(1)}, bf16[592,2048]{1,0:T(8,128)(2,1)}, u32[]{:S(2)}) copy-start(bf16[592,2048]{1,0:T(8,128)(2,1)} %param.8) | copy-start | bytes 7274500
  114.6 54.3 %collective-permute-start.2 = (f32[592,2048]{1,0:T(8,128)}, f32[592,2048]{1,0:T(8,128)}, u32[]{:S(2)}, u32[]{:S(2)}) collective-permute-start(f32[592,2048]{1,0:T(8,128)} %fusion.4), channel_id=1, source_target_pairs={{0,1},{1,0},{2,3},{3,2},{4,5},{5,4},{6,7},{7,6},{8,9},{9,8},{10,11... | collective-permute-start | bytes 14549000 | tf_op jit(solution)/shard_map/ppermute | solution.py:19

commit v2 on v1

v2 whole, which is shorter than its diff:
```python
import jax
import jax.numpy as jnp
from jax import lax
from jax.experimental import pallas as pl
from jax.experimental.pallas import tpu as pltpu
from jax.sharding import Mesh, PartitionSpec as P

AXES = ("x", "zl", "y", "zh", "c")
SIZES = (4, 2, 4, 4, 2)
PLANE, LINE, PAIR = ("x", "y"), ("zl", "zh"), ("c",)
NP, NL = 16, 8
STEPS = (0, 1, 3, 2)
VMEM_LIMIT = 16 * 2**20
WIDE = 2048


def share(block, axes, n):
    return lax.all_to_all(
        jnp.broadcast_to(block[None], (n,) + block.shape), axes, 0, 0, tiled=True
    )


def ring(block, axis):
    return [block] + [
        lax.ppermute(block, axis, [(i, (i + step) % 4) for i in range(4)])
        for step in STEPS[1:]
    ]


def plane_sum(blocks, axes):
    got = lax.all_to_all(blocks, axes, 0, 0, tiled=True)
    return jnp.sum(got.astype(jnp.float32), 0)


def swap(block):
    return lax.ppermute(block, PAIR, [(0, 1), (1, 0)])


def join(stats):
    logs, weight = stats[:, :2], stats[:, 2]
    top = jnp.max(logs, 0)
    logs = top + jnp.log(jnp.sum(jnp.exp(logs - top), 0))
    return jnp.concatenate([logs, jnp.sum(weight, 0)[None]])


def logits_kernel(at, *refs):
    first, second = refs[:4], refs[4:8]
    heads = refs[8:12]
    teach_out, stud_out, stats_out, rows_out = refs[12:16]
    hidden, sem = refs[16:]
    x, y = at[0], at[1]
    half = first[0].shape[2]
    copies = []
    for k in range(4):
        for j in range(4):
            for which, src, dx, dy in (
                (0, first[k], STEPS[j], STEPS[k]),
                (1, second[k], STEPS[k], STEPS[j]),
            ):
                row = ((x - dx) % 4 * 4 + (y - dy) % 4) * 16
                copies.append(
                    pltpu.make_async_copy(
                        src.at[j],
                        hidden.at[pl.ds(row, 16), pl.ds(which * half, half)],
                        sem.at[(k * 4 + j) * 2 + which],
                    )
                )
    for copy in copies:
        copy.start()
    for copy in copies:
        copy.wait()
    rows_out[...] = hidden[:, 2 * WIDE :]
    for h in range(2):
        for out, head, lo in ((teach_out, heads[h], 0), (stud_out, heads[2 + h], 2 * WIDE)):
            out[h] = lax.dot_general(
                head[...],
                hidden[:, lo : lo + head.shape[1]],
                (((1,), (1,)), ((), ())),
                preferred_element_type=jnp.float32,
            )
    for i, out in enumerate((teach_out, stud_out)):
        peak = jnp.max(jnp.max(out[...], 0), 0, keepdims=True)
        terms = jnp.exp(out[...] - peak)
        out[...] = terms
        stats_out[2 * i : 2 * i + 1] = peak
        stats_out[2 * i + 1 : 2 * i + 2] = jnp.sum(jnp.sum(terms, 0), 0, keepdims=True)


def logits(at, first, second, heads):
    ve, nt = heads[0].shape[0], NP * 16
    shape = jax.ShapeDtypeStruct
    return pl.pallas_call(
        logits_kernel,
        out_shape=[
            shape((2, ve, nt), jnp.float32),
            shape((2, ve, nt), jnp.float32),
            shape((4, nt), jnp.float32),
            shape((nt, WIDE), jnp.bfloat16),
        ],
        in_specs=[pl.BlockSpec(memory_space=pltpu.SMEM)]
        + [pl.BlockSpec(memory_space=pl.ANY)] * 8
        + [pl.BlockSpec(memory_space=pltpu.VMEM)] * 4,
        out_specs=[pl.BlockSpec(memory_space=pltpu.VMEM)] * 4,
        scratch_shapes=[
            pltpu.VMEM((nt, 3 * WIDE), jnp.bfloat16),
            pltpu.SemaphoreType.DMA((32,)),
        ],
        compiler_params=pltpu.CompilerParams(vmem_limit_bytes=VMEM_LIMIT),
        cost_estimate=pl.CostEstimate(
            flops=2 * 2 * ve * nt * 3 * WIDE,
            bytes_accessed=2 * ve * 3 * WIDE * 2 + nt * 3 * WIDE * 2,
            transcendentals=4 * ve * nt,
        ),
    )(at, *first, *second, *heads)


def grad_kernel(teach, stud, scale, head0, head1, grad_out, part_out):
    for h in range(2):
        grad_out[h] = (stud[h] * scale[1:2] - teach[h] * scale[0:1]).astype(jnp.bfloat16)
    for n in range(0, WIDE, 512):
        total = sum(
            lax.dot_general(
                grad_out[h],
                head[:, n : n + 512],
                (((0,), (0,)), ((), ())),
                preferred_element_type=jnp.float32,
            )
            for h, head in enumerate((head0, head1))
        )
        part_out[:, n : n + 512] = total.astype(part_out.dtype)


def grads(teach, stud, scale, head0, head1):
    ve, nt = teach.shape[1:]
    shape = jax.ShapeDtypeStruct
    vmem = pl.BlockSpec(memory_space=pltpu.VMEM)
    return pl.pallas_call(
        grad_kernel,
        out_shape=[
            shape((2, ve, nt), jnp.bfloat16),
            shape((nt, WIDE), jnp.bfloat16),
        ],
        in_specs=[vmem] * 5,
        out_specs=[vmem] * 2,
        compiler_params=pltpu.CompilerParams(vmem_limit_bytes=VMEM_LIMIT),
        cost_estimate=pl.CostEstimate(
            flops=2 * 2 * ve * nt * WIDE,
            bytes_accessed=2 * ve * WIDE * 2 + 2 * 2 * ve * nt * 4,
            transcendentals=0,
        ),
    )(teach, stud, scale, head0, head1)


def on_device(teacher_hidden, student_hidden, teacher_head, student_head, loss_weight):
    tok, dt = teacher_hidden.shape
    ds = student_hidden.shape[1]
    nt = tok * NP * NL
    heads = (teacher_head, swap(teacher_head), student_head, swap(student_head))

    x, y = lax.axis_index("x"), lax.axis_index("y")
    mine = jnp.concatenate([teacher_hidden, student_hidden], 1)
    line = share(mine, LINE, NL).reshape(NL * tok, dt + ds)
    line, heads = lax.optimization_barrier((line, heads))
    half = (dt + ds) // 2
    first = ring(jnp.stack(ring(line[:, :half], "x")), "y")
    second = ring(jnp.stack(ring(line[:, half:], "y")), "x")
    teach, stud, stats, rows = logits(jnp.stack([x, y]), first, second, heads)

    z = lax.axis_index("zl") * 4 + lax.axis_index("zh")
    spot = (x * 4 + y) * NL + z
    weight = lax.dynamic_update_slice(
        jnp.zeros((nt,), jnp.float32), loss_weight, (spot * tok,)
    )
    peak, total = stats[0::2], stats[1::2]
    both = jnp.concatenate([peak + jnp.log(total), weight[None]])
    both = join(share(join(share(both, PLANE, NP)), LINE, NL))
    scale = both[2] * jnp.exp(peak - both[:2])
    grad, part = grads(teach, stud, scale, heads[2], heads[3])

    (rows, grad), part = lax.optimization_barrier(((rows, grad), part))
    part = plane_sum(part.reshape(NP, NL * tok, ds), PLANE).reshape(NL, tok, ds)
    theirs = swap(jnp.dot(grad[1], rows, preferred_element_type=jnp.float32))
    ours = jnp.dot(grad[0], rows, preferred_element_type=jnp.float32)
    part, ours, theirs = lax.optimization_barrier((part, ours, theirs))
    hidden_grad = plane_sum(part, LINE)
    return hidden_grad, (ours + theirs).astype(jnp.bfloat16)


def solution(mesh):
    fine = Mesh(mesh.devices.reshape(SIZES), AXES)
    split = P(AXES, None)
    return jax.shard_map(
        on_device,
        mesh=fine,
        in_specs=(split, split, split, split, P(AXES)),
        out_specs=(split, split),
        check_vma=False,
    )
```

time: 174 us -> 141 us (0.81)
  blocking collectives: 86.6 us -> 40.1 us
  starting transfers between devices: 7.36 us -> 28.4 us
  matrix products: 24.5 us -> 6.97 us
  Pallas kernels: 0 us -> 13.8 us
  waiting for transfers between devices: 41.6 us -> 28.1 us
  local copies, waits for them, and re-layouts: 5.39 us -> 13.4 us
    all_to_all x2 -> x0, blocking collectives: 45.1 us -> none  [the longest x1 32.6 us: on_device(): lax.all_to_all(part.reshape(NP, NL * tok, ds), PLANE, 0, 0, tiled=True)]
    all_to_all x1 -> x2, waiting for transfers between devices: 41.5 us -> 16.6 us  [plane_sum(): got = lax.all_to_all(blocks, axes, 0, 0, tiled=True)]
    ppermute x0 -> x12, starting transfers between devices: none -> 19.7 us  [ring(): lax.ppermute(block, axis, [(i, (i + step) % 4) for i in range(4)])]
    dot_general x8 -> x2, matrix products: 24.5 us -> 6.97 us  [the longest x1 3.95 us: on_device(): ours = jnp.dot(grad[0], rows, preferred_element_type=jnp.float32)]
    pallas_call x0 -> x2, Pallas kernels: none -> 13.8 us  [the longest x1 10.2 us: logits(): pl.pallas_call(logits_kernel, out_shape=[shape((2, ve, nt), jnp.float32),...]
    ppermute x0 -> x12, waiting for transfers between devices: none -> 11.6 us  [ring(): lax.ppermute(block, axis, [(i, (i + step) % 4) for i in range(4)])]
    unnamed x12 -> x28, local copies, waits for them, and re-layouts: 1.24 us -> 11.5 us
    convert_element_type x0 -> x1, other arithmetic: none -> 6.02 us  [on_device(): return (hidden_grad, (ours + theirs).astype(jnp.bfloat16))]
  transfers between devices with their start and end apart: 4 -> 17, of which waited for: 1 -> 8; matrix products, arithmetic and copies ran while one was open for 13% -> 9% of each run, Pallas kernels for 0% -> 0%
where the time goes in v2:
time: 141 us; the launch traced here: 140 us
  blocking collectives  40.1 us (28%)
  starting transfers between devices  28.4 us (20%)
  waiting for transfers between devices  28.1 us (20%)
  Pallas kernels  13.8 us (10%)
  local copies, waits for them, and re-layouts  13.4 us (10%)
  other arithmetic  8.11 us (6%)
  matrix products  6.97 us (5%)
    all_to_all x3, blocking collectives, share(): lax.all_to_all(jnp.broadcast_to(block[None], (n,) + block.shape), axes, 0...  40.1 us
    ppermute x12, starting transfers between devices, ring(): lax.ppermute(block, axis, [(i, (i + step) % 4) for i in range(4)])  19.7 us
    all_to_all x2, waiting for transfers between devices, plane_sum(): got = lax.all_to_all(blocks, axes, 0, 0, tiled=True)  16.6 us
    ppermute x12, waiting for transfers between devices, ring(): lax.ppermute(block, axis, [(i, (i + step) % 4) for i in range(4)])  11.6 us
    unnamed x28, local copies, waits for them, and re-layouts  11.5 us
    pallas_call x1, Pallas kernels, logits(): pl.pallas_call(logits_kernel, out_shape=[shape((2, ve, nt), jnp.float32),...  10.2 us
    all_to_all x2, starting transfers between devices, plane_sum(): got = lax.all_to_all(blocks, axes, 0, 0, tiled=True)  8.13 us
    convert_element_type x1, other arithmetic, on_device(): return (hidden_grad, (ours + theirs).astype(jnp.bfloat16))  6.02 us
  transfers between devices with their start and end apart: 17, of which 8 were waited for; matrix products, arithmetic and copies ran while one was open for 9% of the time, Pallas kernels for 0%

profile of v2, /device:TPU:32, one launch (start us, length us, event | category | flops | bytes accessed | tf_op | source)
XLA Modules:
  0.0 139.7 jit_solution(17019061878133964907)
XLA Ops:
  2.2 17.5 %all_to_all.25 = bf16[8,2,6144]{2,1,0:T(2,128)(2,1)S(1)} all-to-all(bf16[8,2,6144]{2,1,0:T(2,128)(2,1)S(1)} %broadcast_in_dim.12), channel_id=1, replica_groups=mesh['x'=4,'zl'=2,'y'=4,'zh'=4,'c'=2] {'zl','zh'}, dimensions={0} | all-to-all | bytes 393216 | tf_op jit(solution)/shard_map/all_to_all | solution.py:18
  19.9 1.7 %collective-permute-start.8 = (bf16[16,3072]{1,0:T(8,128)(2,1)S(1)}, bf16[16,3072]{1,0:T(8,128)(2,1)S(1)}, u32[]{:S(2)}, u32[]{:S(2)}) collective-permute-start(bf16[16,3072]{1,0:T(8,128)(2,1)S(1)} %get-tuple-element.38), channel_id=1, source_target_pairs={{0,8},{8,16},{16,24},{24,0},{1,9},{9,17},{17,25},{25,1},{2,10},{10... | collective-permute-start | bytes 294920 | tf_op jit(solution)/shard_map/ppermute | solution.py:25
  21.5 1.7 %collective-permute-start.9 = (bf16[16,3072]{1,0:T(8,128)(2,1)S(1)}, bf16[16,3072]{1,0:T(8,128)(2,1)S(1)}, u32[]{:S(2)}, u32[]{:S(2)}) collective-permute-start(bf16[16,3072]{1,0:T(8,128)(2,1)S(1)} %get-tuple-element.38), channel_id=1, source_target_pairs={{0,24},{8,0},{16,8},{24,16},{1,25},{9,1},{17,9},{25,17},{2,26},{10... | collective-permute-start | bytes 294920 | tf_op jit(solution)/shard_map/ppermute | solution.py:25
  23.2 2.0 %collective-permute-start.10 = (bf16[16,3072]{1,0:T(8,128)(2,1)S(1)}, bf16[16,3072]{1,0:T(8,128)(2,1)S(1)}, u32[]{:S(2)}, u32[]{:S(2)}) collective-permute-start(bf16[16,3072]{1,0:T(8,128)(2,1)S(1)} %get-tuple-element.38), channel_id=1, source_target_pairs={{0,16},{8,24},{16,0},{24,8},{1,17},{9,25},{17,1},{25,9},{2,18},{10... | collective-permute-start | bytes 294920 | tf_op jit(solution)/shard_map/ppermute | solution.py:25
  26.6 1.7 %collective-permute-start.3 = (bf16[16,3072]{1,0:T(8,128)(2,1)S(1)}, bf16[16,3072]{1,0:T(8,128)(2,1)S(1)}, u32[]{:S(2)}, u32[]{:S(2)}) collective-permute-start(bf16[16,3072]{1,0:T(8,128)(2,1)S(1)} %get-tuple-element.39), channel_id=1, source_target_pairs={{0,192},{64,0},{128,64},{192,128},{1,193},{65,1},{129,65},{193,129... | collective-permute-start | bytes 294920 | tf_op jit(solution)/shard_map/ppermute | solution.py:25
  28.4 1.8 %collective-permute-start.4 = (bf16[16,3072]{1,0:T(8,128)(2,1)S(1)}, bf16[16,3072]{1,0:T(8,128)(2,1)S(1)}, u32[]{:S(2)}, u32[]{:S(2)}) collective-permute-start(bf16[16,3072]{1,0:T(8,128)(2,1)S(1)} %get-tuple-element.39), channel_id=1, source_target_pairs={{0,128},{64,192},{128,0},{192,64},{1,129},{65,193},{129,1},{193,65... | collective-permute-start | bytes 294920 | tf_op jit(solution)/shard_map/ppermute | solution.py:25
  30.9 2.6 %collective-permute-start.12 = (bf16[4,16,3072]{2,1,0:T(8,128)(2,1)S(1)}, bf16[4,16,3072]{2,1,0:T(8,128)(2,1)}, u32[]{:S(2)}, u32[]{:S(2)}) collective-permute-start(bf16[4,16,3072]{2,1,0:T(8,128)(2,1)S(1)} %pad_maximum_fusion.1.refs_4_), channel_id=1, source_target_pairs={{0,192},{64,0},{128,64},{192,128},{1,193},{65,1},{129,65},{193,129... | collective-permute-start | bytes 1179656 | tf_op jit(solution)/shard_map/ppermute | solution.py:25
  36.4 2.6 %collective-permute-start.6 = (bf16[4,16,3072]{2,1,0:T(8,128)(2,1)S(1)}, bf16[4,16,3072]{2,1,0:T(8,128)(2,1)}, u32[]{:S(2)}, u32[]{:S(2)}) collective-permute-start(bf16[4,16,3072]{2,1,0:T(8,128)(2,1)S(1)} %pad_maximum_fusion.refs_0_), channel_id=1, source_target_pairs={{0,24},{8,0},{16,8},{24,16},{1,25},{9,1},{17,9},{25,17},{2,26},{10... | collective-permute-start | bytes 1179656 | tf_op jit(solution)/shard_map/ppermute | solution.py:25
  39.0 4.5 %collective-permute-done.11.refs_5_ = bf16[4,16,3072]{2,1,0:T(8,128)(2,1)S(1)} collective-permute-done((bf16[4,16,3072]{2,1,0:T(8,128)(2,1)S(1)}, bf16[4,16,3072]{2,1,0:T(8,128)(2,1)S(1)}, u32[]{:S(2)}, u32[]{:S(2)}) %collective-permute-start.11) | collective-permute-done | bytes 393248 | tf_op jit(solution)/shard_map/ppermute | solution.py:25
  44.3 1.8 %collective-permute-start.7 = (bf16[4,16,3072]{2,1,0:T(8,128)(2,1)S(1)}, bf16[4,16,3072]{2,1,0:T(8,128)(2,1)}, u32[]{:S(2)}, u32[]{:S(2)}) collective-permute-start(bf16[4,16,3072]{2,1,0:T(8,128)(2,1)S(1)} %pad_maximum_fusion.refs_0_), channel_id=1, source_target_pairs={{0,16},{8,24},{16,0},{24,8},{1,17},{9,25},{17,1},{25,9},{2,18},{10... | collective-permute-start | bytes 1179656 | tf_op jit(solution)/shard_map/ppermute | solution.py:25
  48.5 1.5 %collective-permute-done.13.refs_7_ = bf16[4,16,3072]{2,1,0:T(8,128)(2,1)} collective-permute-done((bf16[4,16,3072]{2,1,0:T(8,128)(2,1)S(1)}, bf16[4,16,3072]{2,1,0:T(8,128)(2,1)}, u32[]{:S(2)}, u32[]{:S(2)}) %collective-permute-start.13) | collective-permute-done | bytes 393248 | tf_op jit(solution)/shard_map/ppermute | solution.py:25
  50.0 2.8 %collective-permute-done.6.refs_2_ = bf16[4,16,3072]{2,1,0:T(8,128)(2,1)} collective-permute-done((bf16[4,16,3072]{2,1,0:T(8,128)(2,1)S(1)}, bf16[4,16,3072]{2,1,0:T(8,128)(2,1)}, u32[]{:S(2)}, u32[]{:S(2)}) %collective-permute-start.6) | collective-permute-done | bytes 393248 | tf_op jit(solution)/shard_map/ppermute | solution.py:25
  53.7 2.4 %copy-done.1 = bf16[592,4096]{1,0:T(8,128)(2,1)S(1)} copy-done((bf16[592,4096]{1,0:T(8,128)(2,1)S(1)}, bf16[592,4096]{1,0:T(8,128)(2,1)}, u32[]{:S(2)}) %copy-start.1) | copy-done | bytes 4849688
  59.0 10.2 %shard_map.68 = (f32[2,592,256]{2,1,0:T(8,128)S(1)}, f32[2,592,256]{2,1,0:T(8,128)S(1)}, f32[4,256]{1,0:T(4,128)S(1)}, bf16[256,2048]{1,0:T(8,128)(2,1)S(1)}) custom-call(s32[2]{0:T(128)S(1)} %pad_add_fusion.at, bf16[4,16,3072]{2,1,0:T(8,128)(2,1)S(1)} %copy-done.6, bf16[4,16,3072]{2,1,0:T(8,128)(2,1)} %collective-permute-done.5.refs_1_, ...), custom_call_target="tpu_custom_call" | custom-call | flops 3724541952 | bytes 17694720 | tf_op jit(solution)/shard_map/pallas_call | solution.py:92
  71.4 12.9 %all_to_all.26 = f32[16,3,256]{2,1,0:T(4,128)S(1)} all-to-all(f32[16,3,256]{2,1,0:T(4,128)S(1)} %broadcast_in_dim.15), channel_id=1, replica_groups=mesh['x'=4,'zl'=2,'y'=4,'zh'=4,'c'=2] {'x','y'}, dimensions={0} | all-to-all | bytes 98304 | tf_op jit(solution)/shard_map/all_to_all | solution.py:18
  84.5 9.7 %all_to_all.27 = f32[8,3,256]{2,1,0:T(4,128)S(1)} all-to-all(f32[8,3,256]{2,1,0:T(4,128)S(1)} %broadcast_in_dim.17), channel_id=1, replica_groups=mesh['x'=4,'zl'=2,'y'=4,'zh'=4,'c'=2] {'zl','zh'}, dimensions={0} | all-to-all | bytes 49152 | tf_op jit(solution)/shard_map/all_to_all | solution.py:18
  96.9 3.6 %shard_map.69 = (bf16[2,592,256]{2,1,0:T(8,128)(2,1)S(1)}, bf16[256,2048]{1,0:T(8,128)(2,1)S(1)}) custom-call(f32[2,592,256]{2,1,0:T(8,128)S(1)} %copy-done.8, f32[2,592,256]{2,1,0:T(8,128)S(1)} %copy-done.10, f32[2,256]{1,0:T(2,128)S(1)} %exponential_multiply_fusion.scale, bf16[592,2048]{1,0:T(8,128)(2,1)S(1)} %copy-done, ...), custom_call_target="tpu_custom_call" | custom-call | flops 1241513984 | bytes 7274496 | tf_op jit(solution)/shard_map/pallas_call | solution.py:137
  100.5 3.0 %fusion = f32[592,2048]{1,0:T(8,128)} fusion(bf16[256,2048]{1,0:T(8,128)(2,1)S(1)} %get-tuple-element.32, bf16[2,592,256]{2,1,0:T(8,128)(2,1)S(1)} %get-tuple-element.31), kind=kOutput, calls=%fused_computation.4 | convolution fusion | flops 620756992 | bytes 6201344 | tf_op jit(solution)/shard_map/dot_general | solution.py:182
  103.5 3.7 %all-to-all-start.3 = ((bf16[16,16,2048]{2,1,0:T(8,128)(2,1)}), bf16[16,16,2048]{2,1,0:T(8,128)(2,1)S(1)}, u32[]{:S(2)}, u32[]{:S(2)}) async-start(bf16[16,16,2048]{2,1,0:T(8,128)(2,1)} %bitcast.23), calls=%async_computation.3 | async-start | bytes 2097152 | tf_op jit(solution)/shard_map/all_to_all | solution.py:31
  107.2 3.9 %fusion.2 = f32[592,2048]{1,0:T(8,128)} fusion(bf16[256,2048]{1,0:T(8,128)(2,1)S(1)} %get-tuple-element.32, bf16[2,592,256]{2,1,0:T(8,128)(2,1)} %copy-done.2), kind=kOutput, calls=%fused_computation.6 | convolution fusion | flops 620756992 | bytes 6201344 | tf_op jit(solution)/shard_map/dot_general | solution.py:183
  111.1 15.0 %all-to-all-done.3 = bf16[16,16,2048]{2,1,0:T(8,128)(2,1)S(1)} async-done(((bf16[16,16,2048]{2,1,0:T(8,128)(2,1)}), bf16[16,16,2048]{2,1,0:T(8,128)(2,1)S(1)}, u32[]{:S(2)}, u32[]{:S(2)}) %all-to-all-start.3) | async-done | bytes 1048608 | tf_op jit(solution)/shard_map/all_to_all | solution.py:31
  127.0 4.5 %all-to-all-start.4 = ((f32[8,2,2048]{2,1,0:T(2,128)}), f32[8,2,2048]{2,1,0:T(2,128)S(1)}, u32[]{:S(2)}, u32[]{:S(2)}) async-start(f32[8,2,2048]{2,1,0:T(2,128)} %reshape.23), calls=%async_computation.4 | async-start | bytes 262144 | tf_op jit(solution)/shard_map/all_to_all | solution.py:31
  131.5 6.0 %add_convert_fusion = bf16[592,2048]{1,0:T(8,128)(2,1)} fusion(f32[592,2048]{1,0:T(8,128)} %fusion.2, f32[592,2048]{1,0:T(8,128)} %collective-permute-done.14), kind=kLoop, calls=%fused_computation | loop fusion | flops 2424832 | bytes 12124160 | tf_op jit(solution)/shard_map/convert_element_type | solution.py:186
  137.5 1.6 %all-to-all-done.4 = f32[8,2,2048]{2,1,0:T(2,128)S(1)} async-done(((f32[8,2,2048]{2,1,0:T(2,128)}), f32[8,2,2048]{2,1,0:T(2,128)S(1)}, u32[]{:S(2)}, u32[]{:S(2)}) %all-to-all-start.4) | async-done | bytes 131104 | tf_op jit(solution)/shard_map/all_to_all | solution.py:31
  (73 shorter events, 20.2 us)
Async XLA Ops:
  0.6 53.0 %copy-start = (bf16[592,2048]{1,0:T(8,128)(2,1)S(1)}, bf16[592,2048]{1,0:T(8,128)(2,1)}, u32[]{:S(2)}) copy-start(bf16[592,2048]{1,0:T(8,128)(2,1)} %head0) | copy-start | bytes 7274500
  0.6 19.2 %collective-permute-start = (bf16[592,4096]{1,0:T(8,128)(2,1)}, bf16[592,4096]{1,0:T(8,128)(2,1)}, u32[]{:S(2)}, u32[]{:S(2)}) collective-permute-start(bf16[592,4096]{1,0:T(8,128)(2,1)} %refs_8_), channel_id=1, source_target_pairs={{0,1},{1,0},{2,3},{3,2},{4,5},{5,4},{6,7},{7,6},{8,9},{9,8},{10,11... | collective-permute-start | bytes 14549000 | tf_op jit(solution)/shard_map/ppermute | solution.py:36
  0.7 19.1 %collective-permute-start.1 = (bf16[592,2048]{1,0:T(8,128)(2,1)}, bf16[592,2048]{1,0:T(8,128)(2,1)}, u32[]{:S(2)}, u32[]{:S(2)}) collective-permute-start(bf16[592,2048]{1,0:T(8,128)(2,1)} %head0), channel_id=1, source_target_pairs={{0,1},{1,0},{2,3},{3,2},{4,5},{5,4},{6,7},{7,6},{8,9},{9,8},{10,11... | collective-permute-start | bytes 7274504 | tf_op jit(solution)/shard_map/ppermute | solution.py:36
  19.9 8.5 %collective-permute-start.8 = (bf16[16,3072]{1,0:T(8,128)(2,1)S(1)}, bf16[16,3072]{1,0:T(8,128)(2,1)S(1)}, u32[]{:S(2)}, u32[]{:S(2)}) collective-permute-start(bf16[16,3072]{1,0:T(8,128)(2,1)S(1)} %get-tuple-element.38), channel_id=1, source_target_pairs={{0,8},{8,16},{16,24},{24,0},{1,9},{9,17},{17,25},{25,1},{2,10},{10... | collective-permute-start | bytes 294920 | tf_op jit(solution)/shard_map/ppermute | solution.py:25
  21.5 8.7 %collective-permute-start.9 = (bf16[16,3072]{1,0:T(8,128)(2,1)S(1)}, bf16[16,3072]{1,0:T(8,128)(2,1)S(1)}, u32[]{:S(2)}, u32[]{:S(2)}) collective-permute-start(bf16[16,3072]{1,0:T(8,128)(2,1)S(1)} %get-tuple-element.38), channel_id=1, source_target_pairs={{0,24},{8,0},{16,8},{24,16},{1,25},{9,1},{17,9},{25,17},{2,26},{10... | collective-permute-start | bytes 294920 | tf_op jit(solution)/shard_map/ppermute | solution.py:25
  23.2 7.0 %collective-permute-start.10 = (bf16[16,3072]{1,0:T(8,128)(2,1)S(1)}, bf16[16,3072]{1,0:T(8,128)(2,1)S(1)}, u32[]{:S(2)}, u32[]{:S(2)}) collective-permute-start(bf16[16,3072]{1,0:T(8,128)(2,1)S(1)} %get-tuple-element.38), channel_id=1, source_target_pairs={{0,16},{8,24},{16,0},{24,8},{1,17},{9,25},{17,1},{25,9},{2,18},{10... | collective-permute-start | bytes 294920 | tf_op jit(solution)/shard_map/ppermute | solution.py:25
  25.1 8.4 %collective-permute-start.2 = (bf16[16,3072]{1,0:T(8,128)(2,1)S(1)}, bf16[16,3072]{1,0:T(8,128)(2,1)S(1)}, u32[]{:S(2)}, u32[]{:S(2)}) collective-permute-start(bf16[16,3072]{1,0:T(8,128)(2,1)S(1)} %get-tuple-element.39), channel_id=1, source_target_pairs={{0,64},{64,128},{128,192},{192,0},{1,65},{65,129},{129,193},{193,1... | collective-permute-start | bytes 294920 | tf_op jit(solution)/shard_map/ppermute | solution.py:25
  26.6 7.8 %collective-permute-start.3 = (bf16[16,3072]{1,0:T(8,128)(2,1)S(1)}, bf16[16,3072]{1,0:T(8,128)(2,1)S(1)}, u32[]{:S(2)}, u32[]{:S(2)}) collective-permute-start(bf16[16,3072]{1,0:T(8,128)(2,1)S(1)} %get-tuple-element.39), channel_id=1, source_target_pairs={{0,192},{64,0},{128,64},{192,128},{1,193},{65,1},{129,65},{193,129... | collective-permute-start | bytes 294920 | tf_op jit(solution)/shard_map/ppermute | solution.py:25
  28.4 7.2 %collective-permute-start.4 = (bf16[16,3072]{1,0:T(8,128)(2,1)S(1)}, bf16[16,3072]{1,0:T(8,128)(2,1)S(1)}, u32[]{:S(2)}, u32[]{:S(2)}) collective-permute-start(bf16[16,3072]{1,0:T(8,128)(2,1)S(1)} %get-tuple-element.39), channel_id=1, source_target_pairs={{0,128},{64,192},{128,0},{192,64},{1,129},{65,193},{129,1},{193,65... | collective-permute-start | bytes 294920 | tf_op jit(solution)/shard_map/ppermute | solution.py:25
  30.3 22.5 %copy-start.3 = (bf16[4,16,3072]{2,1,0:T(8,128)(2,1)}, bf16[4,16,3072]{2,1,0:T(8,128)(2,1)S(1)}, u32[]{:S(2)}) copy-start(bf16[4,16,3072]{2,1,0:T(8,128)(2,1)S(1)} %pad_maximum_fusion.1.refs_4_) | copy-start | bytes 1179652
  30.3 13.2 %collective-permute-start.11 = (bf16[4,16,3072]{2,1,0:T(8,128)(2,1)S(1)}, bf16[4,16,3072]{2,1,0:T(8,128)(2,1)S(1)}, u32[]{:S(2)}, u32[]{:S(2)}) collective-permute-start(bf16[4,16,3072]{2,1,0:T(8,128)(2,1)S(1)} %pad_maximum_fusion.1.refs_4_), channel_id=1, source_target_pairs={{0,64},{64,128},{128,192},{192,0},{1,65},{65,129},{129,193},{193,1... | collective-permute-start | bytes 1179656 | tf_op jit(solution)/shard_map/ppermute | solution.py:25
  30.9 17.5 %collective-permute-start.12 = (bf16[4,16,3072]{2,1,0:T(8,128)(2,1)S(1)}, bf16[4,16,3072]{2,1,0:T(8,128)(2,1)}, u32[]{:S(2)}, u32[]{:S(2)}) collective-permute-start(bf16[4,16,3072]{2,1,0:T(8,128)(2,1)S(1)} %pad_maximum_fusion.1.refs_4_), channel_id=1, source_target_pairs={{0,192},{64,0},{128,64},{192,128},{1,193},{65,1},{129,65},{193,129... | collective-permute-start | bytes 1179656 | tf_op jit(solution)/shard_map/ppermute | solution.py:25
  33.6 16.4 %collective-permute-start.13 = (bf16[4,16,3072]{2,1,0:T(8,128)(2,1)S(1)}, bf16[4,16,3072]{2,1,0:T(8,128)(2,1)}, u32[]{:S(2)}, u32[]{:S(2)}) collective-permute-start(bf16[4,16,3072]{2,1,0:T(8,128)(2,1)S(1)} %pad_maximum_fusion.1.refs_4_), channel_id=1, source_target_pairs={{0,128},{64,192},{128,0},{192,64},{1,129},{65,193},{129,1},{193,65... | collective-permute-start | bytes 1179656 | tf_op jit(solution)/shard_map/ppermute | solution.py:25
  35.7 14.3 %collective-permute-start.5 = (bf16[4,16,3072]{2,1,0:T(8,128)(2,1)S(1)}, bf16[4,16,3072]{2,1,0:T(8,128)(2,1)}, u32[]{:S(2)}, u32[]{:S(2)}) collective-permute-start(bf16[4,16,3072]{2,1,0:T(8,128)(2,1)S(1)} %pad_maximum_fusion.refs_0_), channel_id=1, source_target_pairs={{0,8},{8,16},{16,24},{24,0},{1,9},{9,17},{17,25},{25,1},{2,10},{10... | collective-permute-start | bytes 1179656 | tf_op jit(solution)/shard_map/ppermute | solution.py:25
  36.4 16.3 %collective-permute-start.6 = (bf16[4,16,3072]{2,1,0:T(8,128)(2,1)S(1)}, bf16[4,16,3072]{2,1,0:T(8,128)(2,1)}, u32[]{:S(2)}, u32[]{:S(2)}) collective-permute-start(bf16[4,16,3072]{2,1,0:T(8,128)(2,1)S(1)} %pad_maximum_fusion.refs_0_), channel_id=1, source_target_pairs={{0,24},{8,0},{16,8},{24,16},{1,25},{9,1},{17,9},{25,17},{2,26},{10... | collective-permute-start | bytes 1179656 | tf_op jit(solution)/shard_map/ppermute | solution.py:25
  44.3 9.4 %collective-permute-start.7 = (bf16[4,16,3072]{2,1,0:T(8,128)(2,1)S(1)}, bf16[4,16,3072]{2,1,0:T(8,128)(2,1)}, u32[]{:S(2)}, u32[]{:S(2)}) collective-permute-start(bf16[4,16,3072]{2,1,0:T(8,128)(2,1)S(1)} %pad_maximum_fusion.refs_0_), channel_id=1, source_target_pairs={{0,16},{8,24},{16,0},{24,8},{1,17},{9,25},{17,1},{25,9},{2,18},{10... | collective-permute-start | bytes 1179656 | tf_op jit(solution)/shard_map/ppermute | solution.py:25
  53.7 2.4 %copy-start.1 = (bf16[592,4096]{1,0:T(8,128)(2,1)S(1)}, bf16[592,4096]{1,0:T(8,128)(2,1)}, u32[]{:S(2)}) copy-start(bf16[592,4096]{1,0:T(8,128)(2,1)} %refs_8_) | copy-start | bytes 14548996
  94.3 1.3 copy-start.8
  95.6 1.3 copy-start.10
  100.5 3.0 %copy-start.2 = (bf16[2,592,256]{2,1,0:T(8,128)(2,1)}, bf16[2,592,256]{2,1,0:T(8,128)(2,1)S(1)}, u32[]{:S(2)}) copy-start(bf16[2,592,256]{2,1,0:T(8,128)(2,1)S(1)} %get-tuple-element.31) | copy-start | bytes 1818628
  100.5 3.0 %copy-start.11 = (bf16[256,2048]{1,0:T(8,128)(2,1)}, bf16[256,2048]{1,0:T(8,128)(2,1)S(1)}, u32[]{:S(2)}) copy-start(bf16[256,2048]{1,0:T(8,128)(2,1)S(1)} %get-tuple-element.30) | copy-start | bytes 3145732
  103.5 23.5 %collective-permute-start.14 = (f32[592,2048]{1,0:T(8,128)}, f32[592,2048]{1,0:T(8,128)}, u32[]{:S(2)}, u32[]{:S(2)}) collective-permute-start(f32[592,2048]{1,0:T(8,128)} %fusion), channel_id=1, source_target_pairs={{0,1},{1,0},{2,3},{3,2},{4,5},{5,4},{6,7},{7,6},{8,9},{9,8},{10,11... | collective-permute-start | bytes 14549000 | tf_op jit(solution)/shard_map/ppermute | solution.py:36
  103.5 22.6 %all-to-all-start.3 = ((bf16[16,16,2048]{2,1,0:T(8,128)(2,1)}), bf16[16,16,2048]{2,1,0:T(8,128)(2,1)S(1)}, u32[]{:S(2)}, u32[]{:S(2)}) async-start(bf16[16,16,2048]{2,1,0:T(8,128)(2,1)} %bitcast.23), calls=%async_computation.3 | async-start | bytes 2097152 | tf_op jit(solution)/shard_map/all_to_all | solution.py:31
  127.0 12.1 %all-to-all-start.4 = ((f32[8,2,2048]{2,1,0:T(2,128)}), f32[8,2,2048]{2,1,0:T(2,128)S(1)}, u32[]{:S(2)}, u32[]{:S(2)}) async-start(f32[8,2,2048]{2,1,0:T(2,128)} %reshape.23), calls=%async_computation.4 | async-start | bytes 262144 | tf_op jit(solution)/shard_map/all_to_all | solution.py:31
  (7 other events, 6.6 us)

commit v3 on v2

v3 whole, which is shorter than its diff:
```python
import jax
import jax.numpy as jnp
from jax import lax
from jax.experimental import pallas as pl
from jax.experimental.pallas import tpu as pltpu
from jax.sharding import Mesh, PartitionSpec as P

AXES = ("x", "zl", "y", "zh", "c")
SIZES = (4, 2, 4, 4, 2)
PLANE, LINE, PAIR = ("x", "y"), ("zl", "zh"), ("c",)
NP, NL = 16, 8
STEPS = (0, 1, 3, 2)
VMEM_LIMIT = 62 * 2**20
HBM, SMEM = pl.BlockSpec(memory_space=pltpu.HBM), pl.BlockSpec(memory_space=pltpu.SMEM)
VMEM = pl.BlockSpec(memory_space=pltpu.VMEM)
WIDE = 2048


def share(block, axes, n):
    return lax.all_to_all(
        jnp.broadcast_to(block[None], (n,) + block.shape), axes, 0, 0, tiled=True
    )


def ring(block, axis):
    return [block] + [
        lax.ppermute(block, axis, [(i, (i + step) % 4) for i in range(4)])
        for step in STEPS[1:]
    ]


def join(rows, nt):
    logs = rows[:, :, : 2 * nt]
    top = jnp.max(logs, 0)
    logs = top + jnp.log(jnp.sum(jnp.exp(logs - top), 0))
    return jnp.concatenate([logs, jnp.sum(rows[:, :, 2 * nt :], 0)], 1)


def plane_sum(blocks, axes):
    got = lax.all_to_all(blocks, axes, 0, 0, tiled=True)
    return jnp.sum(got.astype(jnp.float32), 0)


def swap(block):
    return lax.ppermute(block, PAIR, [(0, 1), (1, 0)])


def logits_kernel(at, weight, *refs):
    first, second = refs[:4], refs[4:8]
    heads = refs[8:12]
    teach_out, stud_out, rows_out, logs_out, base_out = refs[12:17]
    hidden, held, terms, sem, out_sem = refs[17:]
    x, y = at[0], at[1]
    half = WIDE // 2
    copies = []

    def block(src, lo, dst, col, n, row):
        copies.append(
            pltpu.make_async_copy(
                src.at[:, pl.ds(lo, n)],
                dst.at[pl.ds(row, 16), pl.ds(col, n)],
                sem.at[len(copies)],
            )
        )

    for k in range(4):
        for j in range(4):
            row = ((x - STEPS[j]) % 4 * 4 + (y - STEPS[k]) % 4) * 16
            block(first[k].at[j], 0, hidden.at[1], 0, WIDE, row)
            block(first[k].at[j], WIDE, hidden.at[2], 0, half, row)
            row = ((x - STEPS[k]) % 4 * 4 + (y - STEPS[j]) % 4) * 16
            block(second[k].at[j], 0, hidden.at[2], half, half, row)
            block(second[k].at[j], half, hidden.at[0], 0, WIDE, row)
    loads = []
    for h in range(2):
        for head, lo in ((heads[2 + h], 0), (heads[h], 0), (heads[h], WIDE)):
            n = len(loads)
            loads.append(
                pltpu.make_async_copy(
                    head.at[:, pl.ds(lo, WIDE)], held.at[n], sem.at[64 + n]
                )
            )
    for copy in copies + loads[:2]:
        copy.start()
    terms[...] = jnp.zeros_like(terms)
    for copy in copies:
        copy.wait()
    rows = pltpu.make_async_copy(hidden.at[0], rows_out, out_sem.at[0])
    rows.start()

    nt = NP * 16

    def finish(i):
        mine = terms.at[2 * i : 2 * i + 2]
        peak = jnp.max(jnp.max(mine[...], 0), 0, keepdims=True)
        value = jnp.exp(mine[...] - peak)
        mine[...] = value
        outs[i].start()
        total = jnp.sum(jnp.sum(value, 0), 0, keepdims=True)
        logs_out[:, i * nt : (i + 1) * nt] = peak + jnp.log(total)
        base_out[i : i + 1] = peak

    outs = [
        pltpu.make_async_copy(terms.at[2 * i : 2 * i + 2], out, out_sem.at[1 + i])
        for i, out in enumerate((stud_out, teach_out))
    ]

    @pl.loop(0, 6)
    def _(n):
        for i in range(6):

            @pl.when(n == i)
            def _():
                loads[i].wait()
                if i + 2 < 6:
                    loads[i + 2].start()

        j = n % 3
        terms[n // 3 + jnp.where(j > 0, 2, 0)] += lax.dot_general(
            held[n], hidden[j], (((1,), (1,)), ((), ())), preferred_element_type=jnp.float32
        )

        @pl.when(n == 3)
        def _():
            finish(0)

    finish(1)
    logs_out[:, 2 * nt :] = weight[...]
    rows.wait()
    for copy in outs:
        copy.wait()


def logits(at, weight, first, second, heads):
    ve, nt = heads[0].shape[0], NP * 16
    shape = jax.ShapeDtypeStruct
    return pl.pallas_call(
        logits_kernel,
        out_shape=[
            shape((2, ve, nt), jnp.float32),
            shape((2, ve, nt), jnp.float32),
            shape((nt, WIDE), jnp.bfloat16),
            shape((1, 3 * nt), jnp.float32),
            shape((2, nt), jnp.float32),
        ],
        in_specs=[SMEM, VMEM] + [HBM] * 12,
        out_specs=[HBM] * 3 + [VMEM] * 2,
        scratch_shapes=[
            pltpu.VMEM((3, nt, WIDE), jnp.bfloat16),
            pltpu.VMEM((6, ve, WIDE), jnp.bfloat16),
            pltpu.VMEM((4, ve, nt), jnp.float32),
            pltpu.SemaphoreType.DMA((70,)),
            pltpu.SemaphoreType.DMA((3,)),
        ],
        compiler_params=pltpu.CompilerParams(vmem_limit_bytes=VMEM_LIMIT),
        cost_estimate=pl.CostEstimate(
            flops=2 * 2 * ve * nt * 3 * WIDE,
            bytes_accessed=2 * ve * 3 * WIDE * 2 + nt * 3 * WIDE * 2,
            transcendentals=4 * ve * nt,
        ),
    )(at, weight, *first, *second, *heads)


def grad_kernel(teach, stud, head0, head1, rows, logs, base, *refs):
    ours_out, theirs_out, part_out = refs[:3]
    terms_t, terms_s, held, row, grad, theirs, sem, out_sem = refs[3:]
    pairs = []
    for h in (1, 0):
        pairs += [(stud.at[h], terms_s.at[h]), (teach.at[h], terms_t.at[h])]
    pairs.insert(2, (rows, row))
    pairs += [(head1, held.at[1]), (head0, held.at[0])]
    loads = [
        pltpu.make_async_copy(src, dst, sem.at[i]) for i, (src, dst) in enumerate(pairs)
    ]
    for copy in loads:
        copy.start()
    nt = base.shape[1]
    weight = logs[:, 2 * nt :]
    scale = [
        weight * jnp.exp(base[i : i + 1] - logs[:, i * nt : (i + 1) * nt]) for i in range(2)
    ]

    def gradient(h):
        grad[h] = (terms_s[h] * scale[0] - terms_t[h] * scale[1]).astype(jnp.bfloat16)

    loads[0].wait()
    loads[1].wait()
    gradient(1)
    loads[2].wait()

    @pl.loop(0, 4)
    def _(n):
        cols = pl.ds(pl.multiple_of(n * 512, 512), 512)
        theirs[:, cols] = jnp.dot(
            grad[1], row[:, cols], preferred_element_type=jnp.float32
        ).astype(theirs.dtype)

    outs = [pltpu.make_async_copy(theirs, theirs_out, out_sem.at[0])]
    outs[0].start()
    loads[3].wait()
    loads[4].wait()
    gradient(0)
    outs.append(pltpu.make_async_copy(grad.at[0], ours_out, out_sem.at[1]))
    outs[1].start()
    loads[5].wait()
    loads[6].wait()

    @pl.loop(0, 4)
    def _(n):
        cols = pl.ds(pl.multiple_of(n * 512, 512), 512)
        total = sum(
            lax.dot_general(
                grad[h],
                held[h, :, cols],
                (((0,), (0,)), ((), ())),
                preferred_element_type=jnp.float32,
            )
            for h in range(2)
        )
        part_out[:, cols] = total.astype(part_out.dtype)

    for copy in outs:
        copy.wait()


def grads(teach, stud, head0, head1, rows, logs, base):
    ve, nt = teach.shape[1:]
    shape = jax.ShapeDtypeStruct
    return pl.pallas_call(
        grad_kernel,
        out_shape=[
            shape((ve, nt), jnp.bfloat16),
            shape((ve, WIDE), jnp.bfloat16),
            shape((nt, WIDE), jnp.bfloat16),
        ],
        in_specs=[HBM] * 5 + [VMEM] * 2,
        out_specs=[HBM] * 2 + [VMEM],
        scratch_shapes=[
            pltpu.VMEM((2, ve, nt), jnp.float32),
            pltpu.VMEM((2, ve, nt), jnp.float32),
            pltpu.VMEM((2, ve, WIDE), jnp.bfloat16),
            pltpu.VMEM((nt, WIDE), jnp.bfloat16),
            pltpu.VMEM((2, ve, nt), jnp.bfloat16),
            pltpu.VMEM((ve, WIDE), jnp.bfloat16),
            pltpu.SemaphoreType.DMA((7,)),
            pltpu.SemaphoreType.DMA((2,)),
        ],
        compiler_params=pltpu.CompilerParams(vmem_limit_bytes=VMEM_LIMIT),
        cost_estimate=pl.CostEstimate(
            flops=3 * 2 * ve * nt * WIDE,
            bytes_accessed=2 * ve * WIDE * 2 + 2 * 2 * ve * nt * 4 + ve * WIDE * 2,
            transcendentals=0,
        ),
    )(teach, stud, head0, head1, rows, logs, base)


def on_device(teacher_hidden, student_hidden, teacher_head, student_head, loss_weight):
    tok, dt = teacher_hidden.shape
    ds = student_hidden.shape[1]
    nt = tok * NP * NL
    heads = (teacher_head, swap(teacher_head), student_head, swap(student_head))

    x, y = lax.axis_index("x"), lax.axis_index("y")
    mine = jnp.concatenate([teacher_hidden, student_hidden], 1)
    line = share(mine, LINE, NL).reshape(NL * tok, -1)
    line, heads = lax.optimization_barrier((line, heads))
    half = (dt + ds) // 2
    z = lax.axis_index("zl") * 4 + lax.axis_index("zh")
    weight = lax.dynamic_update_slice(
        jnp.zeros((1, nt), jnp.float32), loss_weight[None], (0, ((x * 4 + y) * NL + z) * tok)
    )
    second = ring(jnp.stack(ring(line[:, half:], "y")), "x")
    first = ring(jnp.stack(ring(line[:, :half], "x")), "y")
    teach, stud, rows, logs, base = logits(jnp.stack([x, y]), weight, first, second, heads)
    logs = join(share(join(share(logs, PLANE, NP), nt), LINE, NL), nt)
    grad, theirs, part = grads(teach, stud, heads[2], heads[3], rows, logs, base)

    theirs = swap(theirs)
    part = plane_sum(part.reshape(NP, NL * tok, ds), PLANE).reshape(NL, tok, ds)
    ours = jnp.dot(grad, rows, preferred_element_type=jnp.float32)
    part, ours, theirs = lax.optimization_barrier((part, ours, theirs))
    hidden_grad = plane_sum(part, LINE)
    return hidden_grad, (ours + theirs).astype(jnp.bfloat16)


def solution(mesh):
    fine = Mesh(mesh.devices.reshape(SIZES), AXES)
    split = P(AXES, None)
    return jax.shard_map(
        on_device,
        mesh=fine,
        in_specs=(split, split, split, split, P(AXES)),
        out_specs=(split, split),
        check_vma=False,
    )
```

time: 141 us -> 138 us (0.979)
  local copies, waits for them, and re-layouts: 13.4 us -> 2 us
  Pallas kernels: 13.8 us -> 19.6 us
  waiting for transfers between devices: 28.1 us -> 32.7 us
  matrix products: 6.97 us -> 2.97 us
    unnamed x28 -> x22, local copies, waits for them, and re-layouts: 11.5 us -> 0.82 us
    pallas_call x1, Pallas kernels: 3.56 us -> 7.61 us  [grads(): pl.pallas_call(grad_kernel, out_shape=[shape((ve, nt), jnp.bfloat16), sha...]
    dot_general x2 -> x1, matrix products: 6.97 us -> 2.97 us  [on_device(): ours = jnp.dot(grad, rows, preferred_element_type=jnp.float32)]
    ppermute x12, waiting for transfers between devices: 11.6 us -> 14.9 us  [ring(): lax.ppermute(block, axis, [(i, (i + step) % 4) for i in range(4)])]
    pallas_call x1, Pallas kernels: 10.2 us -> 12 us  [logits(): pl.pallas_call(logits_kernel, out_shape=[shape((2, ve, nt), jnp.float32),...]
  transfers between devices with their start and end apart: 17 -> 17, of which waited for: 8 -> 9; matrix products, arithmetic and copies ran while one was open for 9% -> 8% of each run, Pallas kernels for 0% -> 0%
where the time goes in v3:
time: 138 us; the launch traced here: 137 us
  blocking collectives  41 us (30%)
  waiting for transfers between devices  32.7 us (24%)
  starting transfers between devices  28.8 us (21%)
  Pallas kernels  19.6 us (14%)
  other arithmetic  9.23 us (7%)
  matrix products  2.97 us (2%)
  local copies, waits for them, and re-layouts  2 us (1%)
    all_to_all x3, blocking collectives, share(): lax.all_to_all(jnp.broadcast_to(block[None], (n,) + block.shape), axes, 0...  41 us
    ppermute x12, starting transfers between devices, ring(): lax.ppermute(block, axis, [(i, (i + step) % 4) for i in range(4)])  19.7 us
    all_to_all x2, waiting for transfers between devices, plane_sum(): got = lax.all_to_all(blocks, axes, 0, 0, tiled=True)  17.8 us
    ppermute x12, waiting for transfers between devices, ring(): lax.ppermute(block, axis, [(i, (i + step) % 4) for i in range(4)])  14.9 us
    pallas_call x1, Pallas kernels, logits(): pl.pallas_call(logits_kernel, out_shape=[shape((2, ve, nt), jnp.float32),...  12 us
    all_to_all x2, starting transfers between devices, plane_sum(): got = lax.all_to_all(blocks, axes, 0, 0, tiled=True)  8.4 us
    pallas_call x1, Pallas kernels, grads(): pl.pallas_call(grad_kernel, out_shape=[shape((ve, nt), jnp.bfloat16), sha...  7.61 us
    convert_element_type x1, other arithmetic, on_device(): return (hidden_grad, (ours + theirs).astype(jnp.bfloat16))  5.45 us
  transfers between devices with their start and end apart: 17, of which 9 were waited for; matrix products, arithmetic and copies ran while one was open for 8% of the time, Pallas kernels for 0%

profile of v3, /device:TPU:32, one launch (start us, length us, event | category | flops | bytes accessed | tf_op | source)
XLA Modules:
  0.0 137.1 jit_solution(1198699366308155447)
XLA Ops:
  2.1 17.6 %all_to_all.25 = bf16[8,2,6144]{2,1,0:T(2,128)(2,1)S(1)} all-to-all(bf16[8,2,6144]{2,1,0:T(2,128)(2,1)S(1)} %broadcast_in_dim.32), channel_id=1, replica_groups=mesh['x'=4,'zl'=2,'y'=4,'zh'=4,'c'=2] {'zl','zh'}, dimensions={0} | all-to-all | bytes 393216 | tf_op jit(solution)/shard_map/all_to_all | solution.py:20
  19.9 2.8 %collective-permute-start.3 = (bf16[16,3072]{1,0:T(8,128)(2,1)S(1)}, bf16[16,3072]{1,0:T(8,128)(2,1)S(1)}, u32[]{:S(2)}, u32[]{:S(2)}) collective-permute-start(bf16[16,3072]{1,0:T(8,128)(2,1)S(1)} %get-tuple-element.37), channel_id=1, source_target_pairs={{0,192},{64,0},{128,64},{192,128},{1,193},{65,1},{129,65},{193,129... | collective-permute-start | bytes 294920 | tf_op jit(solution)/shard_map/ppermute | solution.py:27
  22.7 2.3 %collective-permute-start.4 = (bf16[16,3072]{1,0:T(8,128)(2,1)S(1)}, bf16[16,3072]{1,0:T(8,128)(2,1)S(1)}, u32[]{:S(2)}, u32[]{:S(2)}) collective-permute-start(bf16[16,3072]{1,0:T(8,128)(2,1)S(1)} %get-tuple-element.37), channel_id=1, source_target_pairs={{0,128},{64,192},{128,0},{192,64},{1,129},{65,193},{129,1},{193,65... | collective-permute-start | bytes 294920 | tf_op jit(solution)/shard_map/ppermute | solution.py:27
  25.0 3.0 %collective-permute-start.9 = (bf16[16,3072]{1,0:T(8,128)(2,1)S(1)}, bf16[16,3072]{1,0:T(8,128)(2,1)S(1)}, u32[]{:S(2)}, u32[]{:S(2)}) collective-permute-start(bf16[16,3072]{1,0:T(8,128)(2,1)S(1)} %get-tuple-element.36), channel_id=1, source_target_pairs={{0,24},{8,0},{16,8},{24,16},{1,25},{9,1},{17,9},{25,17},{2,26},{10... | collective-permute-start | bytes 294920 | tf_op jit(solution)/shard_map/ppermute | solution.py:27
  28.0 2.2 %collective-permute-start.10 = (bf16[16,3072]{1,0:T(8,128)(2,1)S(1)}, bf16[16,3072]{1,0:T(8,128)(2,1)S(1)}, u32[]{:S(2)}, u32[]{:S(2)}) collective-permute-start(bf16[16,3072]{1,0:T(8,128)(2,1)S(1)} %get-tuple-element.36), channel_id=1, source_target_pairs={{0,16},{8,24},{16,0},{24,8},{1,17},{9,25},{17,1},{25,9},{2,18},{10... | collective-permute-start | bytes 294920 | tf_op jit(solution)/shard_map/ppermute | solution.py:27
  30.3 2.6 %collective-permute-start.7 = (bf16[4,16,3072]{2,1,0:T(8,128)(2,1)S(1)}, bf16[4,16,3072]{2,1,0:T(8,128)(2,1)S(1)}, u32[]{:S(2)}, u32[]{:S(2)}) collective-permute-start(bf16[4,16,3072]{2,1,0:T(8,128)(2,1)S(1)} %pad_maximum_fusion.refs_0_), channel_id=1, source_target_pairs={{0,16},{8,24},{16,0},{24,8},{1,17},{9,25},{17,1},{25,9},{2,18},{10... | collective-permute-start | bytes 1179656 | tf_op jit(solution)/shard_map/ppermute | solution.py:27
  32.9 2.0 %collective-permute-start.6 = (bf16[4,16,3072]{2,1,0:T(8,128)(2,1)S(1)}, bf16[4,16,3072]{2,1,0:T(8,128)(2,1)S(1)}, u32[]{:S(2)}, u32[]{:S(2)}) collective-permute-start(bf16[4,16,3072]{2,1,0:T(8,128)(2,1)S(1)} %pad_maximum_fusion.refs_0_), channel_id=1, source_target_pairs={{0,24},{8,0},{16,8},{24,16},{1,25},{9,1},{17,9},{25,17},{2,26},{10... | collective-permute-start | bytes 1179656 | tf_op jit(solution)/shard_map/ppermute | solution.py:27
  34.9 3.3 %collective-permute-done.9 = bf16[16,3072]{1,0:T(8,128)(2,1)S(1)} collective-permute-done((bf16[16,3072]{1,0:T(8,128)(2,1)S(1)}, bf16[16,3072]{1,0:T(8,128)(2,1)S(1)}, u32[]{:S(2)}, u32[]{:S(2)}) %collective-permute-start.9) | collective-permute-done | bytes 98336 | tf_op jit(solution)/shard_map/ppermute | solution.py:27
  38.3 3.1 %collective-permute-done.8 = bf16[16,3072]{1,0:T(8,128)(2,1)S(1)} collective-permute-done((bf16[16,3072]{1,0:T(8,128)(2,1)S(1)}, bf16[16,3072]{1,0:T(8,128)(2,1)S(1)}, u32[]{:S(2)}, u32[]{:S(2)}) %collective-permute-start.8) | collective-permute-done | bytes 98336 | tf_op jit(solution)/shard_map/ppermute | solution.py:27
  41.5 1.9 %collective-permute-start.13 = (bf16[4,16,3072]{2,1,0:T(8,128)(2,1)S(1)}, bf16[4,16,3072]{2,1,0:T(8,128)(2,1)S(1)}, u32[]{:S(2)}, u32[]{:S(2)}) collective-permute-start(bf16[4,16,3072]{2,1,0:T(8,128)(2,1)S(1)} %pad_maximum_fusion.1.refs_4_), channel_id=1, source_target_pairs={{0,128},{64,192},{128,0},{192,64},{1,129},{65,193},{129,1},{193,65... | collective-permute-start | bytes 1179656 | tf_op jit(solution)/shard_map/ppermute | solution.py:27
  43.3 2.7 %collective-permute-start.12 = (bf16[4,16,3072]{2,1,0:T(8,128)(2,1)S(1)}, bf16[4,16,3072]{2,1,0:T(8,128)(2,1)S(1)}, u32[]{:S(2)}, u32[]{:S(2)}) collective-permute-start(bf16[4,16,3072]{2,1,0:T(8,128)(2,1)S(1)} %pad_maximum_fusion.1.refs_4_), channel_id=1, source_target_pairs={{0,192},{64,0},{128,64},{192,128},{1,193},{65,1},{129,65},{193,129... | collective-permute-start | bytes 1179656 | tf_op jit(solution)/shard_map/ppermute | solution.py:27
  47.0 2.3 %collective-permute-done.6.refs_2_ = bf16[4,16,3072]{2,1,0:T(8,128)(2,1)S(1)} collective-permute-done((bf16[4,16,3072]{2,1,0:T(8,128)(2,1)S(1)}, bf16[4,16,3072]{2,1,0:T(8,128)(2,1)S(1)}, u32[]{:S(2)}, u32[]{:S(2)}) %collective-permute-start.6) | collective-permute-done | bytes 393248 | tf_op jit(solution)/shard_map/ppermute | solution.py:27
  49.3 1.6 %collective-permute-done.5.refs_1_ = bf16[4,16,3072]{2,1,0:T(8,128)(2,1)S(1)} collective-permute-done((bf16[4,16,3072]{2,1,0:T(8,128)(2,1)S(1)}, bf16[4,16,3072]{2,1,0:T(8,128)(2,1)S(1)}, u32[]{:S(2)}, u32[]{:S(2)}) %collective-permute-start.5) | collective-permute-done | bytes 393248 | tf_op jit(solution)/shard_map/ppermute | solution.py:27
  51.1 2.7 %collective-permute-done.12.refs_6_ = bf16[4,16,3072]{2,1,0:T(8,128)(2,1)S(1)} collective-permute-done((bf16[4,16,3072]{2,1,0:T(8,128)(2,1)S(1)}, bf16[4,16,3072]{2,1,0:T(8,128)(2,1)S(1)}, u32[]{:S(2)}, u32[]{:S(2)}) %collective-permute-start.12) | collective-permute-done | bytes 393248 | tf_op jit(solution)/shard_map/ppermute | solution.py:27
  56.3 12.0 %shard_map.68 = (f32[2,592,256]{2,1,0:T(8,128)}, f32[2,592,256]{2,1,0:T(8,128)}, bf16[256,2048]{1,0:T(8,128)(2,1)}, f32[1,768]{1,0:T(1,128)}, f32[2,256]{1,0:T(2,128)}) custom-call(s32[2]{0:T(128)} %pad_add_fusion.at, f32[1,256]{1,0:T(1,128)} %copy-done.9, bf16[4,16,3072]{2,1,0:T(8,128)(2,1)} %copy-done.1, bf16[4,16,3072]{2,1,0:T(8,128)(2,1)} %copy-done.6, ...), custom_call_target="tpu_custom_call" | custom-call | flops 3724541952 | bytes 17694720 | tf_op jit(solution)/shard_map/pallas_call | solution.py:137
  69.0 13.7 %all_to_all.26 = f32[16,1,768]{2,1,0:T(1,128)S(1)} all-to-all(f32[16,1,768]{2,1,0:T(1,128)S(1)} %broadcast_in_dim.34), channel_id=1, replica_groups=mesh['x'=4,'zl'=2,'y'=4,'zh'=4,'c'=2] {'x','y'}, dimensions={0} | all-to-all | bytes 98304 | tf_op jit(solution)/shard_map/all_to_all | solution.py:20
  82.9 9.6 %all_to_all.27 = f32[8,1,768]{2,1,0:T(1,128)S(1)} all-to-all(f32[8,1,768]{2,1,0:T(1,128)S(1)} %broadcast_in_dim.36), channel_id=1, replica_groups=mesh['x'=4,'zl'=2,'y'=4,'zh'=4,'c'=2] {'zl','zh'}, dimensions={0} | all-to-all | bytes 49152 | tf_op jit(solution)/shard_map/all_to_all | solution.py:20
  93.2 7.6 %shard_map.69 = (bf16[592,256]{1,0:T(8,128)(2,1)}, bf16[592,2048]{1,0:T(8,128)(2,1)}, bf16[256,2048]{1,0:T(8,128)(2,1)}) custom-call(f32[2,592,256]{2,1,0:T(8,128)} %get-tuple-element.23.teach, f32[2,592,256]{2,1,0:T(8,128)} %get-tuple-element.24.stud, bf16[592,2048]{1,0:T(8,128)(2,1)} %head0, bf16[592,2048]{1,0:T(8,128)(2,1)} %collective-permute-done.1.refs_11_.head1, ...), custom_call_target="tpu_custom_call" | custom-call | flops 1862270976 | bytes 9699328 | tf_op jit(solution)/shard_map/pallas_call | solution.py:229
  101.0 3.8 %all-to-all-start.3 = ((bf16[16,16,2048]{2,1,0:T(8,128)(2,1)}), bf16[16,16,2048]{2,1,0:T(8,128)(2,1)S(1)}, u32[]{:S(2)}, u32[]{:S(2)}) async-start(bf16[16,16,2048]{2,1,0:T(8,128)(2,1)} %bitcast.20), calls=%async_computation.3 | async-start | bytes 2097152 | tf_op jit(solution)/shard_map/all_to_all | solution.py:40
  104.8 3.0 %fusion.6 = f32[592,2048]{1,0:T(8,128)} fusion(bf16[592,256]{1,0:T(8,128)(2,1)S(1)} %copy-done.3, bf16[256,2048]{1,0:T(8,128)(2,1)S(1)} %copy-done), kind=kOutput, calls=%fused_computation.24 | convolution fusion | flops 620756992 | bytes 6201344 | tf_op jit(solution)/shard_map/dot_general | solution.py:280
  107.7 15.6 %all-to-all-done.3 = bf16[16,16,2048]{2,1,0:T(8,128)(2,1)S(1)} async-done(((bf16[16,16,2048]{2,1,0:T(8,128)(2,1)}), bf16[16,16,2048]{2,1,0:T(8,128)(2,1)S(1)}, u32[]{:S(2)}, u32[]{:S(2)}) %all-to-all-start.3) | async-done | bytes 1048608 | tf_op jit(solution)/shard_map/all_to_all | solution.py:40
  124.3 4.6 %all-to-all-start.4 = ((f32[8,2,2048]{2,1,0:T(2,128)}), f32[8,2,2048]{2,1,0:T(2,128)S(1)}, u32[]{:S(2)}, u32[]{:S(2)}) async-start(f32[8,2,2048]{2,1,0:T(2,128)} %reshape.72), calls=%async_computation.4 | async-start | bytes 262144 | tf_op jit(solution)/shard_map/all_to_all | solution.py:40
  128.9 5.4 %add_convert_fusion = bf16[592,2048]{1,0:T(8,128)(2,1)} fusion(f32[592,2048]{1,0:T(8,128)} %fusion.6, bf16[592,2048]{1,0:T(8,128)(2,1)} %collective-permute-done.14), kind=kLoop, calls=%fused_computation | loop fusion | flops 3637248 | bytes 9699328 | tf_op jit(solution)/shard_map/convert_element_type | solution.py:283
  134.3 2.2 %all-to-all-done.4 = f32[8,2,2048]{2,1,0:T(2,128)S(1)} async-done(((f32[8,2,2048]{2,1,0:T(2,128)}), f32[8,2,2048]{2,1,0:T(2,128)S(1)}, u32[]{:S(2)}, u32[]{:S(2)}) %all-to-all-start.4) | async-done | bytes 131104 | tf_op jit(solution)/shard_map/all_to_all | solution.py:40
  (64 shorter events, 8.5 us)
Async XLA Ops:
  0.6 45.6 %copy-start.10 = (f32[2]{0:T(128)S(1)}, f32[2]{0:T(128)}, u32[]{:S(2)}) copy-start(f32[2]{0:T(128)} %param.9) | copy-start | bytes 28
  0.6 19.2 %collective-permute-start = (bf16[592,4096]{1,0:T(8,128)(2,1)}, bf16[592,4096]{1,0:T(8,128)(2,1)}, u32[]{:S(2)}, u32[]{:S(2)}) collective-permute-start(bf16[592,4096]{1,0:T(8,128)(2,1)} %refs_8_), channel_id=1, source_target_pairs={{0,1},{1,0},{2,3},{3,2},{4,5},{5,4},{6,7},{7,6},{8,9},{9,8},{10,11... | collective-permute-start | bytes 14549000 | tf_op jit(solution)/shard_map/ppermute | solution.py:45
  0.7 19.1 %collective-permute-start.1 = (bf16[592,2048]{1,0:T(8,128)(2,1)}, bf16[592,2048]{1,0:T(8,128)(2,1)}, u32[]{:S(2)}, u32[]{:S(2)}) collective-permute-start(bf16[592,2048]{1,0:T(8,128)(2,1)} %head0), channel_id=1, source_target_pairs={{0,1},{1,0},{2,3},{3,2},{4,5},{5,4},{6,7},{7,6},{8,9},{9,8},{10,11... | collective-permute-start | bytes 7274504 | tf_op jit(solution)/shard_map/ppermute | solution.py:45
  19.9 8.1 %collective-permute-start.3 = (bf16[16,3072]{1,0:T(8,128)(2,1)S(1)}, bf16[16,3072]{1,0:T(8,128)(2,1)S(1)}, u32[]{:S(2)}, u32[]{:S(2)}) collective-permute-start(bf16[16,3072]{1,0:T(8,128)(2,1)S(1)} %get-tuple-element.37), channel_id=1, source_target_pairs={{0,192},{64,0},{128,64},{192,128},{1,193},{65,1},{129,65},{193,129... | collective-permute-start | bytes 294920 | tf_op jit(solution)/shard_map/ppermute | solution.py:27
  22.7 7.5 %collective-permute-start.2 = (bf16[16,3072]{1,0:T(8,128)(2,1)S(1)}, bf16[16,3072]{1,0:T(8,128)(2,1)S(1)}, u32[]{:S(2)}, u32[]{:S(2)}) collective-permute-start(bf16[16,3072]{1,0:T(8,128)(2,1)S(1)} %get-tuple-element.37), channel_id=1, source_target_pairs={{0,64},{64,128},{128,192},{192,0},{1,65},{65,129},{129,193},{193,1... | collective-permute-start | bytes 294920 | tf_op jit(solution)/shard_map/ppermute | solution.py:27
  22.7 7.5 %collective-permute-start.4 = (bf16[16,3072]{1,0:T(8,128)(2,1)S(1)}, bf16[16,3072]{1,0:T(8,128)(2,1)S(1)}, u32[]{:S(2)}, u32[]{:S(2)}) collective-permute-start(bf16[16,3072]{1,0:T(8,128)(2,1)S(1)} %get-tuple-element.37), channel_id=1, source_target_pairs={{0,128},{64,192},{128,0},{192,64},{1,129},{65,193},{129,1},{193,65... | collective-permute-start | bytes 294920 | tf_op jit(solution)/shard_map/ppermute | solution.py:27
  25.0 13.3 %collective-permute-start.9 = (bf16[16,3072]{1,0:T(8,128)(2,1)S(1)}, bf16[16,3072]{1,0:T(8,128)(2,1)S(1)}, u32[]{:S(2)}, u32[]{:S(2)}) collective-permute-start(bf16[16,3072]{1,0:T(8,128)(2,1)S(1)} %get-tuple-element.36), channel_id=1, source_target_pairs={{0,24},{8,0},{16,8},{24,16},{1,25},{9,1},{17,9},{25,17},{2,26},{10... | collective-permute-start | bytes 294920 | tf_op jit(solution)/shard_map/ppermute | solution.py:27
  28.0 13.4 %collective-permute-start.8 = (bf16[16,3072]{1,0:T(8,128)(2,1)S(1)}, bf16[16,3072]{1,0:T(8,128)(2,1)S(1)}, u32[]{:S(2)}, u32[]{:S(2)}) collective-permute-start(bf16[16,3072]{1,0:T(8,128)(2,1)S(1)} %get-tuple-element.36), channel_id=1, source_target_pairs={{0,8},{8,16},{16,24},{24,0},{1,9},{9,17},{17,25},{25,1},{2,10},{10... | collective-permute-start | bytes 294920 | tf_op jit(solution)/shard_map/ppermute | solution.py:27
  28.0 13.4 %collective-permute-start.10 = (bf16[16,3072]{1,0:T(8,128)(2,1)S(1)}, bf16[16,3072]{1,0:T(8,128)(2,1)S(1)}, u32[]{:S(2)}, u32[]{:S(2)}) collective-permute-start(bf16[16,3072]{1,0:T(8,128)(2,1)S(1)} %get-tuple-element.36), channel_id=1, source_target_pairs={{0,16},{8,24},{16,0},{24,8},{1,17},{9,25},{17,1},{25,9},{2,18},{10... | collective-permute-start | bytes 294920 | tf_op jit(solution)/shard_map/ppermute | solution.py:27
  30.3 26.0 %copy-start.1 = (bf16[4,16,3072]{2,1,0:T(8,128)(2,1)}, bf16[4,16,3072]{2,1,0:T(8,128)(2,1)S(1)}, u32[]{:S(2)}) copy-start(bf16[4,16,3072]{2,1,0:T(8,128)(2,1)S(1)} %pad_maximum_fusion.refs_0_) | copy-start | bytes 1179652
  30.3 15.7 %collective-permute-start.7 = (bf16[4,16,3072]{2,1,0:T(8,128)(2,1)S(1)}, bf16[4,16,3072]{2,1,0:T(8,128)(2,1)S(1)}, u32[]{:S(2)}, u32[]{:S(2)}) collective-permute-start(bf16[4,16,3072]{2,1,0:T(8,128)(2,1)S(1)} %pad_maximum_fusion.refs_0_), channel_id=1, source_target_pairs={{0,16},{8,24},{16,0},{24,8},{1,17},{9,25},{17,1},{25,9},{2,18},{10... | collective-permute-start | bytes 1179656 | tf_op jit(solution)/shard_map/ppermute | solution.py:27
  32.9 16.4 %collective-permute-start.6 = (bf16[4,16,3072]{2,1,0:T(8,128)(2,1)S(1)}, bf16[4,16,3072]{2,1,0:T(8,128)(2,1)S(1)}, u32[]{:S(2)}, u32[]{:S(2)}) collective-permute-start(bf16[4,16,3072]{2,1,0:T(8,128)(2,1)S(1)} %pad_maximum_fusion.refs_0_), channel_id=1, source_target_pairs={{0,24},{8,0},{16,8},{24,16},{1,25},{9,1},{17,9},{25,17},{2,26},{10... | collective-permute-start | bytes 1179656 | tf_op jit(solution)/shard_map/ppermute | solution.py:27
  38.3 12.6 %collective-permute-start.5 = (bf16[4,16,3072]{2,1,0:T(8,128)(2,1)S(1)}, bf16[4,16,3072]{2,1,0:T(8,128)(2,1)S(1)}, u32[]{:S(2)}, u32[]{:S(2)}) collective-permute-start(bf16[4,16,3072]{2,1,0:T(8,128)(2,1)S(1)} %pad_maximum_fusion.refs_0_), channel_id=1, source_target_pairs={{0,8},{8,16},{16,24},{24,0},{1,9},{9,17},{17,25},{25,1},{2,10},{10... | collective-permute-start | bytes 1179656 | tf_op jit(solution)/shard_map/ppermute | solution.py:27
  41.4 14.8 %copy-start.2 = (bf16[4,16,3072]{2,1,0:T(8,128)(2,1)}, bf16[4,16,3072]{2,1,0:T(8,128)(2,1)S(1)}, u32[]{:S(2)}) copy-start(bf16[4,16,3072]{2,1,0:T(8,128)(2,1)S(1)} %pad_maximum_fusion.1.refs_4_) | copy-start | bytes 1179652
  41.5 9.7 %collective-permute-start.13 = (bf16[4,16,3072]{2,1,0:T(8,128)(2,1)S(1)}, bf16[4,16,3072]{2,1,0:T(8,128)(2,1)S(1)}, u32[]{:S(2)}, u32[]{:S(2)}) collective-permute-start(bf16[4,16,3072]{2,1,0:T(8,128)(2,1)S(1)} %pad_maximum_fusion.1.refs_4_), channel_id=1, source_target_pairs={{0,128},{64,192},{128,0},{192,64},{1,129},{65,193},{129,1},{193,65... | collective-permute-start | bytes 1179656 | tf_op jit(solution)/shard_map/ppermute | solution.py:27
  43.3 10.5 %collective-permute-start.12 = (bf16[4,16,3072]{2,1,0:T(8,128)(2,1)S(1)}, bf16[4,16,3072]{2,1,0:T(8,128)(2,1)S(1)}, u32[]{:S(2)}, u32[]{:S(2)}) collective-permute-start(bf16[4,16,3072]{2,1,0:T(8,128)(2,1)S(1)} %pad_maximum_fusion.1.refs_4_), channel_id=1, source_target_pairs={{0,192},{64,0},{128,64},{192,128},{1,193},{65,1},{129,65},{193,129... | collective-permute-start | bytes 1179656 | tf_op jit(solution)/shard_map/ppermute | solution.py:27
  46.0 10.2 %copy-start.4 = (bf16[4,16,3072]{2,1,0:T(8,128)(2,1)}, bf16[4,16,3072]{2,1,0:T(8,128)(2,1)S(1)}, u32[]{:S(2)}) copy-start(bf16[4,16,3072]{2,1,0:T(8,128)(2,1)S(1)} %collective-permute-done.7.refs_3_) | copy-start | bytes 1179652
  46.0 10.2 %collective-permute-start.11 = (bf16[4,16,3072]{2,1,0:T(8,128)(2,1)S(1)}, bf16[4,16,3072]{2,1,0:T(8,128)(2,1)}, u32[]{:S(2)}, u32[]{:S(2)}) collective-permute-start(bf16[4,16,3072]{2,1,0:T(8,128)(2,1)S(1)} %pad_maximum_fusion.1.refs_4_), channel_id=1, source_target_pairs={{0,64},{64,128},{128,192},{192,0},{1,65},{65,129},{129,193},{193,1... | collective-permute-start | bytes 1179656 | tf_op jit(solution)/shard_map/ppermute | solution.py:27
  46.4 9.9 %copy-start.9 = (f32[1,256]{1,0:T(1,128)}, f32[1,256]{1,0:T(1,128)S(1)}, u32[]{:S(2)}) copy-start(f32[1,256]{1,0:T(1,128)S(1)} %dynamic_update_slice.3.weight) | copy-start | bytes 3076
  49.3 7.0 %copy-start.5 = (bf16[4,16,3072]{2,1,0:T(8,128)(2,1)}, bf16[4,16,3072]{2,1,0:T(8,128)(2,1)S(1)}, u32[]{:S(2)}) copy-start(bf16[4,16,3072]{2,1,0:T(8,128)(2,1)S(1)} %collective-permute-done.6.refs_2_) | copy-start | bytes 1179652
  50.9 5.3 %copy-start.6 = (bf16[4,16,3072]{2,1,0:T(8,128)(2,1)}, bf16[4,16,3072]{2,1,0:T(8,128)(2,1)S(1)}, u32[]{:S(2)}) copy-start(bf16[4,16,3072]{2,1,0:T(8,128)(2,1)S(1)} %collective-permute-done.5.refs_1_) | copy-start | bytes 1179652
  100.9 23.4 %collective-permute-start.14 = (bf16[592,2048]{1,0:T(8,128)(2,1)}, bf16[592,2048]{1,0:T(8,128)(2,1)}, u32[]{:S(2)}, u32[]{:S(2)}) collective-permute-start(bf16[592,2048]{1,0:T(8,128)(2,1)} %get-tuple-element.30), channel_id=1, source_target_pairs={{0,1},{1,0},{2,3},{3,2},{4,5},{5,4},{6,7},{7,6},{8,9},{9,8},{10,11... | collective-permute-start | bytes 7274504 | tf_op jit(solution)/shard_map/ppermute | solution.py:45
  101.0 22.4 %all-to-all-start.3 = ((bf16[16,16,2048]{2,1,0:T(8,128)(2,1)}), bf16[16,16,2048]{2,1,0:T(8,128)(2,1)S(1)}, u32[]{:S(2)}, u32[]{:S(2)}) async-start(bf16[16,16,2048]{2,1,0:T(8,128)(2,1)} %bitcast.20), calls=%async_computation.3 | async-start | bytes 2097152 | tf_op jit(solution)/shard_map/all_to_all | solution.py:40
  124.3 12.2 %all-to-all-start.4 = ((f32[8,2,2048]{2,1,0:T(2,128)}), f32[8,2,2048]{2,1,0:T(2,128)S(1)}, u32[]{:S(2)}, u32[]{:S(2)}) async-start(f32[8,2,2048]{2,1,0:T(2,128)} %reshape.72), calls=%async_computation.4 | async-start | bytes 262144 | tf_op jit(solution)/shard_map/all_to_all | solution.py:40
  (4 other events, 11.4 us)

commit v4 on v3

--- a/solution.py
+++ b/solution.py
@@ -14,6 +14,7 @@
 HBM, SMEM = pl.BlockSpec(memory_space=pltpu.HBM), pl.BlockSpec(memory_space=pltpu.SMEM)
 VMEM = pl.BlockSpec(memory_space=pltpu.VMEM)
 WIDE = 2048
+FLIGHT = 4
 
 
 def share(block, axes, n):
@@ -80,7 +81,7 @@
                     head.at[:, pl.ds(lo, WIDE)], held.at[n], sem.at[64 + n]
                 )
             )
-    for copy in copies + loads[:2]:
+    for copy in copies + loads[:FLIGHT]:
         copy.start()
     terms[...] = jnp.zeros_like(terms)
     for copy in copies:
@@ -97,7 +98,9 @@
         mine[...] = value
         outs[i].start()
         total = jnp.sum(jnp.sum(value, 0), 0, keepdims=True)
-        logs_out[:, i * nt : (i + 1) * nt] = peak + jnp.log(total)
+        logs_out[:, :, i * nt : (i + 1) * nt] = jnp.broadcast_to(
+            peak + jnp.log(total), (NP, 1, nt)
+        )
         base_out[i : i + 1] = peak
 
     outs = [
@@ -112,8 +115,8 @@
             @pl.when(n == i)
             def _():
                 loads[i].wait()
-                if i + 2 < 6:
-                    loads[i + 2].start()
+                if i + FLIGHT < 6:
+                    loads[i + FLIGHT].start()
 
         j = n % 3
         terms[n // 3 + jnp.where(j > 0, 2, 0)] += lax.dot_general(
@@ -125,7 +128,7 @@
             finish(0)
 
     finish(1)
-    logs_out[:, 2 * nt :] = weight[...]
+    logs_out[:, :, 2 * nt :] = jnp.broadcast_to(weight[...], (NP, 1, nt))
     rows.wait()
     for copy in outs:
         copy.wait()
@@ -140,7 +143,7 @@
             shape((2, ve, nt), jnp.float32),
             shape((2, ve, nt), jnp.float32),
             shape((nt, WIDE), jnp.bfloat16),
-            shape((1, 3 * nt), jnp.float32),
+            shape((NP, 1, 3 * nt), jnp.float32),
             shape((2, nt), jnp.float32),
         ],
         in_specs=[SMEM, VMEM] + [HBM] * 12,
@@ -175,9 +178,10 @@
     for copy in loads:
         copy.start()
     nt = base.shape[1]
-    weight = logs[:, 2 * nt :]
+    every = join(logs[...], nt)
+    weight = every[:, 2 * nt :]
     scale = [
-        weight * jnp.exp(base[i : i + 1] - logs[:, i * nt : (i + 1) * nt]) for i in range(2)
+        weight * jnp.exp(base[i : i + 1] - every[:, i * nt : (i + 1) * nt]) for i in range(2)
     ]
 
     def gradient(h):
@@ -272,7 +276,8 @@
     second = ring(jnp.stack(ring(line[:, half:], "y")), "x")
     first = ring(jnp.stack(ring(line[:, :half], "x")), "y")
     teach, stud, rows, logs, base = logits(jnp.stack([x, y]), weight, first, second, heads)
-    logs = join(share(join(share(logs, PLANE, NP), nt), LINE, NL), nt)
+    logs = join(lax.all_to_all(logs, PLANE, 0, 0, tiled=True), nt)
+    logs = share(logs, LINE, NL)
     grad, theirs, part = grads(teach, stud, heads[2], heads[3], rows, logs, base)
 
     theirs = swap(theirs)

time: 138 us -> 137 us (level)
    all_to_all x0 -> x1, blocking collectives: none -> 14 us  [on_device(): logs = join(lax.all_to_all(logs, PLANE, 0, 0, tiled=True), nt)]
    all_to_all x3 -> x2, blocking collectives: 41 us -> 27.3 us  [share(): lax.all_to_all(jnp.broadcast_to(block[None], (n,) + block.shape), axes, 0...]
where the time goes in v4:
time: 137 us; the launch traced here: 136 us
  blocking collectives  41.3 us (30%)
  waiting for transfers between devices  32.7 us (24%)
  starting transfers between devices  28.8 us (21%)
  Pallas kernels  19.6 us (14%)
  other arithmetic  7.88 us (6%)
  matrix products  2.98 us (2%)
  local copies, waits for them, and re-layouts  1.96 us (1%)
    all_to_all x2, blocking collectives, share(): lax.all_to_all(jnp.broadcast_to(block[None], (n,) + block.shape), axes, 0...  27.3 us
    ppermute x12, starting transfers between devices, ring(): lax.ppermute(block, axis, [(i, (i + step) % 4) for i in range(4)])  19.7 us
    all_to_all x2, waiting for transfers between devices, plane_sum(): got = lax.all_to_all(blocks, axes, 0, 0, tiled=True)  17.8 us
    ppermute x12, waiting for transfers between devices, ring(): lax.ppermute(block, axis, [(i, (i + step) % 4) for i in range(4)])  14.9 us
    all_to_all x1, blocking collectives, on_device(): logs = join(lax.all_to_all(logs, PLANE, 0, 0, tiled=True), nt)  14 us
    pallas_call x1, Pallas kernels, logits(): pl.pallas_call(logits_kernel, out_shape=[shape((2, ve, nt), jnp.float32),...  11.9 us
    all_to_all x2, starting transfers between devices, plane_sum(): got = lax.all_to_all(blocks, axes, 0, 0, tiled=True)  8.4 us
    pallas_call x1, Pallas kernels, grads(): pl.pallas_call(grad_kernel, out_shape=[shape((ve, nt), jnp.bfloat16), sha...  7.67 us
  transfers between devices with their start and end apart: 17, of which 9 were waited for; matrix products, arithmetic and copies ran while one was open for 8% of the time, Pallas kernels for 0%

profile of v4, /device:TPU:32, one launch (start us, length us, event | category | flops | bytes accessed | tf_op | source)
XLA Modules:
  0.0 136.0 jit_solution(78975384681803532)
XLA Ops:
  2.1 17.6 %all_to_all.25 = bf16[8,2,6144]{2,1,0:T(2,128)(2,1)S(1)} all-to-all(bf16[8,2,6144]{2,1,0:T(2,128)(2,1)S(1)} %broadcast_in_dim.23), channel_id=1, replica_groups=mesh['x'=4,'zl'=2,'y'=4,'zh'=4,'c'=2] {'zl','zh'}, dimensions={0} | all-to-all | bytes 393216 | tf_op jit(solution)/shard_map/all_to_all | solution.py:21
  19.9 2.8 %collective-permute-start.3 = (bf16[16,3072]{1,0:T(8,128)(2,1)S(1)}, bf16[16,3072]{1,0:T(8,128)(2,1)S(1)}, u32[]{:S(2)}, u32[]{:S(2)}) collective-permute-start(bf16[16,3072]{1,0:T(8,128)(2,1)S(1)} %get-tuple-element.37), channel_id=1, source_target_pairs={{0,192},{64,0},{128,64},{192,128},{1,193},{65,1},{129,65},{193,129... | collective-permute-start | bytes 294920 | tf_op jit(solution)/shard_map/ppermute | solution.py:28
  22.7 2.3 %collective-permute-start.4 = (bf16[16,3072]{1,0:T(8,128)(2,1)S(1)}, bf16[16,3072]{1,0:T(8,128)(2,1)S(1)}, u32[]{:S(2)}, u32[]{:S(2)}) collective-permute-start(bf16[16,3072]{1,0:T(8,128)(2,1)S(1)} %get-tuple-element.37), channel_id=1, source_target_pairs={{0,128},{64,192},{128,0},{192,64},{1,129},{65,193},{129,1},{193,65... | collective-permute-start | bytes 294920 | tf_op jit(solution)/shard_map/ppermute | solution.py:28
  25.0 3.0 %collective-permute-start.9 = (bf16[16,3072]{1,0:T(8,128)(2,1)S(1)}, bf16[16,3072]{1,0:T(8,128)(2,1)S(1)}, u32[]{:S(2)}, u32[]{:S(2)}) collective-permute-start(bf16[16,3072]{1,0:T(8,128)(2,1)S(1)} %get-tuple-element.36), channel_id=1, source_target_pairs={{0,24},{8,0},{16,8},{24,16},{1,25},{9,1},{17,9},{25,17},{2,26},{10... | collective-permute-start | bytes 294920 | tf_op jit(solution)/shard_map/ppermute | solution.py:28
  28.0 2.2 %collective-permute-start.10 = (bf16[16,3072]{1,0:T(8,128)(2,1)S(1)}, bf16[16,3072]{1,0:T(8,128)(2,1)S(1)}, u32[]{:S(2)}, u32[]{:S(2)}) collective-permute-start(bf16[16,3072]{1,0:T(8,128)(2,1)S(1)} %get-tuple-element.36), channel_id=1, source_target_pairs={{0,16},{8,24},{16,0},{24,8},{1,17},{9,25},{17,1},{25,9},{2,18},{10... | collective-permute-start | bytes 294920 | tf_op jit(solution)/shard_map/ppermute | solution.py:28
  30.3 2.6 %collective-permute-start.7 = (bf16[4,16,3072]{2,1,0:T(8,128)(2,1)S(1)}, bf16[4,16,3072]{2,1,0:T(8,128)(2,1)S(1)}, u32[]{:S(2)}, u32[]{:S(2)}) collective-permute-start(bf16[4,16,3072]{2,1,0:T(8,128)(2,1)S(1)} %pad_maximum_fusion.refs_0_), channel_id=1, source_target_pairs={{0,16},{8,24},{16,0},{24,8},{1,17},{9,25},{17,1},{25,9},{2,18},{10... | collective-permute-start | bytes 1179656 | tf_op jit(solution)/shard_map/ppermute | solution.py:28
  32.9 2.0 %collective-permute-start.6 = (bf16[4,16,3072]{2,1,0:T(8,128)(2,1)S(1)}, bf16[4,16,3072]{2,1,0:T(8,128)(2,1)S(1)}, u32[]{:S(2)}, u32[]{:S(2)}) collective-permute-start(bf16[4,16,3072]{2,1,0:T(8,128)(2,1)S(1)} %pad_maximum_fusion.refs_0_), channel_id=1, source_target_pairs={{0,24},{8,0},{16,8},{24,16},{1,25},{9,1},{17,9},{25,17},{2,26},{10... | collective-permute-start | bytes 1179656 | tf_op jit(solution)/shard_map/ppermute | solution.py:28
  34.9 3.3 %collective-permute-done.9 = bf16[16,3072]{1,0:T(8,128)(2,1)S(1)} collective-permute-done((bf16[16,3072]{1,0:T(8,128)(2,1)S(1)}, bf16[16,3072]{1,0:T(8,128)(2,1)S(1)}, u32[]{:S(2)}, u32[]{:S(2)}) %collective-permute-start.9) | collective-permute-done | bytes 98336 | tf_op jit(solution)/shard_map/ppermute | solution.py:28
  38.3 3.1 %collective-permute-done.8 = bf16[16,3072]{1,0:T(8,128)(2,1)S(1)} collective-permute-done((bf16[16,3072]{1,0:T(8,128)(2,1)S(1)}, bf16[16,3072]{1,0:T(8,128)(2,1)S(1)}, u32[]{:S(2)}, u32[]{:S(2)}) %collective-permute-start.8) | collective-permute-done | bytes 98336 | tf_op jit(solution)/shard_map/ppermute | solution.py:28
  41.5 1.9 %collective-permute-start.13 = (bf16[4,16,3072]{2,1,0:T(8,128)(2,1)S(1)}, bf16[4,16,3072]{2,1,0:T(8,128)(2,1)S(1)}, u32[]{:S(2)}, u32[]{:S(2)}) collective-permute-start(bf16[4,16,3072]{2,1,0:T(8,128)(2,1)S(1)} %pad_maximum_fusion.1.refs_4_), channel_id=1, source_target_pairs={{0,128},{64,192},{128,0},{192,64},{1,129},{65,193},{129,1},{193,65... | collective-permute-start | bytes 1179656 | tf_op jit(solution)/shard_map/ppermute | solution.py:28
  43.3 2.7 %collective-permute-start.12 = (bf16[4,16,3072]{2,1,0:T(8,128)(2,1)S(1)}, bf16[4,16,3072]{2,1,0:T(8,128)(2,1)S(1)}, u32[]{:S(2)}, u32[]{:S(2)}) collective-permute-start(bf16[4,16,3072]{2,1,0:T(8,128)(2,1)S(1)} %pad_maximum_fusion.1.refs_4_), channel_id=1, source_target_pairs={{0,192},{64,0},{128,64},{192,128},{1,193},{65,1},{129,65},{193,129... | collective-permute-start | bytes 1179656 | tf_op jit(solution)/shard_map/ppermute | solution.py:28
  47.0 2.3 %collective-permute-done.6.refs_2_ = bf16[4,16,3072]{2,1,0:T(8,128)(2,1)S(1)} collective-permute-done((bf16[4,16,3072]{2,1,0:T(8,128)(2,1)S(1)}, bf16[4,16,3072]{2,1,0:T(8,128)(2,1)S(1)}, u32[]{:S(2)}, u32[]{:S(2)}) %collective-permute-start.6) | collective-permute-done | bytes 393248 | tf_op jit(solution)/shard_map/ppermute | solution.py:28
  49.3 1.6 %collective-permute-done.5.refs_1_ = bf16[4,16,3072]{2,1,0:T(8,128)(2,1)S(1)} collective-permute-done((bf16[4,16,3072]{2,1,0:T(8,128)(2,1)S(1)}, bf16[4,16,3072]{2,1,0:T(8,128)(2,1)S(1)}, u32[]{:S(2)}, u32[]{:S(2)}) %collective-permute-start.5) | collective-permute-done | bytes 393248 | tf_op jit(solution)/shard_map/ppermute | solution.py:28
  51.1 2.7 %collective-permute-done.12.refs_6_ = bf16[4,16,3072]{2,1,0:T(8,128)(2,1)S(1)} collective-permute-done((bf16[4,16,3072]{2,1,0:T(8,128)(2,1)S(1)}, bf16[4,16,3072]{2,1,0:T(8,128)(2,1)S(1)}, u32[]{:S(2)}, u32[]{:S(2)}) %collective-permute-start.12) | collective-permute-done | bytes 393248 | tf_op jit(solution)/shard_map/ppermute | solution.py:28
  56.3 11.9 %shard_map.68 = (f32[2,592,256]{2,1,0:T(8,128)}, f32[2,592,256]{2,1,0:T(8,128)}, bf16[256,2048]{1,0:T(8,128)(2,1)}, f32[16,1,768]{2,1,0:T(1,128)}, f32[2,256]{1,0:T(2,128)}) custom-call(s32[2]{0:T(128)} %pad_add_fusion.at, f32[1,256]{1,0:T(1,128)} %copy-done.9, bf16[4,16,3072]{2,1,0:T(8,128)(2,1)} %copy-done.1, bf16[4,16,3072]{2,1,0:T(8,128)(2,1)} %copy-done.6, ...), custom_call_target="tpu_custom_call" | custom-call | flops 3724541952 | bytes 17694720 | tf_op jit(solution)/shard_map/pallas_call | solution.py:140
  68.2 14.0 %all_to_all.26 = f32[16,1,768]{2,1,0:T(1,128)S(1)} all-to-all(f32[16,1,768]{2,1,0:T(1,128)} %get-tuple-element.26), channel_id=1, replica_groups=mesh['x'=4,'zl'=2,'y'=4,'zh'=4,'c'=2] {'x','y'}, dimensions={0} | all-to-all | bytes 98304 | tf_op jit(solution)/shard_map/all_to_all | solution.py:279
  82.3 9.7 %all_to_all.27.logs = f32[8,1,768]{2,1,0:T(1,128)} all-to-all(f32[8,1,768]{2,1,0:T(1,128)S(1)} %broadcast_in_dim.25), channel_id=1, replica_groups=mesh['x'=4,'zl'=2,'y'=4,'zh'=4,'c'=2] {'zl','zh'}, dimensions={0} | all-to-all | bytes 49152 | tf_op jit(solution)/shard_map/all_to_all | solution.py:21
  92.1 7.7 %shard_map.69 = (bf16[592,256]{1,0:T(8,128)(2,1)}, bf16[592,2048]{1,0:T(8,128)(2,1)}, bf16[256,2048]{1,0:T(8,128)(2,1)}) custom-call(f32[2,592,256]{2,1,0:T(8,128)} %get-tuple-element.23.teach, f32[2,592,256]{2,1,0:T(8,128)} %get-tuple-element.24.stud, bf16[592,2048]{1,0:T(8,128)(2,1)} %head0, bf16[592,2048]{1,0:T(8,128)(2,1)} %collective-permute-done.1.refs_11_.head1, ...), custom_call_target="tpu_custom_call" | custom-call | flops 1862270976 | bytes 9699328 | tf_op jit(solution)/shard_map/pallas_call | solution.py:233
  99.9 3.8 %all-to-all-start.3 = ((bf16[16,16,2048]{2,1,0:T(8,128)(2,1)}), bf16[16,16,2048]{2,1,0:T(8,128)(2,1)S(1)}, u32[]{:S(2)}, u32[]{:S(2)}) async-start(bf16[16,16,2048]{2,1,0:T(8,128)(2,1)} %bitcast.18), calls=%async_computation.3 | async-start | bytes 2097152 | tf_op jit(solution)/shard_map/all_to_all | solution.py:41
  103.7 3.0 %fusion = f32[592,2048]{1,0:T(8,128)} fusion(bf16[592,256]{1,0:T(8,128)(2,1)S(1)} %copy-done.3, bf16[256,2048]{1,0:T(8,128)(2,1)S(1)} %copy-done), kind=kOutput, calls=%fused_computation.13 | convolution fusion | flops 620756992 | bytes 6201344 | tf_op jit(solution)/shard_map/dot_general | solution.py:285
  106.7 15.6 %all-to-all-done.3 = bf16[16,16,2048]{2,1,0:T(8,128)(2,1)S(1)} async-done(((bf16[16,16,2048]{2,1,0:T(8,128)(2,1)}), bf16[16,16,2048]{2,1,0:T(8,128)(2,1)S(1)}, u32[]{:S(2)}, u32[]{:S(2)}) %all-to-all-start.3) | async-done | bytes 1048608 | tf_op jit(solution)/shard_map/all_to_all | solution.py:41
  123.2 4.6 %all-to-all-start.4 = ((f32[8,2,2048]{2,1,0:T(2,128)}), f32[8,2,2048]{2,1,0:T(2,128)S(1)}, u32[]{:S(2)}, u32[]{:S(2)}) async-start(f32[8,2,2048]{2,1,0:T(2,128)} %reshape.44), calls=%async_computation.4 | async-start | bytes 262144 | tf_op jit(solution)/shard_map/all_to_all | solution.py:41
  127.8 5.4 %add_convert_fusion = bf16[592,2048]{1,0:T(8,128)(2,1)} fusion(f32[592,2048]{1,0:T(8,128)} %fusion, bf16[592,2048]{1,0:T(8,128)(2,1)} %collective-permute-done.14), kind=kLoop, calls=%fused_computation | loop fusion | flops 3637248 | bytes 9699328 | tf_op jit(solution)/shard_map/convert_element_type | solution.py:288
  133.2 2.2 %all-to-all-done.4 = f32[8,2,2048]{2,1,0:T(2,128)S(1)} async-done(((f32[8,2,2048]{2,1,0:T(2,128)}), f32[8,2,2048]{2,1,0:T(2,128)S(1)}, u32[]{:S(2)}, u32[]{:S(2)}) %all-to-all-start.4) | async-done | bytes 131104 | tf_op jit(solution)/shard_map/all_to_all | solution.py:41
  (57 shorter events, 7.1 us)
Async XLA Ops:
  0.6 45.6 %copy-start.10 = (f32[2]{0:T(128)S(1)}, f32[2]{0:T(128)}, u32[]{:S(2)}) copy-start(f32[2]{0:T(128)} %param.9) | copy-start | bytes 28
  0.6 19.2 %collective-permute-start = (bf16[592,4096]{1,0:T(8,128)(2,1)}, bf16[592,4096]{1,0:T(8,128)(2,1)}, u32[]{:S(2)}, u32[]{:S(2)}) collective-permute-start(bf16[592,4096]{1,0:T(8,128)(2,1)} %refs_8_), channel_id=1, source_target_pairs={{0,1},{1,0},{2,3},{3,2},{4,5},{5,4},{6,7},{7,6},{8,9},{9,8},{10,11... | collective-permute-start | bytes 14549000 | tf_op jit(solution)/shard_map/ppermute | solution.py:46
  0.7 19.1 %collective-permute-start.1 = (bf16[592,2048]{1,0:T(8,128)(2,1)}, bf16[592,2048]{1,0:T(8,128)(2,1)}, u32[]{:S(2)}, u32[]{:S(2)}) collective-permute-start(bf16[592,2048]{1,0:T(8,128)(2,1)} %head0), channel_id=1, source_target_pairs={{0,1},{1,0},{2,3},{3,2},{4,5},{5,4},{6,7},{7,6},{8,9},{9,8},{10,11... | collective-permute-start | bytes 7274504 | tf_op jit(solution)/shard_map/ppermute | solution.py:46
  19.9 8.1 %collective-permute-start.3 = (bf16[16,3072]{1,0:T(8,128)(2,1)S(1)}, bf16[16,3072]{1,0:T(8,128)(2,1)S(1)}, u32[]{:S(2)}, u32[]{:S(2)}) collective-permute-start(bf16[16,3072]{1,0:T(8,128)(2,1)S(1)} %get-tuple-element.37), channel_id=1, source_target_pairs={{0,192},{64,0},{128,64},{192,128},{1,193},{65,1},{129,65},{193,129... | collective-permute-start | bytes 294920 | tf_op jit(solution)/shard_map/ppermute | solution.py:28
  22.7 7.5 %collective-permute-start.2 = (bf16[16,3072]{1,0:T(8,128)(2,1)S(1)}, bf16[16,3072]{1,0:T(8,128)(2,1)S(1)}, u32[]{:S(2)}, u32[]{:S(2)}) collective-permute-start(bf16[16,3072]{1,0:T(8,128)(2,1)S(1)} %get-tuple-element.37), channel_id=1, source_target_pairs={{0,64},{64,128},{128,192},{192,0},{1,65},{65,129},{129,193},{193,1... | collective-permute-start | bytes 294920 | tf_op jit(solution)/shard_map/ppermute | solution.py:28
  22.7 7.5 %collective-permute-start.4 = (bf16[16,3072]{1,0:T(8,128)(2,1)S(1)}, bf16[16,3072]{1,0:T(8,128)(2,1)S(1)}, u32[]{:S(2)}, u32[]{:S(2)}) collective-permute-start(bf16[16,3072]{1,0:T(8,128)(2,1)S(1)} %get-tuple-element.37), channel_id=1, source_target_pairs={{0,128},{64,192},{128,0},{192,64},{1,129},{65,193},{129,1},{193,65... | collective-permute-start | bytes 294920 | tf_op jit(solution)/shard_map/ppermute | solution.py:28
  25.0 13.3 %collective-permute-start.9 = (bf16[16,3072]{1,0:T(8,128)(2,1)S(1)}, bf16[16,3072]{1,0:T(8,128)(2,1)S(1)}, u32[]{:S(2)}, u32[]{:S(2)}) collective-permute-start(bf16[16,3072]{1,0:T(8,128)(2,1)S(1)} %get-tuple-element.36), channel_id=1, source_target_pairs={{0,24},{8,0},{16,8},{24,16},{1,25},{9,1},{17,9},{25,17},{2,26},{10... | collective-permute-start | bytes 294920 | tf_op jit(solution)/shard_map/ppermute | solution.py:28
  28.0 13.4 %collective-permute-start.8 = (bf16[16,3072]{1,0:T(8,128)(2,1)S(1)}, bf16[16,3072]{1,0:T(8,128)(2,1)S(1)}, u32[]{:S(2)}, u32[]{:S(2)}) collective-permute-start(bf16[16,3072]{1,0:T(8,128)(2,1)S(1)} %get-tuple-element.36), channel_id=1, source_target_pairs={{0,8},{8,16},{16,24},{24,0},{1,9},{9,17},{17,25},{25,1},{2,10},{10... | collective-permute-start | bytes 294920 | tf_op jit(solution)/shard_map/ppermute | solution.py:28
  28.0 13.4 %collective-permute-start.10 = (bf16[16,3072]{1,0:T(8,128)(2,1)S(1)}, bf16[16,3072]{1,0:T(8,128)(2,1)S(1)}, u32[]{:S(2)}, u32[]{:S(2)}) collective-permute-start(bf16[16,3072]{1,0:T(8,128)(2,1)S(1)} %get-tuple-element.36), channel_id=1, source_target_pairs={{0,16},{8,24},{16,0},{24,8},{1,17},{9,25},{17,1},{25,9},{2,18},{10... | collective-permute-start | bytes 294920 | tf_op jit(solution)/shard_map/ppermute | solution.py:28
  30.3 26.0 %copy-start.1 = (bf16[4,16,3072]{2,1,0:T(8,128)(2,1)}, bf16[4,16,3072]{2,1,0:T(8,128)(2,1)S(1)}, u32[]{:S(2)}) copy-start(bf16[4,16,3072]{2,1,0:T(8,128)(2,1)S(1)} %pad_maximum_fusion.refs_0_) | copy-start | bytes 1179652
  30.3 15.7 %collective-permute-start.7 = (bf16[4,16,3072]{2,1,0:T(8,128)(2,1)S(1)}, bf16[4,16,3072]{2,1,0:T(8,128)(2,1)S(1)}, u32[]{:S(2)}, u32[]{:S(2)}) collective-permute-start(bf16[4,16,3072]{2,1,0:T(8,128)(2,1)S(1)} %pad_maximum_fusion.refs_0_), channel_id=1, source_target_pairs={{0,16},{8,24},{16,0},{24,8},{1,17},{9,25},{17,1},{25,9},{2,18},{10... | collective-permute-start | bytes 1179656 | tf_op jit(solution)/shard_map/ppermute | solution.py:28
  32.9 16.4 %collective-permute-start.6 = (bf16[4,16,3072]{2,1,0:T(8,128)(2,1)S(1)}, bf16[4,16,3072]{2,1,0:T(8,128)(2,1)S(1)}, u32[]{:S(2)}, u32[]{:S(2)}) collective-permute-start(bf16[4,16,3072]{2,1,0:T(8,128)(2,1)S(1)} %pad_maximum_fusion.refs_0_), channel_id=1, source_target_pairs={{0,24},{8,0},{16,8},{24,16},{1,25},{9,1},{17,9},{25,17},{2,26},{10... | collective-permute-start | bytes 1179656 | tf_op jit(solution)/shard_map/ppermute | solution.py:28
  38.3 12.6 %collective-permute-start.5 = (bf16[4,16,3072]{2,1,0:T(8,128)(2,1)S(1)}, bf16[4,16,3072]{2,1,0:T(8,128)(2,1)S(1)}, u32[]{:S(2)}, u32[]{:S(2)}) collective-permute-start(bf16[4,16,3072]{2,1,0:T(8,128)(2,1)S(1)} %pad_maximum_fusion.refs_0_), channel_id=1, source_target_pairs={{0,8},{8,16},{16,24},{24,0},{1,9},{9,17},{17,25},{25,1},{2,10},{10... | collective-permute-start | bytes 1179656 | tf_op jit(solution)/shard_map/ppermute | solution.py:28
  41.4 14.8 %copy-start.2 = (bf16[4,16,3072]{2,1,0:T(8,128)(2,1)}, bf16[4,16,3072]{2,1,0:T(8,128)(2,1)S(1)}, u32[]{:S(2)}) copy-start(bf16[4,16,3072]{2,1,0:T(8,128)(2,1)S(1)} %pad_maximum_fusion.1.refs_4_) | copy-start | bytes 1179652
  41.5 9.7 %collective-permute-start.13 = (bf16[4,16,3072]{2,1,0:T(8,128)(2,1)S(1)}, bf16[4,16,3072]{2,1,0:T(8,128)(2,1)S(1)}, u32[]{:S(2)}, u32[]{:S(2)}) collective-permute-start(bf16[4,16,3072]{2,1,0:T(8,128)(2,1)S(1)} %pad_maximum_fusion.1.refs_4_), channel_id=1, source_target_pairs={{0,128},{64,192},{128,0},{192,64},{1,129},{65,193},{129,1},{193,65... | collective-permute-start | bytes 1179656 | tf_op jit(solution)/shard_map/ppermute | solution.py:28
  43.3 10.5 %collective-permute-start.12 = (bf16[4,16,3072]{2,1,0:T(8,128)(2,1)S(1)}, bf16[4,16,3072]{2,1,0:T(8,128)(2,1)S(1)}, u32[]{:S(2)}, u32[]{:S(2)}) collective-permute-start(bf16[4,16,3072]{2,1,0:T(8,128)(2,1)S(1)} %pad_maximum_fusion.1.refs_4_), channel_id=1, source_target_pairs={{0,192},{64,0},{128,64},{192,128},{1,193},{65,1},{129,65},{193,129... | collective-permute-start | bytes 1179656 | tf_op jit(solution)/shard_map/ppermute | solution.py:28
  46.0 10.2 %copy-start.4 = (bf16[4,16,3072]{2,1,0:T(8,128)(2,1)}, bf16[4,16,3072]{2,1,0:T(8,128)(2,1)S(1)}, u32[]{:S(2)}) copy-start(bf16[4,16,3072]{2,1,0:T(8,128)(2,1)S(1)} %collective-permute-done.7.refs_3_) | copy-start | bytes 1179652
  46.0 10.2 %collective-permute-start.11 = (bf16[4,16,3072]{2,1,0:T(8,128)(2,1)S(1)}, bf16[4,16,3072]{2,1,0:T(8,128)(2,1)}, u32[]{:S(2)}, u32[]{:S(2)}) collective-permute-start(bf16[4,16,3072]{2,1,0:T(8,128)(2,1)S(1)} %pad_maximum_fusion.1.refs_4_), channel_id=1, source_target_pairs={{0,64},{64,128},{128,192},{192,0},{1,65},{65,129},{129,193},{193,1... | collective-permute-start | bytes 1179656 | tf_op jit(solution)/shard_map/ppermute | solution.py:28
  46.4 9.9 %copy-start.9 = (f32[1,256]{1,0:T(1,128)}, f32[1,256]{1,0:T(1,128)S(1)}, u32[]{:S(2)}) copy-start(f32[1,256]{1,0:T(1,128)S(1)} %dynamic_update_slice.3.weight) | copy-start | bytes 3076
  49.3 7.0 %copy-start.5 = (bf16[4,16,3072]{2,1,0:T(8,128)(2,1)}, bf16[4,16,3072]{2,1,0:T(8,128)(2,1)S(1)}, u32[]{:S(2)}) copy-start(bf16[4,16,3072]{2,1,0:T(8,128)(2,1)S(1)} %collective-permute-done.6.refs_2_) | copy-start | bytes 1179652
  50.9 5.3 %copy-start.6 = (bf16[4,16,3072]{2,1,0:T(8,128)(2,1)}, bf16[4,16,3072]{2,1,0:T(8,128)(2,1)S(1)}, u32[]{:S(2)}) copy-start(bf16[4,16,3072]{2,1,0:T(8,128)(2,1)S(1)} %collective-permute-done.5.refs_1_) | copy-start | bytes 1179652
  99.8 23.4 %collective-permute-start.14 = (bf16[592,2048]{1,0:T(8,128)(2,1)}, bf16[592,2048]{1,0:T(8,128)(2,1)}, u32[]{:S(2)}, u32[]{:S(2)}) collective-permute-start(bf16[592,2048]{1,0:T(8,128)(2,1)} %get-tuple-element.30), channel_id=1, source_target_pairs={{0,1},{1,0},{2,3},{3,2},{4,5},{5,4},{6,7},{7,6},{8,9},{9,8},{10,11... | collective-permute-start | bytes 7274504 | tf_op jit(solution)/shard_map/ppermute | solution.py:46
  99.9 22.4 %all-to-all-start.3 = ((bf16[16,16,2048]{2,1,0:T(8,128)(2,1)}), bf16[16,16,2048]{2,1,0:T(8,128)(2,1)S(1)}, u32[]{:S(2)}, u32[]{:S(2)}) async-start(bf16[16,16,2048]{2,1,0:T(8,128)(2,1)} %bitcast.18), calls=%async_computation.3 | async-start | bytes 2097152 | tf_op jit(solution)/shard_map/all_to_all | solution.py:41
  123.2 12.2 %all-to-all-start.4 = ((f32[8,2,2048]{2,1,0:T(2,128)}), f32[8,2,2048]{2,1,0:T(2,128)S(1)}, u32[]{:S(2)}, u32[]{:S(2)}) async-start(f32[8,2,2048]{2,1,0:T(2,128)} %reshape.44), calls=%async_computation.4 | async-start | bytes 262144 | tf_op jit(solution)/shard_map/all_to_all | solution.py:41
  (4 other events, 11.4 us)

commit v5 on v4

--- a/solution.py
+++ b/solution.py
@@ -165,8 +165,8 @@
 
 
 def grad_kernel(teach, stud, head0, head1, rows, logs, base, *refs):
-    ours_out, theirs_out, part_out = refs[:3]
-    terms_t, terms_s, held, row, grad, theirs, sem, out_sem = refs[3:]
+    ours_out, part_out, *theirs_out = refs[:6]
+    terms_t, terms_s, held, row, grad, theirs, sem, out_sem = refs[6:]
     pairs = []
     for h in (1, 0):
         pairs += [(stud.at[h], terms_s.at[h]), (teach.at[h], terms_t.at[h])]
@@ -195,17 +195,21 @@
     @pl.loop(0, 4)
     def _(n):
         cols = pl.ds(pl.multiple_of(n * 512, 512), 512)
-        theirs[:, cols] = jnp.dot(
+        theirs[n] = jnp.dot(
             grad[1], row[:, cols], preferred_element_type=jnp.float32
         ).astype(theirs.dtype)
 
-    outs = [pltpu.make_async_copy(theirs, theirs_out, out_sem.at[0])]
-    outs[0].start()
+    outs = [
+        pltpu.make_async_copy(theirs.at[i], out, out_sem.at[1 + i])
+        for i, out in enumerate(theirs_out)
+    ]
+    for copy in outs:
+        copy.start()
     loads[3].wait()
     loads[4].wait()
     gradient(0)
-    outs.append(pltpu.make_async_copy(grad.at[0], ours_out, out_sem.at[1]))
-    outs[1].start()
+    outs.append(pltpu.make_async_copy(grad.at[0], ours_out, out_sem.at[0]))
+    outs[-1].start()
     loads[5].wait()
     loads[6].wait()
 
@@ -234,20 +238,20 @@
         grad_kernel,
         out_shape=[
             shape((ve, nt), jnp.bfloat16),
-            shape((ve, WIDE), jnp.bfloat16),
             shape((nt, WIDE), jnp.bfloat16),
-        ],
+        ]
+        + [shape((ve, WIDE // 4), jnp.bfloat16)] * 4,
         in_specs=[HBM] * 5 + [VMEM] * 2,
-        out_specs=[HBM] * 2 + [VMEM],
+        out_specs=[HBM, VMEM] + [HBM] * 4,
         scratch_shapes=[
             pltpu.VMEM((2, ve, nt), jnp.float32),
             pltpu.VMEM((2, ve, nt), jnp.float32),
             pltpu.VMEM((2, ve, WIDE), jnp.bfloat16),
             pltpu.VMEM((nt, WIDE), jnp.bfloat16),
             pltpu.VMEM((2, ve, nt), jnp.bfloat16),
-            pltpu.VMEM((ve, WIDE), jnp.bfloat16),
+            pltpu.VMEM((4, ve, WIDE // 4), jnp.bfloat16),
             pltpu.SemaphoreType.DMA((7,)),
-            pltpu.SemaphoreType.DMA((2,)),
+            pltpu.SemaphoreType.DMA((5,)),
         ],
         compiler_params=pltpu.CompilerParams(vmem_limit_bytes=VMEM_LIMIT),
         cost_estimate=pl.CostEstimate(
@@ -278,9 +282,9 @@
     teach, stud, rows, logs, base = logits(jnp.stack([x, y]), weight, first, second, heads)
     logs = join(lax.all_to_all(logs, PLANE, 0, 0, tiled=True), nt)
     logs = share(logs, LINE, NL)
-    grad, theirs, part = grads(teach, stud, heads[2], heads[3], rows, logs, base)
-
-    theirs = swap(theirs)
+    grad, part, *theirs = grads(teach, stud, heads[2], heads[3], rows, logs, base)
+
+    theirs = jnp.concatenate([swap(block) for block in theirs], 1)
     part = plane_sum(part.reshape(NP, NL * tok, ds), PLANE).reshape(NL, tok, ds)
     ours = jnp.dot(grad, rows, preferred_element_type=jnp.float32)
     part, ours, theirs = lax.optimization_barrier((part, ours, theirs))

time: 137 us -> 132 us (0.964)
  waiting for transfers between devices: 32.7 us -> 24.8 us
  local copies, waits for them, and re-layouts: 1.96 us -> 3.5 us
    all_to_all x2, waiting for transfers between devices: 17.8 us -> 10.5 us  [plane_sum(): got = lax.all_to_all(blocks, axes, 0, 0, tiled=True)]
  transfers between devices with their start and end apart: 17 -> 20, of which waited for: 9 -> 9; matrix products, arithmetic and copies ran while one was open for 8% -> 9% of each run, Pallas kernels for 0% -> 0%
where the time goes in v5:
time: 132 us
  blocking collectives  41.5 us (31%)
  starting transfers between devices  29.7 us (22%)
  waiting for transfers between devices  24.8 us (19%)
  Pallas kernels  19.6 us (15%)
  other arithmetic  8 us (6%)
  matrix products  3.93 us (3%)
  local copies, waits for them, and re-layouts  3.5 us (3%)
    all_to_all x2, blocking collectives, share(): lax.all_to_all(jnp.broadcast_to(block[None], (n,) + block.shape), axes, 0...  27.3 us
    ppermute x12, starting transfers between devices, ring(): lax.ppermute(block, axis, [(i, (i + step) % 4) for i in range(4)])  19.7 us
    ppermute x12, waiting for transfers between devices, ring(): lax.ppermute(block, axis, [(i, (i + step) % 4) for i in range(4)])  14.3 us
    all_to_all x1, blocking collectives, on_device(): logs = join(lax.all_to_all(logs, PLANE, 0, 0, tiled=True), nt)  14.1 us
    pallas_call x1, Pallas kernels, logits(): pl.pallas_call(logits_kernel, out_shape=[shape((2, ve, nt), jnp.float32),...  11.8 us
    all_to_all x2, waiting for transfers between devices, plane_sum(): got = lax.all_to_all(blocks, axes, 0, 0, tiled=True)  10.5 us
    all_to_all x2, starting transfers between devices, plane_sum(): got = lax.all_to_all(blocks, axes, 0, 0, tiled=True)  8.26 us
    pallas_call x1, Pallas kernels, grads(): pl.pallas_call(grad_kernel, out_shape=[shape((ve, nt), jnp.bfloat16), sha...  7.8 us
  transfers between devices with their start and end apart: 20, of which 9 were waited for; matrix products, arithmetic and copies ran while one was open for 9% of the time, Pallas kernels for 0%

profile of v5, /device:TPU:32, one launch (start us, length us, event | category | flops | bytes accessed | tf_op | source)
XLA Modules:
  0.0 131.8 jit_solution(15614683908849350213)
XLA Ops:
  2.1 17.6 %all_to_all.25 = bf16[8,2,6144]{2,1,0:T(2,128)(2,1)S(1)} all-to-all(bf16[8,2,6144]{2,1,0:T(2,128)(2,1)S(1)} %broadcast_in_dim.23), channel_id=1, replica_groups=mesh['x'=4,'zl'=2,'y'=4,'zh'=4,'c'=2] {'zl','zh'}, dimensions={0} | all-to-all | bytes 393216 | tf_op jit(solution)/shard_map/all_to_all | solution.py:21
  19.8 2.8 %collective-permute-start.3 = (bf16[16,3072]{1,0:T(8,128)(2,1)S(1)}, bf16[16,3072]{1,0:T(8,128)(2,1)S(1)}, u32[]{:S(2)}, u32[]{:S(2)}) collective-permute-start(bf16[16,3072]{1,0:T(8,128)(2,1)S(1)} %get-tuple-element.43), channel_id=1, source_target_pairs={{0,192},{64,0},{128,64},{192,128},{1,193},{65,1},{129,65},{193,129... | collective-permute-start | bytes 294920 | tf_op jit(solution)/shard_map/ppermute | solution.py:28
  22.7 2.3 %collective-permute-start.4 = (bf16[16,3072]{1,0:T(8,128)(2,1)S(1)}, bf16[16,3072]{1,0:T(8,128)(2,1)S(1)}, u32[]{:S(2)}, u32[]{:S(2)}) collective-permute-start(bf16[16,3072]{1,0:T(8,128)(2,1)S(1)} %get-tuple-element.43), channel_id=1, source_target_pairs={{0,128},{64,192},{128,0},{192,64},{1,129},{65,193},{129,1},{193,65... | collective-permute-start | bytes 294920 | tf_op jit(solution)/shard_map/ppermute | solution.py:28
  25.0 3.0 %collective-permute-start.9 = (bf16[16,3072]{1,0:T(8,128)(2,1)S(1)}, bf16[16,3072]{1,0:T(8,128)(2,1)S(1)}, u32[]{:S(2)}, u32[]{:S(2)}) collective-permute-start(bf16[16,3072]{1,0:T(8,128)(2,1)S(1)} %get-tuple-element.42), channel_id=1, source_target_pairs={{0,24},{8,0},{16,8},{24,16},{1,25},{9,1},{17,9},{25,17},{2,26},{10... | collective-permute-start | bytes 294920 | tf_op jit(solution)/shard_map/ppermute | solution.py:28
  28.0 2.2 %collective-permute-start.10 = (bf16[16,3072]{1,0:T(8,128)(2,1)S(1)}, bf16[16,3072]{1,0:T(8,128)(2,1)S(1)}, u32[]{:S(2)}, u32[]{:S(2)}) collective-permute-start(bf16[16,3072]{1,0:T(8,128)(2,1)S(1)} %get-tuple-element.42), channel_id=1, source_target_pairs={{0,16},{8,24},{16,0},{24,8},{1,17},{9,25},{17,1},{25,9},{2,18},{10... | collective-permute-start | bytes 294920 | tf_op jit(solution)/shard_map/ppermute | solution.py:28
  30.3 2.6 %collective-permute-start.7 = (bf16[4,16,3072]{2,1,0:T(8,128)(2,1)S(1)}, bf16[4,16,3072]{2,1,0:T(8,128)(2,1)S(1)}, u32[]{:S(2)}, u32[]{:S(2)}) collective-permute-start(bf16[4,16,3072]{2,1,0:T(8,128)(2,1)S(1)} %pad_maximum_fusion.1.refs_0_), channel_id=1, source_target_pairs={{0,16},{8,24},{16,0},{24,8},{1,17},{9,25},{17,1},{25,9},{2,18},{10... | collective-permute-start | bytes 1179656 | tf_op jit(solution)/shard_map/ppermute | solution.py:28
  32.9 2.0 %collective-permute-start.6 = (bf16[4,16,3072]{2,1,0:T(8,128)(2,1)S(1)}, bf16[4,16,3072]{2,1,0:T(8,128)(2,1)S(1)}, u32[]{:S(2)}, u32[]{:S(2)}) collective-permute-start(bf16[4,16,3072]{2,1,0:T(8,128)(2,1)S(1)} %pad_maximum_fusion.1.refs_0_), channel_id=1, source_target_pairs={{0,24},{8,0},{16,8},{24,16},{1,25},{9,1},{17,9},{25,17},{2,26},{10... | collective-permute-start | bytes 1179656 | tf_op jit(solution)/shard_map/ppermute | solution.py:28
  34.9 3.4 %collective-permute-done.9 = bf16[16,3072]{1,0:T(8,128)(2,1)S(1)} collective-permute-done((bf16[16,3072]{1,0:T(8,128)(2,1)S(1)}, bf16[16,3072]{1,0:T(8,128)(2,1)S(1)}, u32[]{:S(2)}, u32[]{:S(2)}) %collective-permute-start.9) | collective-permute-done | bytes 98336 | tf_op jit(solution)/shard_map/ppermute | solution.py:28
  38.3 3.1 %collective-permute-done.8 = bf16[16,3072]{1,0:T(8,128)(2,1)S(1)} collective-permute-done((bf16[16,3072]{1,0:T(8,128)(2,1)S(1)}, bf16[16,3072]{1,0:T(8,128)(2,1)S(1)}, u32[]{:S(2)}, u32[]{:S(2)}) %collective-permute-start.8) | collective-permute-done | bytes 98336 | tf_op jit(solution)/shard_map/ppermute | solution.py:28
  41.4 1.9 %collective-permute-start.13 = (bf16[4,16,3072]{2,1,0:T(8,128)(2,1)S(1)}, bf16[4,16,3072]{2,1,0:T(8,128)(2,1)S(1)}, u32[]{:S(2)}, u32[]{:S(2)}) collective-permute-start(bf16[4,16,3072]{2,1,0:T(8,128)(2,1)S(1)} %pad_maximum_fusion.2.refs_4_), channel_id=1, source_target_pairs={{0,128},{64,192},{128,0},{192,64},{1,129},{65,193},{129,1},{193,65... | collective-permute-start | bytes 1179656 | tf_op jit(solution)/shard_map/ppermute | solution.py:28
  43.3 2.7 %collective-permute-start.12 = (bf16[4,16,3072]{2,1,0:T(8,128)(2,1)S(1)}, bf16[4,16,3072]{2,1,0:T(8,128)(2,1)S(1)}, u32[]{:S(2)}, u32[]{:S(2)}) collective-permute-start(bf16[4,16,3072]{2,1,0:T(8,128)(2,1)S(1)} %pad_maximum_fusion.2.refs_4_), channel_id=1, source_target_pairs={{0,192},{64,0},{128,64},{192,128},{1,193},{65,1},{129,65},{193,129... | collective-permute-start | bytes 1179656 | tf_op jit(solution)/shard_map/ppermute | solution.py:28
  47.6 1.6 %collective-permute-done.6.refs_2_ = bf16[4,16,3072]{2,1,0:T(8,128)(2,1)S(1)} collective-permute-done((bf16[4,16,3072]{2,1,0:T(8,128)(2,1)S(1)}, bf16[4,16,3072]{2,1,0:T(8,128)(2,1)S(1)}, u32[]{:S(2)}, u32[]{:S(2)}) %collective-permute-start.6) | collective-permute-done | bytes 393248 | tf_op jit(solution)/shard_map/ppermute | solution.py:28
  51.1 2.7 %collective-permute-done.12.refs_6_ = bf16[4,16,3072]{2,1,0:T(8,128)(2,1)S(1)} collective-permute-done((bf16[4,16,3072]{2,1,0:T(8,128)(2,1)S(1)}, bf16[4,16,3072]{2,1,0:T(8,128)(2,1)S(1)}, u32[]{:S(2)}, u32[]{:S(2)}) %collective-permute-start.12) | collective-permute-done | bytes 393248 | tf_op jit(solution)/shard_map/ppermute | solution.py:28
  56.2 11.8 %shard_map.68 = (f32[2,592,256]{2,1,0:T(8,128)}, f32[2,592,256]{2,1,0:T(8,128)}, bf16[256,2048]{1,0:T(8,128)(2,1)}, f32[16,1,768]{2,1,0:T(1,128)}, f32[2,256]{1,0:T(2,128)}) custom-call(s32[2]{0:T(128)} %pad_add_fusion.at, f32[1,256]{1,0:T(1,128)} %copy-done.8, bf16[4,16,3072]{2,1,0:T(8,128)(2,1)} %copy-done.1, bf16[4,16,3072]{2,1,0:T(8,128)(2,1)} %copy-done.5, ...), custom_call_target="tpu_custom_call" | custom-call | flops 3724541952 | bytes 17694720 | tf_op jit(solution)/shard_map/pallas_call | solution.py:140
  68.1 14.1 %all_to_all.26 = f32[16,1,768]{2,1,0:T(1,128)S(1)} all-to-all(f32[16,1,768]{2,1,0:T(1,128)} %get-tuple-element.29), channel_id=1, replica_groups=mesh['x'=4,'zl'=2,'y'=4,'zh'=4,'c'=2] {'x','y'}, dimensions={0} | all-to-all | bytes 98304 | tf_op jit(solution)/shard_map/all_to_all | solution.py:283
  82.4 9.7 %all_to_all.27.logs = f32[8,1,768]{2,1,0:T(1,128)} all-to-all(f32[8,1,768]{2,1,0:T(1,128)S(1)} %broadcast_in_dim.25), channel_id=1, replica_groups=mesh['x'=4,'zl'=2,'y'=4,'zh'=4,'c'=2] {'zl','zh'}, dimensions={0} | all-to-all | bytes 49152 | tf_op jit(solution)/shard_map/all_to_all | solution.py:21
  92.1 7.8 %shard_map.69 = (bf16[592,256]{1,0:T(8,128)(2,1)}, bf16[256,2048]{1,0:T(8,128)(2,1)}, bf16[592,512]{1,0:T(8,128)(2,1)}, bf16[592,512]{1,0:T(8,128)(2,1)}, bf16[5...) custom-call(f32[2,592,256]{2,1,0:T(8,128)} %get-tuple-element.26.teach, f32[2,592,256]{2,1,0:T(8,128)} %get-tuple-element.27.stud, ...), custom_call_target="tpu_custom_call" | custom-call | flops 1862270976 | bytes 9699328 | tf_op jit(solution)/shard_map/pallas_call | solution.py:237
  100.0 3.7 %all-to-all-start.3 = ((bf16[16,16,2048]{2,1,0:T(8,128)(2,1)}), bf16[16,16,2048]{2,1,0:T(8,128)(2,1)S(1)}, u32[]{:S(2)}, u32[]{:S(2)}) async-start(bf16[16,16,2048]{2,1,0:T(8,128)(2,1)} %bitcast.18), calls=%async_computation.3 | async-start | bytes 2097152 | tf_op jit(solution)/shard_map/all_to_all | solution.py:41
  104.7 3.9 %fusion = f32[592,2048]{1,0:T(8,128)} fusion(bf16[592,256]{1,0:T(8,128)(2,1)} %get-tuple-element.32, bf16[256,2048]{1,0:T(8,128)(2,1)S(1)} %copy-done), kind=kOutput, calls=%fused_computation.14 | convolution fusion | flops 620756992 | bytes 6201344 | tf_op jit(solution)/shard_map/dot_general | solution.py:289
  109.0 7.5 %all-to-all-done.3 = bf16[16,16,2048]{2,1,0:T(8,128)(2,1)S(1)} async-done(((bf16[16,16,2048]{2,1,0:T(8,128)(2,1)}), bf16[16,16,2048]{2,1,0:T(8,128)(2,1)S(1)}, u32[]{:S(2)}, u32[]{:S(2)}) %all-to-all-start.3) | async-done | bytes 1048608 | tf_op jit(solution)/shard_map/all_to_all | solution.py:41
  117.3 1.6 %reshape.44 = f32[8,2,2048]{2,1,0:T(2,128)} reshape(f32[16,2048]{1,0:T(8,128)} %convert_reduce_fusion) | data formatting | bytes 262144 | tf_op jit(solution)/shard_map/reshape | solution.py:288
  118.9 4.6 %all-to-all-start.4 = ((f32[8,2,2048]{2,1,0:T(2,128)}), f32[8,2,2048]{2,1,0:T(2,128)S(1)}, u32[]{:S(2)}, u32[]{:S(2)}) async-start(f32[8,2,2048]{2,1,0:T(2,128)} %reshape.44), calls=%async_computation.4 | async-start | bytes 262144 | tf_op jit(solution)/shard_map/all_to_all | solution.py:41
  123.5 4.6 %add_convert_fusion = bf16[592,2048]{1,0:T(8,128)(2,1)} fusion(f32[592,2048]{1,0:T(8,128)} %fusion, bf16[592,2048]{1,0:T(8,128)(2,1)S(1)} %pad_maximum_fusion), kind=kLoop, calls=%fused_computation | loop fusion | flops 3637248 | bytes 9699328 | tf_op jit(solution)/shard_map/convert_element_type | solution.py:292
  128.1 3.0 %all-to-all-done.4 = f32[8,2,2048]{2,1,0:T(2,128)S(1)} async-done(((f32[8,2,2048]{2,1,0:T(2,128)}), f32[8,2,2048]{2,1,0:T(2,128)S(1)}, u32[]{:S(2)}, u32[]{:S(2)}) %all-to-all-start.4) | async-done | bytes 131104 | tf_op jit(solution)/shard_map/all_to_all | solution.py:41
  (60 shorter events, 10.6 us)
Async XLA Ops:
  0.6 19.2 %collective-permute-start = (bf16[592,4096]{1,0:T(8,128)(2,1)}, bf16[592,4096]{1,0:T(8,128)(2,1)}, u32[]{:S(2)}, u32[]{:S(2)}) collective-permute-start(bf16[592,4096]{1,0:T(8,128)(2,1)} %refs_8_), channel_id=1, source_target_pairs={{0,1},{1,0},{2,3},{3,2},{4,5},{5,4},{6,7},{7,6},{8,9},{9,8},{10,11... | collective-permute-start | bytes 14549000 | tf_op jit(solution)/shard_map/ppermute | solution.py:46
  0.7 19.1 %collective-permute-start.1 = (bf16[592,2048]{1,0:T(8,128)(2,1)}, bf16[592,2048]{1,0:T(8,128)(2,1)}, u32[]{:S(2)}, u32[]{:S(2)}) collective-permute-start(bf16[592,2048]{1,0:T(8,128)(2,1)} %head0), channel_id=1, source_target_pairs={{0,1},{1,0},{2,3},{3,2},{4,5},{5,4},{6,7},{7,6},{8,9},{9,8},{10,11... | collective-permute-start | bytes 7274504 | tf_op jit(solution)/shard_map/ppermute | solution.py:46
  19.8 8.1 %collective-permute-start.3 = (bf16[16,3072]{1,0:T(8,128)(2,1)S(1)}, bf16[16,3072]{1,0:T(8,128)(2,1)S(1)}, u32[]{:S(2)}, u32[]{:S(2)}) collective-permute-start(bf16[16,3072]{1,0:T(8,128)(2,1)S(1)} %get-tuple-element.43), channel_id=1, source_target_pairs={{0,192},{64,0},{128,64},{192,128},{1,193},{65,1},{129,65},{193,129... | collective-permute-start | bytes 294920 | tf_op jit(solution)/shard_map/ppermute | solution.py:28
  22.7 7.5 %collective-permute-start.2 = (bf16[16,3072]{1,0:T(8,128)(2,1)S(1)}, bf16[16,3072]{1,0:T(8,128)(2,1)S(1)}, u32[]{:S(2)}, u32[]{:S(2)}) collective-permute-start(bf16[16,3072]{1,0:T(8,128)(2,1)S(1)} %get-tuple-element.43), channel_id=1, source_target_pairs={{0,64},{64,128},{128,192},{192,0},{1,65},{65,129},{129,193},{193,1... | collective-permute-start | bytes 294920 | tf_op jit(solution)/shard_map/ppermute | solution.py:28
  22.7 7.5 %collective-permute-start.4 = (bf16[16,3072]{1,0:T(8,128)(2,1)S(1)}, bf16[16,3072]{1,0:T(8,128)(2,1)S(1)}, u32[]{:S(2)}, u32[]{:S(2)}) collective-permute-start(bf16[16,3072]{1,0:T(8,128)(2,1)S(1)} %get-tuple-element.43), channel_id=1, source_target_pairs={{0,128},{64,192},{128,0},{192,64},{1,129},{65,193},{129,1},{193,65... | collective-permute-start | bytes 294920 | tf_op jit(solution)/shard_map/ppermute | solution.py:28
  25.0 13.3 %collective-permute-start.9 = (bf16[16,3072]{1,0:T(8,128)(2,1)S(1)}, bf16[16,3072]{1,0:T(8,128)(2,1)S(1)}, u32[]{:S(2)}, u32[]{:S(2)}) collective-permute-start(bf16[16,3072]{1,0:T(8,128)(2,1)S(1)} %get-tuple-element.42), channel_id=1, source_target_pairs={{0,24},{8,0},{16,8},{24,16},{1,25},{9,1},{17,9},{25,17},{2,26},{10... | collective-permute-start | bytes 294920 | tf_op jit(solution)/shard_map/ppermute | solution.py:28
  28.0 13.4 %collective-permute-start.8 = (bf16[16,3072]{1,0:T(8,128)(2,1)S(1)}, bf16[16,3072]{1,0:T(8,128)(2,1)S(1)}, u32[]{:S(2)}, u32[]{:S(2)}) collective-permute-start(bf16[16,3072]{1,0:T(8,128)(2,1)S(1)} %get-tuple-element.42), channel_id=1, source_target_pairs={{0,8},{8,16},{16,24},{24,0},{1,9},{9,17},{17,25},{25,1},{2,10},{10... | collective-permute-start | bytes 294920 | tf_op jit(solution)/shard_map/ppermute | solution.py:28
  28.0 13.4 %collective-permute-start.10 = (bf16[16,3072]{1,0:T(8,128)(2,1)S(1)}, bf16[16,3072]{1,0:T(8,128)(2,1)S(1)}, u32[]{:S(2)}, u32[]{:S(2)}) collective-permute-start(bf16[16,3072]{1,0:T(8,128)(2,1)S(1)} %get-tuple-element.42), channel_id=1, source_target_pairs={{0,16},{8,24},{16,0},{24,8},{1,17},{9,25},{17,1},{25,9},{2,18},{10... | collective-permute-start | bytes 294920 | tf_op jit(solution)/shard_map/ppermute | solution.py:28
  30.3 26.0 %copy-start.1 = (bf16[4,16,3072]{2,1,0:T(8,128)(2,1)}, bf16[4,16,3072]{2,1,0:T(8,128)(2,1)S(1)}, u32[]{:S(2)}) copy-start(bf16[4,16,3072]{2,1,0:T(8,128)(2,1)S(1)} %pad_maximum_fusion.1.refs_0_) | copy-start | bytes 1179652
  30.3 15.7 %collective-permute-start.7 = (bf16[4,16,3072]{2,1,0:T(8,128)(2,1)S(1)}, bf16[4,16,3072]{2,1,0:T(8,128)(2,1)S(1)}, u32[]{:S(2)}, u32[]{:S(2)}) collective-permute-start(bf16[4,16,3072]{2,1,0:T(8,128)(2,1)S(1)} %pad_maximum_fusion.1.refs_0_), channel_id=1, source_target_pairs={{0,16},{8,24},{16,0},{24,8},{1,17},{9,25},{17,1},{25,9},{2,18},{10... | collective-permute-start | bytes 1179656 | tf_op jit(solution)/shard_map/ppermute | solution.py:28
  32.9 16.4 %collective-permute-start.6 = (bf16[4,16,3072]{2,1,0:T(8,128)(2,1)S(1)}, bf16[4,16,3072]{2,1,0:T(8,128)(2,1)S(1)}, u32[]{:S(2)}, u32[]{:S(2)}) collective-permute-start(bf16[4,16,3072]{2,1,0:T(8,128)(2,1)S(1)} %pad_maximum_fusion.1.refs_0_), channel_id=1, source_target_pairs={{0,24},{8,0},{16,8},{24,16},{1,25},{9,1},{17,9},{25,17},{2,26},{10... | collective-permute-start | bytes 1179656 | tf_op jit(solution)/shard_map/ppermute | solution.py:28
  38.3 12.6 %collective-permute-start.5 = (bf16[4,16,3072]{2,1,0:T(8,128)(2,1)S(1)}, bf16[4,16,3072]{2,1,0:T(8,128)(2,1)S(1)}, u32[]{:S(2)}, u32[]{:S(2)}) collective-permute-start(bf16[4,16,3072]{2,1,0:T(8,128)(2,1)S(1)} %pad_maximum_fusion.1.refs_0_), channel_id=1, source_target_pairs={{0,8},{8,16},{16,24},{24,0},{1,9},{9,17},{17,25},{25,1},{2,10},{10... | collective-permute-start | bytes 1179656 | tf_op jit(solution)/shard_map/ppermute | solution.py:28
  41.4 14.8 %copy-start.2 = (bf16[4,16,3072]{2,1,0:T(8,128)(2,1)}, bf16[4,16,3072]{2,1,0:T(8,128)(2,1)S(1)}, u32[]{:S(2)}) copy-start(bf16[4,16,3072]{2,1,0:T(8,128)(2,1)S(1)} %pad_maximum_fusion.2.refs_4_) | copy-start | bytes 1179652
  41.4 9.7 %collective-permute-start.13 = (bf16[4,16,3072]{2,1,0:T(8,128)(2,1)S(1)}, bf16[4,16,3072]{2,1,0:T(8,128)(2,1)S(1)}, u32[]{:S(2)}, u32[]{:S(2)}) collective-permute-start(bf16[4,16,3072]{2,1,0:T(8,128)(2,1)S(1)} %pad_maximum_fusion.2.refs_4_), channel_id=1, source_target_pairs={{0,128},{64,192},{128,0},{192,64},{1,129},{65,193},{129,1},{193,65... | collective-permute-start | bytes 1179656 | tf_op jit(solution)/shard_map/ppermute | solution.py:28
  43.3 10.5 %collective-permute-start.12 = (bf16[4,16,3072]{2,1,0:T(8,128)(2,1)S(1)}, bf16[4,16,3072]{2,1,0:T(8,128)(2,1)S(1)}, u32[]{:S(2)}, u32[]{:S(2)}) collective-permute-start(bf16[4,16,3072]{2,1,0:T(8,128)(2,1)S(1)} %pad_maximum_fusion.2.refs_4_), channel_id=1, source_target_pairs={{0,192},{64,0},{128,64},{192,128},{1,193},{65,1},{129,65},{193,129... | collective-permute-start | bytes 1179656 | tf_op jit(solution)/shard_map/ppermute | solution.py:28
  46.0 10.2 %copy-start.3 = (bf16[4,16,3072]{2,1,0:T(8,128)(2,1)}, bf16[4,16,3072]{2,1,0:T(8,128)(2,1)S(1)}, u32[]{:S(2)}) copy-start(bf16[4,16,3072]{2,1,0:T(8,128)(2,1)S(1)} %collective-permute-done.7.refs_3_) | copy-start | bytes 1179652
  46.0 10.2 %collective-permute-start.11 = (bf16[4,16,3072]{2,1,0:T(8,128)(2,1)S(1)}, bf16[4,16,3072]{2,1,0:T(8,128)(2,1)}, u32[]{:S(2)}, u32[]{:S(2)}) collective-permute-start(bf16[4,16,3072]{2,1,0:T(8,128)(2,1)S(1)} %pad_maximum_fusion.2.refs_4_), channel_id=1, source_target_pairs={{0,64},{64,128},{128,192},{192,0},{1,65},{65,129},{129,193},{193,1... | collective-permute-start | bytes 1179656 | tf_op jit(solution)/shard_map/ppermute | solution.py:28
  92.1 12.6 %copy-start = (bf16[256,2048]{1,0:T(8,128)(2,1)S(1)}, bf16[256,2048]{1,0:T(8,128)(2,1)}, u32[]{:S(2)}) copy-start(bf16[256,2048]{1,0:T(8,128)(2,1)} %get-tuple-element.28.rows) | copy-start | bytes 3145732
  100.0 16.5 %all-to-all-start.3 = ((bf16[16,16,2048]{2,1,0:T(8,128)(2,1)}), bf16[16,16,2048]{2,1,0:T(8,128)(2,1)S(1)}, u32[]{:S(2)}, u32[]{:S(2)}) async-start(bf16[16,16,2048]{2,1,0:T(8,128)(2,1)} %bitcast.18), calls=%async_computation.3 | async-start | bytes 2097152 | tf_op jit(solution)/shard_map/all_to_all | solution.py:41
  103.6 5.0 %collective-permute-start.14 = (bf16[592,512]{1,0:T(8,128)(2,1)}, bf16[592,512]{1,0:T(8,128)(2,1)S(1)}, u32[]{:S(2)}, u32[]{:S(2)}) collective-permute-start(bf16[592,512]{1,0:T(8,128)(2,1)} %get-tuple-element.33), channel_id=1, source_target_pairs={{0,1},{1,0},{2,3},{3,2},{4,5},{5,4},{6,7},{7,6},{8,9},{9,8},{10,11... | collective-permute-start | bytes 1818632 | tf_op jit(solution)/shard_map/ppermute | solution.py:46
  103.7 5.0 %collective-permute-start.15 = (bf16[592,512]{1,0:T(8,128)(2,1)}, bf16[592,512]{1,0:T(8,128)(2,1)S(1)}, u32[]{:S(2)}, u32[]{:S(2)}) collective-permute-start(bf16[592,512]{1,0:T(8,128)(2,1)} %get-tuple-element.34), channel_id=1, source_target_pairs={{0,1},{1,0},{2,3},{3,2},{4,5},{5,4},{6,7},{7,6},{8,9},{9,8},{10,11... | collective-permute-start | bytes 1818632 | tf_op jit(solution)/shard_map/ppermute | solution.py:46
  104.2 4.5 %collective-permute-start.16 = (bf16[592,512]{1,0:T(8,128)(2,1)}, bf16[592,512]{1,0:T(8,128)(2,1)S(1)}, u32[]{:S(2)}, u32[]{:S(2)}) collective-permute-start(bf16[592,512]{1,0:T(8,128)(2,1)} %get-tuple-element.35), channel_id=1, source_target_pairs={{0,1},{1,0},{2,3},{3,2},{4,5},{5,4},{6,7},{7,6},{8,9},{9,8},{10,11... | collective-permute-start | bytes 1818632 | tf_op jit(solution)/shard_map/ppermute | solution.py:46
  104.3 4.4 %collective-permute-start.17 = (bf16[592,512]{1,0:T(8,128)(2,1)}, bf16[592,512]{1,0:T(8,128)(2,1)S(1)}, u32[]{:S(2)}, u32[]{:S(2)}) collective-permute-start(bf16[592,512]{1,0:T(8,128)(2,1)} %get-tuple-element.36), channel_id=1, source_target_pairs={{0,1},{1,0},{2,3},{3,2},{4,5},{5,4},{6,7},{7,6},{8,9},{9,8},{10,11... | collective-permute-start | bytes 1818632 | tf_op jit(solution)/shard_map/ppermute | solution.py:46
  118.9 12.2 %all-to-all-start.4 = ((f32[8,2,2048]{2,1,0:T(2,128)}), f32[8,2,2048]{2,1,0:T(2,128)S(1)}, u32[]{:S(2)}, u32[]{:S(2)}) async-start(f32[8,2,2048]{2,1,0:T(2,128)} %reshape.44), calls=%async_computation.4 | async-start | bytes 262144 | tf_op jit(solution)/shard_map/all_to_all | solution.py:41
  (5 other events, 25.0 us)

commit v6 on v5

--- a/solution.py
+++ b/solution.py
@@ -9,7 +9,7 @@
 SIZES = (4, 2, 4, 4, 2)
 PLANE, LINE, PAIR = ("x", "y"), ("zl", "zh"), ("c",)
 NP, NL = 16, 8
-STEPS = (0, 1, 3, 2)
+STEPS = (0, 3, 1, 2)
 VMEM_LIMIT = 62 * 2**20
 HBM, SMEM = pl.BlockSpec(memory_space=pltpu.HBM), pl.BlockSpec(memory_space=pltpu.SMEM)
 VMEM = pl.BlockSpec(memory_space=pltpu.VMEM)

time: 132 us -> 131 us (level)
    ppermute x12, waiting for transfers between devices: 14.3 us -> 12.8 us  [ring(): lax.ppermute(block, axis, [(i, (i + step) % 4) for i in range(4)])]
  transfers between devices with their start and end apart: 20 -> 20, of which waited for: 9 -> 5; matrix products, arithmetic and copies ran while one was open for 9% -> 9% of each run, Pallas kernels for 0% -> 0%
where the time goes in v6:
time: 131 us; the launch traced here: 130 us
  blocking collectives  40.5 us (31%)
  starting transfers between devices  29.5 us (23%)
  waiting for transfers between devices  24.1 us (18%)
  Pallas kernels  19.6 us (15%)
  other arithmetic  8 us (6%)
  matrix products  3.94 us (3%)
  local copies, waits for them, and re-layouts  3.5 us (3%)
    all_to_all x2, blocking collectives, share(): lax.all_to_all(jnp.broadcast_to(block[None], (n,) + block.shape), axes, 0...  27.6 us
    ppermute x12, starting transfers between devices, ring(): lax.ppermute(block, axis, [(i, (i + step) % 4) for i in range(4)])  19.6 us
    all_to_all x1, blocking collectives, on_device(): logs = join(lax.all_to_all(logs, PLANE, 0, 0, tiled=True), nt)  12.9 us
    ppermute x12, waiting for transfers between devices, ring(): lax.ppermute(block, axis, [(i, (i + step) % 4) for i in range(4)])  12.8 us
    pallas_call x1, Pallas kernels, logits(): pl.pallas_call(logits_kernel, out_shape=[shape((2, ve, nt), jnp.float32),...  11.8 us
    all_to_all x2, waiting for transfers between devices, plane_sum(): got = lax.all_to_all(blocks, axes, 0, 0, tiled=True)  11.3 us
    all_to_all x2, starting transfers between devices, plane_sum(): got = lax.all_to_all(blocks, axes, 0, 0, tiled=True)  8.26 us
    pallas_call x1, Pallas kernels, grads(): pl.pallas_call(grad_kernel, out_shape=[shape((ve, nt), jnp.bfloat16), sha...  7.8 us
  transfers between devices with their start and end apart: 20, of which 5 were waited for; matrix products, arithmetic and copies ran while one was open for 9% of the time, Pallas kernels for 0%

profile of v6, /device:TPU:32, one launch (start us, length us, event | category | flops | bytes accessed | tf_op | source)
XLA Modules:
  0.0 130.1 jit_solution(15387189526387070831)
XLA Ops:
  2.1 17.6 %all_to_all.25 = bf16[8,2,6144]{2,1,0:T(2,128)(2,1)S(1)} all-to-all(bf16[8,2,6144]{2,1,0:T(2,128)(2,1)S(1)} %broadcast_in_dim.23), channel_id=1, replica_groups=mesh['x'=4,'zl'=2,'y'=4,'zh'=4,'c'=2] {'zl','zh'}, dimensions={0} | all-to-all | bytes 393216 | tf_op jit(solution)/shard_map/all_to_all | solution.py:21
  19.8 1.6 %collective-permute-start.3 = (bf16[16,3072]{1,0:T(8,128)(2,1)S(1)}, bf16[16,3072]{1,0:T(8,128)(2,1)S(1)}, u32[]{:S(2)}, u32[]{:S(2)}) collective-permute-start(bf16[16,3072]{1,0:T(8,128)(2,1)S(1)} %get-tuple-element.43), channel_id=1, source_target_pairs={{0,64},{64,128},{128,192},{192,0},{1,65},{65,129},{129,193},{193,1... | collective-permute-start | bytes 294920 | tf_op jit(solution)/shard_map/ppermute | solution.py:28
  21.4 1.7 %collective-permute-start.2 = (bf16[16,3072]{1,0:T(8,128)(2,1)S(1)}, bf16[16,3072]{1,0:T(8,128)(2,1)S(1)}, u32[]{:S(2)}, u32[]{:S(2)}) collective-permute-start(bf16[16,3072]{1,0:T(8,128)(2,1)S(1)} %get-tuple-element.43), channel_id=1, source_target_pairs={{0,192},{64,0},{128,64},{192,128},{1,193},{65,1},{129,65},{193,129... | collective-permute-start | bytes 294920 | tf_op jit(solution)/shard_map/ppermute | solution.py:28
  23.2 1.8 %collective-permute-start.4 = (bf16[16,3072]{1,0:T(8,128)(2,1)S(1)}, bf16[16,3072]{1,0:T(8,128)(2,1)S(1)}, u32[]{:S(2)}, u32[]{:S(2)}) collective-permute-start(bf16[16,3072]{1,0:T(8,128)(2,1)S(1)} %get-tuple-element.43), channel_id=1, source_target_pairs={{0,128},{64,192},{128,0},{192,64},{1,129},{65,193},{129,1},{193,65... | collective-permute-start | bytes 294920 | tf_op jit(solution)/shard_map/ppermute | solution.py:28
  25.0 1.6 %collective-permute-start.9 = (bf16[16,3072]{1,0:T(8,128)(2,1)S(1)}, bf16[16,3072]{1,0:T(8,128)(2,1)S(1)}, u32[]{:S(2)}, u32[]{:S(2)}) collective-permute-start(bf16[16,3072]{1,0:T(8,128)(2,1)S(1)} %get-tuple-element.42), channel_id=1, source_target_pairs={{0,8},{8,16},{16,24},{24,0},{1,9},{9,17},{17,25},{25,1},{2,10},{10... | collective-permute-start | bytes 294920 | tf_op jit(solution)/shard_map/ppermute | solution.py:28
  26.5 1.7 %collective-permute-start.8 = (bf16[16,3072]{1,0:T(8,128)(2,1)S(1)}, bf16[16,3072]{1,0:T(8,128)(2,1)S(1)}, u32[]{:S(2)}, u32[]{:S(2)}) collective-permute-start(bf16[16,3072]{1,0:T(8,128)(2,1)S(1)} %get-tuple-element.42), channel_id=1, source_target_pairs={{0,24},{8,0},{16,8},{24,16},{1,25},{9,1},{17,9},{25,17},{2,26},{10... | collective-permute-start | bytes 294920 | tf_op jit(solution)/shard_map/ppermute | solution.py:28
  28.2 2.0 %collective-permute-start.10 = (bf16[16,3072]{1,0:T(8,128)(2,1)S(1)}, bf16[16,3072]{1,0:T(8,128)(2,1)S(1)}, u32[]{:S(2)}, u32[]{:S(2)}) collective-permute-start(bf16[16,3072]{1,0:T(8,128)(2,1)S(1)} %get-tuple-element.42), channel_id=1, source_target_pairs={{0,16},{8,24},{16,0},{24,8},{1,17},{9,25},{17,1},{25,9},{2,18},{10... | collective-permute-start | bytes 294920 | tf_op jit(solution)/shard_map/ppermute | solution.py:28
  30.3 2.4 %collective-permute-start.7 = (bf16[4,16,3072]{2,1,0:T(8,128)(2,1)S(1)}, bf16[4,16,3072]{2,1,0:T(8,128)(2,1)S(1)}, u32[]{:S(2)}, u32[]{:S(2)}) collective-permute-start(bf16[4,16,3072]{2,1,0:T(8,128)(2,1)S(1)} %pad_maximum_fusion.1.refs_0_), channel_id=1, source_target_pairs={{0,16},{8,24},{16,0},{24,8},{1,17},{9,25},{17,1},{25,9},{2,18},{10... | collective-permute-start | bytes 1179656 | tf_op jit(solution)/shard_map/ppermute | solution.py:28
  33.3 2.6 %collective-permute-start.5 = (bf16[4,16,3072]{2,1,0:T(8,128)(2,1)S(1)}, bf16[4,16,3072]{2,1,0:T(8,128)(2,1)S(1)}, u32[]{:S(2)}, u32[]{:S(2)}) collective-permute-start(bf16[4,16,3072]{2,1,0:T(8,128)(2,1)S(1)} %pad_maximum_fusion.1.refs_0_), channel_id=1, source_target_pairs={{0,24},{8,0},{16,8},{24,16},{1,25},{9,1},{17,9},{25,17},{2,26},{10... | collective-permute-start | bytes 1179656 | tf_op jit(solution)/shard_map/ppermute | solution.py:28
  35.9 1.9 %collective-permute-start.13 = (bf16[4,16,3072]{2,1,0:T(8,128)(2,1)S(1)}, bf16[4,16,3072]{2,1,0:T(8,128)(2,1)S(1)}, u32[]{:S(2)}, u32[]{:S(2)}) collective-permute-start(bf16[4,16,3072]{2,1,0:T(8,128)(2,1)S(1)} %pad_maximum_fusion.2.refs_4_), channel_id=1, source_target_pairs={{0,128},{64,192},{128,0},{192,64},{1,129},{65,193},{129,1},{193,65... | collective-permute-start | bytes 1179656 | tf_op jit(solution)/shard_map/ppermute | solution.py:28
  38.4 5.4 %collective-permute-done.7.refs_3_ = bf16[4,16,3072]{2,1,0:T(8,128)(2,1)S(1)} collective-permute-done((bf16[4,16,3072]{2,1,0:T(8,128)(2,1)S(1)}, bf16[4,16,3072]{2,1,0:T(8,128)(2,1)S(1)}, u32[]{:S(2)}, u32[]{:S(2)}) %collective-permute-start.7) | collective-permute-done | bytes 393248 | tf_op jit(solution)/shard_map/ppermute | solution.py:28
  46.5 3.5 %collective-permute-done.6.refs_2_ = bf16[4,16,3072]{2,1,0:T(8,128)(2,1)S(1)} collective-permute-done((bf16[4,16,3072]{2,1,0:T(8,128)(2,1)S(1)}, bf16[4,16,3072]{2,1,0:T(8,128)(2,1)S(1)}, u32[]{:S(2)}, u32[]{:S(2)}) %collective-permute-start.6) | collective-permute-done | bytes 393248 | tf_op jit(solution)/shard_map/ppermute | solution.py:28
  50.0 3.8 %collective-permute-done.12.refs_6_ = bf16[4,16,3072]{2,1,0:T(8,128)(2,1)S(1)} collective-permute-done((bf16[4,16,3072]{2,1,0:T(8,128)(2,1)S(1)}, bf16[4,16,3072]{2,1,0:T(8,128)(2,1)S(1)}, u32[]{:S(2)}, u32[]{:S(2)}) %collective-permute-start.12) | collective-permute-done | bytes 393248 | tf_op jit(solution)/shard_map/ppermute | solution.py:28
  54.6 11.8 %shard_map.68 = (f32[2,592,256]{2,1,0:T(8,128)}, f32[2,592,256]{2,1,0:T(8,128)}, bf16[256,2048]{1,0:T(8,128)(2,1)}, f32[16,1,768]{2,1,0:T(1,128)}, f32[2,256]{1,0:T(2,128)}) custom-call(s32[2]{0:T(128)} %pad_add_fusion.at, f32[1,256]{1,0:T(1,128)} %copy-done.8, bf16[4,16,3072]{2,1,0:T(8,128)(2,1)} %copy-done.1, bf16[4,16,3072]{2,1,0:T(8,128)(2,1)} %copy-done.5, ...), custom_call_target="tpu_custom_call" | custom-call | flops 3724541952 | bytes 17694720 | tf_op jit(solution)/shard_map/pallas_call | solution.py:140
  66.4 12.9 %all_to_all.26 = f32[16,1,768]{2,1,0:T(1,128)S(1)} all-to-all(f32[16,1,768]{2,1,0:T(1,128)} %get-tuple-element.29), channel_id=1, replica_groups=mesh['x'=4,'zl'=2,'y'=4,'zh'=4,'c'=2] {'x','y'}, dimensions={0} | all-to-all | bytes 98304 | tf_op jit(solution)/shard_map/all_to_all | solution.py:283
  79.6 10.0 %all_to_all.27.logs = f32[8,1,768]{2,1,0:T(1,128)} all-to-all(f32[8,1,768]{2,1,0:T(1,128)S(1)} %broadcast_in_dim.25), channel_id=1, replica_groups=mesh['x'=4,'zl'=2,'y'=4,'zh'=4,'c'=2] {'zl','zh'}, dimensions={0} | all-to-all | bytes 49152 | tf_op jit(solution)/shard_map/all_to_all | solution.py:21
  89.6 7.8 %shard_map.69 = (bf16[592,256]{1,0:T(8,128)(2,1)}, bf16[256,2048]{1,0:T(8,128)(2,1)}, bf16[592,512]{1,0:T(8,128)(2,1)}, bf16[592,512]{1,0:T(8,128)(2,1)}, bf16[5...) custom-call(f32[2,592,256]{2,1,0:T(8,128)} %get-tuple-element.26.teach, f32[2,592,256]{2,1,0:T(8,128)} %get-tuple-element.27.stud, ...), custom_call_target="tpu_custom_call" | custom-call | flops 1862270976 | bytes 9699328 | tf_op jit(solution)/shard_map/pallas_call | solution.py:237
  97.4 3.7 %all-to-all-start.3 = ((bf16[16,16,2048]{2,1,0:T(8,128)(2,1)}), bf16[16,16,2048]{2,1,0:T(8,128)(2,1)S(1)}, u32[]{:S(2)}, u32[]{:S(2)}) async-start(bf16[16,16,2048]{2,1,0:T(8,128)(2,1)} %bitcast.18), calls=%async_computation.3 | async-start | bytes 2097152 | tf_op jit(solution)/shard_map/all_to_all | solution.py:41
  102.2 3.9 %fusion = f32[592,2048]{1,0:T(8,128)} fusion(bf16[592,256]{1,0:T(8,128)(2,1)} %get-tuple-element.32, bf16[256,2048]{1,0:T(8,128)(2,1)S(1)} %copy-done), kind=kOutput, calls=%fused_computation.14 | convolution fusion | flops 620756992 | bytes 6201344 | tf_op jit(solution)/shard_map/dot_general | solution.py:289
  106.4 8.3 %all-to-all-done.3 = bf16[16,16,2048]{2,1,0:T(8,128)(2,1)S(1)} async-done(((bf16[16,16,2048]{2,1,0:T(8,128)(2,1)}), bf16[16,16,2048]{2,1,0:T(8,128)(2,1)S(1)}, u32[]{:S(2)}, u32[]{:S(2)}) %all-to-all-start.3) | async-done | bytes 1048608 | tf_op jit(solution)/shard_map/all_to_all | solution.py:41
  115.6 1.6 %reshape.44 = f32[8,2,2048]{2,1,0:T(2,128)} reshape(f32[16,2048]{1,0:T(8,128)} %convert_reduce_fusion) | data formatting | bytes 262144 | tf_op jit(solution)/shard_map/reshape | solution.py:288
  117.2 4.6 %all-to-all-start.4 = ((f32[8,2,2048]{2,1,0:T(2,128)}), f32[8,2,2048]{2,1,0:T(2,128)S(1)}, u32[]{:S(2)}, u32[]{:S(2)}) async-start(f32[8,2,2048]{2,1,0:T(2,128)} %reshape.44), calls=%async_computation.4 | async-start | bytes 262144 | tf_op jit(solution)/shard_map/all_to_all | solution.py:41
  121.8 4.6 %add_convert_fusion = bf16[592,2048]{1,0:T(8,128)(2,1)} fusion(f32[592,2048]{1,0:T(8,128)} %fusion, bf16[592,2048]{1,0:T(8,128)(2,1)S(1)} %pad_maximum_fusion), kind=kLoop, calls=%fused_computation | loop fusion | flops 3637248 | bytes 9699328 | tf_op jit(solution)/shard_map/convert_element_type | solution.py:292
  126.4 3.0 %all-to-all-done.4 = f32[8,2,2048]{2,1,0:T(2,128)S(1)} async-done(((f32[8,2,2048]{2,1,0:T(2,128)}), f32[8,2,2048]{2,1,0:T(2,128)S(1)}, u32[]{:S(2)}, u32[]{:S(2)}) %all-to-all-start.4) | async-done | bytes 131104 | tf_op jit(solution)/shard_map/all_to_all | solution.py:41
  (60 shorter events, 9.4 us)
Async XLA Ops:
  0.6 19.2 %collective-permute-start = (bf16[592,4096]{1,0:T(8,128)(2,1)}, bf16[592,4096]{1,0:T(8,128)(2,1)}, u32[]{:S(2)}, u32[]{:S(2)}) collective-permute-start(bf16[592,4096]{1,0:T(8,128)(2,1)} %refs_8_), channel_id=1, source_target_pairs={{0,1},{1,0},{2,3},{3,2},{4,5},{5,4},{6,7},{7,6},{8,9},{9,8},{10,11... | collective-permute-start | bytes 14549000 | tf_op jit(solution)/shard_map/ppermute | solution.py:46
  0.7 19.1 %collective-permute-start.1 = (bf16[592,2048]{1,0:T(8,128)(2,1)}, bf16[592,2048]{1,0:T(8,128)(2,1)}, u32[]{:S(2)}, u32[]{:S(2)}) collective-permute-start(bf16[592,2048]{1,0:T(8,128)(2,1)} %head0), channel_id=1, source_target_pairs={{0,1},{1,0},{2,3},{3,2},{4,5},{5,4},{6,7},{7,6},{8,9},{9,8},{10,11... | collective-permute-start | bytes 7274504 | tf_op jit(solution)/shard_map/ppermute | solution.py:46
  19.8 8.4 %collective-permute-start.3 = (bf16[16,3072]{1,0:T(8,128)(2,1)S(1)}, bf16[16,3072]{1,0:T(8,128)(2,1)S(1)}, u32[]{:S(2)}, u32[]{:S(2)}) collective-permute-start(bf16[16,3072]{1,0:T(8,128)(2,1)S(1)} %get-tuple-element.43), channel_id=1, source_target_pairs={{0,64},{64,128},{128,192},{192,0},{1,65},{65,129},{129,193},{193,1... | collective-permute-start | bytes 294920 | tf_op jit(solution)/shard_map/ppermute | solution.py:28
  21.4 8.8 %collective-permute-start.2 = (bf16[16,3072]{1,0:T(8,128)(2,1)S(1)}, bf16[16,3072]{1,0:T(8,128)(2,1)S(1)}, u32[]{:S(2)}, u32[]{:S(2)}) collective-permute-start(bf16[16,3072]{1,0:T(8,128)(2,1)S(1)} %get-tuple-element.43), channel_id=1, source_target_pairs={{0,192},{64,0},{128,64},{192,128},{1,193},{65,1},{129,65},{193,129... | collective-permute-start | bytes 294920 | tf_op jit(solution)/shard_map/ppermute | solution.py:28
  23.2 7.0 %collective-permute-start.4 = (bf16[16,3072]{1,0:T(8,128)(2,1)S(1)}, bf16[16,3072]{1,0:T(8,128)(2,1)S(1)}, u32[]{:S(2)}, u32[]{:S(2)}) collective-permute-start(bf16[16,3072]{1,0:T(8,128)(2,1)S(1)} %get-tuple-element.43), channel_id=1, source_target_pairs={{0,128},{64,192},{128,0},{192,64},{1,129},{65,193},{129,1},{193,65... | collective-permute-start | bytes 294920 | tf_op jit(solution)/shard_map/ppermute | solution.py:28
  25.0 8.3 %collective-permute-start.9 = (bf16[16,3072]{1,0:T(8,128)(2,1)S(1)}, bf16[16,3072]{1,0:T(8,128)(2,1)S(1)}, u32[]{:S(2)}, u32[]{:S(2)}) collective-permute-start(bf16[16,3072]{1,0:T(8,128)(2,1)S(1)} %get-tuple-element.42), channel_id=1, source_target_pairs={{0,8},{8,16},{16,24},{24,0},{1,9},{9,17},{17,25},{25,1},{2,10},{10... | collective-permute-start | bytes 294920 | tf_op jit(solution)/shard_map/ppermute | solution.py:28
  26.5 9.3 %collective-permute-start.8 = (bf16[16,3072]{1,0:T(8,128)(2,1)S(1)}, bf16[16,3072]{1,0:T(8,128)(2,1)S(1)}, u32[]{:S(2)}, u32[]{:S(2)}) collective-permute-start(bf16[16,3072]{1,0:T(8,128)(2,1)S(1)} %get-tuple-element.42), channel_id=1, source_target_pairs={{0,24},{8,0},{16,8},{24,16},{1,25},{9,1},{17,9},{25,17},{2,26},{10... | collective-permute-start | bytes 294920 | tf_op jit(solution)/shard_map/ppermute | solution.py:28
  28.2 7.7 %collective-permute-start.10 = (bf16[16,3072]{1,0:T(8,128)(2,1)S(1)}, bf16[16,3072]{1,0:T(8,128)(2,1)S(1)}, u32[]{:S(2)}, u32[]{:S(2)}) collective-permute-start(bf16[16,3072]{1,0:T(8,128)(2,1)S(1)} %get-tuple-element.42), channel_id=1, source_target_pairs={{0,16},{8,24},{16,0},{24,8},{1,17},{9,25},{17,1},{25,9},{2,18},{10... | collective-permute-start | bytes 294920 | tf_op jit(solution)/shard_map/ppermute | solution.py:28
  30.3 24.3 %copy-start.1 = (bf16[4,16,3072]{2,1,0:T(8,128)(2,1)}, bf16[4,16,3072]{2,1,0:T(8,128)(2,1)S(1)}, u32[]{:S(2)}) copy-start(bf16[4,16,3072]{2,1,0:T(8,128)(2,1)S(1)} %pad_maximum_fusion.1.refs_0_) | copy-start | bytes 1179652
  30.3 13.6 %collective-permute-start.7 = (bf16[4,16,3072]{2,1,0:T(8,128)(2,1)S(1)}, bf16[4,16,3072]{2,1,0:T(8,128)(2,1)S(1)}, u32[]{:S(2)}, u32[]{:S(2)}) collective-permute-start(bf16[4,16,3072]{2,1,0:T(8,128)(2,1)S(1)} %pad_maximum_fusion.1.refs_0_), channel_id=1, source_target_pairs={{0,16},{8,24},{16,0},{24,8},{1,17},{9,25},{17,1},{25,9},{2,18},{10... | collective-permute-start | bytes 1179656 | tf_op jit(solution)/shard_map/ppermute | solution.py:28
  32.6 17.3 %collective-permute-start.6 = (bf16[4,16,3072]{2,1,0:T(8,128)(2,1)S(1)}, bf16[4,16,3072]{2,1,0:T(8,128)(2,1)S(1)}, u32[]{:S(2)}, u32[]{:S(2)}) collective-permute-start(bf16[4,16,3072]{2,1,0:T(8,128)(2,1)S(1)} %pad_maximum_fusion.1.refs_0_), channel_id=1, source_target_pairs={{0,8},{8,16},{16,24},{24,0},{1,9},{9,17},{17,25},{25,1},{2,10},{10... | collective-permute-start | bytes 1179656 | tf_op jit(solution)/shard_map/ppermute | solution.py:28
  33.3 16.6 %collective-permute-start.5 = (bf16[4,16,3072]{2,1,0:T(8,128)(2,1)S(1)}, bf16[4,16,3072]{2,1,0:T(8,128)(2,1)S(1)}, u32[]{:S(2)}, u32[]{:S(2)}) collective-permute-start(bf16[4,16,3072]{2,1,0:T(8,128)(2,1)S(1)} %pad_maximum_fusion.1.refs_0_), channel_id=1, source_target_pairs={{0,24},{8,0},{16,8},{24,16},{1,25},{9,1},{17,9},{25,17},{2,26},{10... | collective-permute-start | bytes 1179656 | tf_op jit(solution)/shard_map/ppermute | solution.py:28
  35.9 18.6 %copy-start.2 = (bf16[4,16,3072]{2,1,0:T(8,128)(2,1)}, bf16[4,16,3072]{2,1,0:T(8,128)(2,1)S(1)}, u32[]{:S(2)}) copy-start(bf16[4,16,3072]{2,1,0:T(8,128)(2,1)S(1)} %pad_maximum_fusion.2.refs_4_) | copy-start | bytes 1179652
  35.9 14.0 %collective-permute-start.13 = (bf16[4,16,3072]{2,1,0:T(8,128)(2,1)S(1)}, bf16[4,16,3072]{2,1,0:T(8,128)(2,1)S(1)}, u32[]{:S(2)}, u32[]{:S(2)}) collective-permute-start(bf16[4,16,3072]{2,1,0:T(8,128)(2,1)S(1)} %pad_maximum_fusion.2.refs_4_), channel_id=1, source_target_pairs={{0,128},{64,192},{128,0},{192,64},{1,129},{65,193},{129,1},{193,65... | collective-permute-start | bytes 1179656 | tf_op jit(solution)/shard_map/ppermute | solution.py:28
  37.8 16.0 %collective-permute-start.12 = (bf16[4,16,3072]{2,1,0:T(8,128)(2,1)S(1)}, bf16[4,16,3072]{2,1,0:T(8,128)(2,1)S(1)}, u32[]{:S(2)}, u32[]{:S(2)}) collective-permute-start(bf16[4,16,3072]{2,1,0:T(8,128)(2,1)S(1)} %pad_maximum_fusion.2.refs_4_), channel_id=1, source_target_pairs={{0,64},{64,128},{128,192},{192,0},{1,65},{65,129},{129,193},{193,1... | collective-permute-start | bytes 1179656 | tf_op jit(solution)/shard_map/ppermute | solution.py:28
  43.9 10.7 %copy-start.3 = (bf16[4,16,3072]{2,1,0:T(8,128)(2,1)}, bf16[4,16,3072]{2,1,0:T(8,128)(2,1)S(1)}, u32[]{:S(2)}) copy-start(bf16[4,16,3072]{2,1,0:T(8,128)(2,1)S(1)} %collective-permute-done.7.refs_3_) | copy-start | bytes 1179652
  43.9 10.7 %collective-permute-start.11 = (bf16[4,16,3072]{2,1,0:T(8,128)(2,1)S(1)}, bf16[4,16,3072]{2,1,0:T(8,128)(2,1)}, u32[]{:S(2)}, u32[]{:S(2)}) collective-permute-start(bf16[4,16,3072]{2,1,0:T(8,128)(2,1)S(1)} %pad_maximum_fusion.2.refs_4_), channel_id=1, source_target_pairs={{0,192},{64,0},{128,64},{192,128},{1,193},{65,1},{129,65},{193,129... | collective-permute-start | bytes 1179656 | tf_op jit(solution)/shard_map/ppermute | solution.py:28
  89.6 12.6 %copy-start = (bf16[256,2048]{1,0:T(8,128)(2,1)S(1)}, bf16[256,2048]{1,0:T(8,128)(2,1)}, u32[]{:S(2)}) copy-start(bf16[256,2048]{1,0:T(8,128)(2,1)} %get-tuple-element.28.rows) | copy-start | bytes 3145732
  97.4 17.4 %all-to-all-start.3 = ((bf16[16,16,2048]{2,1,0:T(8,128)(2,1)}), bf16[16,16,2048]{2,1,0:T(8,128)(2,1)S(1)}, u32[]{:S(2)}, u32[]{:S(2)}) async-start(bf16[16,16,2048]{2,1,0:T(8,128)(2,1)} %bitcast.18), calls=%async_computation.3 | async-start | bytes 2097152 | tf_op jit(solution)/shard_map/all_to_all | solution.py:41
  101.1 5.1 %collective-permute-start.14 = (bf16[592,512]{1,0:T(8,128)(2,1)}, bf16[592,512]{1,0:T(8,128)(2,1)S(1)}, u32[]{:S(2)}, u32[]{:S(2)}) collective-permute-start(bf16[592,512]{1,0:T(8,128)(2,1)} %get-tuple-element.33), channel_id=1, source_target_pairs={{0,1},{1,0},{2,3},{3,2},{4,5},{5,4},{6,7},{7,6},{8,9},{9,8},{10,11... | collective-permute-start | bytes 1818632 | tf_op jit(solution)/shard_map/ppermute | solution.py:46
  101.2 5.0 %collective-permute-start.15 = (bf16[592,512]{1,0:T(8,128)(2,1)}, bf16[592,512]{1,0:T(8,128)(2,1)S(1)}, u32[]{:S(2)}, u32[]{:S(2)}) collective-permute-start(bf16[592,512]{1,0:T(8,128)(2,1)} %get-tuple-element.34), channel_id=1, source_target_pairs={{0,1},{1,0},{2,3},{3,2},{4,5},{5,4},{6,7},{7,6},{8,9},{9,8},{10,11... | collective-permute-start | bytes 1818632 | tf_op jit(solution)/shard_map/ppermute | solution.py:46
  101.7 4.5 %collective-permute-start.16 = (bf16[592,512]{1,0:T(8,128)(2,1)}, bf16[592,512]{1,0:T(8,128)(2,1)S(1)}, u32[]{:S(2)}, u32[]{:S(2)}) collective-permute-start(bf16[592,512]{1,0:T(8,128)(2,1)} %get-tuple-element.35), channel_id=1, source_target_pairs={{0,1},{1,0},{2,3},{3,2},{4,5},{5,4},{6,7},{7,6},{8,9},{9,8},{10,11... | collective-permute-start | bytes 1818632 | tf_op jit(solution)/shard_map/ppermute | solution.py:46
  101.8 4.4 %collective-permute-start.17 = (bf16[592,512]{1,0:T(8,128)(2,1)}, bf16[592,512]{1,0:T(8,128)(2,1)S(1)}, u32[]{:S(2)}, u32[]{:S(2)}) collective-permute-start(bf16[592,512]{1,0:T(8,128)(2,1)} %get-tuple-element.36), channel_id=1, source_target_pairs={{0,1},{1,0},{2,3},{3,2},{4,5},{5,4},{6,7},{7,6},{8,9},{9,8},{10,11... | collective-permute-start | bytes 1818632 | tf_op jit(solution)/shard_map/ppermute | solution.py:46
  117.2 12.2 %all-to-all-start.4 = ((f32[8,2,2048]{2,1,0:T(2,128)}), f32[8,2,2048]{2,1,0:T(2,128)S(1)}, u32[]{:S(2)}, u32[]{:S(2)}) async-start(f32[8,2,2048]{2,1,0:T(2,128)} %reshape.44), calls=%async_computation.4 | async-start | bytes 262144 | tf_op jit(solution)/shard_map/all_to_all | solution.py:41
  (5 other events, 22.6 us)
